TPU v7x, 32 devices: a whole 2x2x4 slice. The times are simulated.
32 devices in a mesh: batch: 8 (over z, x), chan: 4 (over y, core).
Axes of the slice: x: 2, y: 2, z: 4, core: 2. Of those that a mesh axis runs over, the one named last changes fastest.
Arguments:
- features: bfloat16 [64, 628, 2304], P('batch', 'chan'), may hold values from -40 to 40
- crops: int32 [64, 2, 2], P('batch'), may hold values from 0 to 16
- flips: int32 [64, 2], P('batch'), may hold values from 0 to 1
- gain_in: bfloat16 [628], P('chan'), may hold values from 0.099609375 to 1.8984375
- shift_in: bfloat16 [628], P('chan'), may hold values from -3 to 3
- w_reduce: bfloat16 [628, 132], P('chan'), may hold values from -0.25 to 0.25
- gain_mid: bfloat16 [132], P('chan'), may hold values from 0.099609375 to 1.8984375
- shift_mid: bfloat16 [132], P('chan'), may hold values from -3 to 3
- w_spread: bfloat16 [132, 3, 3, 33], P('chan'), may hold values from -0.1875 to 0.1875
- d_passed: bfloat16 [128, 628, 1024], P('batch', 'chan'), may hold values from -3 to 3
- d_new: bfloat16 [128, 33, 1024], P('batch', None, 'chan'), may hold values from -6 to 6
Outputs:
- passed: bfloat16 [128, 628, 1024], P('batch', 'chan')
- new_maps: bfloat16 [128, 33, 1024], P('batch', None, 'chan')
- features_grad: float32 [64, 628, 2304], P('batch', 'chan')
- w_reduce_grad: float32 [628, 132], P('chan')
- w_spread_grad: float32 [132, 3, 3, 33], P('chan')
- gain_in_grad: float32 [628], P('chan')
- shift_in_grad: float32 [628], P('chan')
- gain_mid_grad: float32 [132], P('chan')
- shift_mid_grad: float32 [132], P('chan')
All inputs are finite; a program needn't handle non-finite values.
Results may differ from a plain program's by a relative error of at most 0.0067.
Values may be sent and summed in bfloat16 or wider, within the bound.
A program may use at most 256 MiB of HBM per device.

v0:
```python
import jax
import jax.numpy as jnp
from jax import lax
from jax.sharding import PartitionSpec as P

H = 32
W = 32
MARGIN = 8


epsilon = 1e-05


def cropped(feature_maps, crops, flips):
    channels = feature_maps.shape[1]
    grids = feature_maps.reshape((feature_maps.shape[0], channels, H + 2 * MARGIN, W + 2 * MARGIN))

    def crop_one(item_map, offset, flip_flag):
        window = lax.dynamic_slice(item_map, (jnp.int32(0), offset[0], offset[1]), (channels, H, W))
        return jnp.where(flip_flag > 0, window[:, :, ::-1], window)

    per_item = jax.vmap(jax.vmap(crop_one, in_axes=(None, 0, 0)))(grids, crops, flips)
    return per_item.reshape((-1, channels, H * W))


def placed(grad_views, crops, flips):
    channels = grad_views.shape[1]

    def place_one(grad_view, offset, flip_flag):
        turned = jnp.where(flip_flag > 0, grad_view[:, :, ::-1], grad_view)
        canvas = jnp.zeros((channels, H + 2 * MARGIN, W + 2 * MARGIN), jnp.float32)
        return lax.dynamic_update_slice(canvas, turned, (jnp.int32(0), offset[0], offset[1]))

    per_item = grad_views.reshape((crops.shape[0], 2, channels, H, W))
    summed = jnp.sum(jax.vmap(jax.vmap(place_one))(per_item, crops, flips), axis=1)
    return summed.reshape((crops.shape[0], channels, (H + 2 * MARGIN) * (W + 2 * MARGIN)))


def moments(values, pixel_count):
    mean_val = lax.psum(jnp.sum(values, axis=(0, 2)), "batch") / pixel_count
    centered = values - mean_val[:, None]
    var_val = lax.psum(jnp.sum(centered * centered, axis=(0, 2)), "batch") / pixel_count
    return (mean_val[:, None], lax.rsqrt(var_val + epsilon)[:, None])


def silu_slope(values):
    sigma = jax.nn.sigmoid(values)
    return sigma * (1.0 + values * (1.0 - sigma))


def moved(values, row_step, col_step):
    grid = values.reshape((values.shape[0], values.shape[1], H, W))
    padded = jnp.pad(grid, ((0, 0), (0, 0), (1, 1), (1, 1)))
    window = padded[:, :, 1 + row_step : 1 + row_step + H, 1 + col_step : 1 + col_step + W]
    return window.reshape((values.shape[0], values.shape[1], H * W))


def conv_cells(act_maps, weight):
    summed = None
    for row_step in range(3):
        for col_step in range(3):
            band = moved(act_maps, row_step - 1, col_step - 1)
            product = jnp.einsum(
                "ncp,co->nop",
                band,
                weight[:, row_step, col_step, :],
                preferred_element_type=jnp.float32,
            )
            summed = product if summed is None else summed + product
    return summed


def conv_back(grad_maps, weight):
    summed = None
    for row_step in range(3):
        for col_step in range(3):
            window = moved(grad_maps, 1 - row_step, 1 - col_step)
            product = jnp.einsum(
                "nop,co->ncp",
                window,
                weight[:, row_step, col_step, :],
                preferred_element_type=jnp.float32,
            )
            summed = product if summed is None else summed + product
    return summed


def conv_weight(act_maps, grad_maps):
    outer = []
    for row_step in range(3):
        inner = []
        for col_step in range(3):
            window = moved(act_maps, row_step - 1, col_step - 1)
            inner.append(
                jnp.einsum("ncp,nop->co", window, grad_maps, preferred_element_type=jnp.float32)
            )
        outer.append(jnp.stack(inner, axis=1))
    return jnp.stack(outer, axis=1)


def on_device(
    features,
    crops,
    flips,
    gain_in,
    shift_in,
    w_reduce,
    gain_mid,
    shift_mid,
    w_spread,
    d_passed,
    d_new,
):
    images = crops.shape[0] * 2
    pixel_count = float(images * H * W * lax.axis_size("batch"))
    views = cropped(features, crops, flips)
    inputs = views.astype(jnp.float32)
    mean_in, scale_in = moments(inputs, pixel_count)
    norm_in = (inputs - mean_in) * scale_in
    pre_in = norm_in * gain_in.astype(jnp.float32)[:, None] + shift_in.astype(jnp.float32)[:, None]
    act_in = jax.nn.silu(pre_in).astype(jnp.bfloat16)
    full_grad = lax.all_gather(d_new, "chan", axis=2, tiled=True)
    partial_value = jnp.einsum("ncp,ck->nkp", act_in, w_reduce, preferred_element_type=jnp.float32)
    middle = lax.psum_scatter(partial_value, "chan", scatter_dimension=1, tiled=True)
    mean_mid, scale_mid = moments(middle, pixel_count)
    norm_mid = (middle - mean_mid) * scale_mid
    gain_value = gain_mid.astype(jnp.float32)[:, None]
    pre_mid = norm_mid * gain_value + shift_mid.astype(jnp.float32)[:, None]
    act_mid = jax.nn.silu(pre_mid).astype(jnp.bfloat16)
    term_cells = conv_cells(act_mid, w_spread)
    new_maps = lax.psum_scatter(term_cells, "chan", scatter_dimension=2, tiled=True).astype(
        jnp.bfloat16
    )
    d_act_mid = conv_back(full_grad, w_spread)
    d_pre_mid = d_act_mid * silu_slope(pre_mid)
    w_spread_grad, shift_mid_grad, gain_mid_grad = lax.psum(
        (
            conv_weight(act_mid, full_grad),
            jnp.sum(d_pre_mid, axis=(0, 2)),
            jnp.sum(d_pre_mid * norm_mid, axis=(0, 2)),
        ),
        "batch",
    )
    d_own = (
        gain_value
        * scale_mid
        * (
            d_pre_mid
            - shift_mid_grad[:, None] / pixel_count
            - norm_mid * gain_mid_grad[:, None] / pixel_count
        )
    ).astype(jnp.bfloat16)
    d_middle = lax.all_gather(d_own, "chan", axis=1, tiled=True)
    d_act_in = jnp.einsum("nkp,ck->ncp", d_middle, w_reduce, preferred_element_type=jnp.float32)
    local_w_grad = jnp.einsum("ncp,nkp->ck", act_in, d_middle, preferred_element_type=jnp.float32)
    d_pre_in = d_act_in * silu_slope(pre_in)
    w_reduce_grad, shift_in_grad, gain_in_grad = lax.psum(
        (local_w_grad, jnp.sum(d_pre_in, axis=(0, 2)), jnp.sum(d_pre_in * norm_in, axis=(0, 2))),
        "batch",
    )
    d_views = gain_in.astype(jnp.float32)[:, None] * scale_in * (
        d_pre_in
        - shift_in_grad[:, None] / pixel_count
        - norm_in * gain_in_grad[:, None] / pixel_count
    ) + d_passed.astype(jnp.float32)
    features_grad = placed(d_views, crops, flips)
    return (
        views,
        new_maps,
        features_grad,
        w_reduce_grad,
        w_spread_grad,
        gain_in_grad,
        shift_in_grad,
        gain_mid_grad,
        shift_mid_grad,
    )


def solution(mesh):
    return jax.shard_map(
        on_device,
        mesh=mesh,
        in_specs=(
            P("batch", "chan", None),
            P("batch", None, None),
            P("batch", None),
            P("chan"),
            P("chan"),
            P("chan", None),
            P("chan"),
            P("chan"),
            P("chan", None, None, None),
            P("batch", "chan", None),
            P("batch", None, "chan"),
        ),
        out_specs=(
            P("batch", "chan", None),
            P("batch", None, "chan"),
            P("batch", "chan", None),
            P("chan", None),
            P("chan", None, None, None),
            P("chan"),
            P("chan"),
            P("chan"),
            P("chan"),
        ),
        check_vma=False,
    )
```

profile of v0, /device:TPU:24, one launch (start us, length us, event | category | flops | bytes accessed | tf_op | source)
XLA Modules:
  0.0 2300.4 jit_solution(8615411927973138027)
XLA Ops:
  26.0 75.2 %while.2 = (s32[]{:T(128)}, bf16[8,157,48,48]{1,3,2,0:T(8,128)(2,1)}, s32[16,4]{1,0:T(8,128)S(1)}, bf16[16,157,32,32]{1,3,2,0:T(8,128)(2,1)}, s32[]{:T(128)}) while((s32[]{:T(128)}, bf16[8,157,48,48]{1,3,2,0:T(8,128)(2,1)}, s32[16,4]{1,0:T(8,128)S(1)}, bf16[16,157,32,32]{1,3,2,0:T(8,128)(2,1)}, s32[]{:T(128)}) %tuple.93), condition=%wide.while_cond, body=%wide.while_body.sunk | while | flops 2 | bytes 1050245 | solution.py:19
  101.2 19.7 rev.6
  155.0 19.2 psum.71
  211.1 29.5 %pad_slice_fusion.4 = (bf16[16,33,32,32]{3,2,0,1:T(8,128)(2,1)}, bf16[16,33,32,32]{3,2,0,1:T(8,128)(2,1)}, bf16[16,33,32,32]{3,2,0,1:T(8,128)(2,1)}, bf16[16,33,...) fusion(bf16[16,33,32,32]{3,2,0,1:T(8,128)(2,1)} %reshape.155), kind=kLoop, calls=%fused_computation.23 | loop fusion | bytes 9732096 | tf_op jit(solution)/shard_map/slice | solution.py:54
  317.9 18.1 psum.72
  337.4 18.7 psum.73
  367.2 18.6 all-reduce.3
  399.2 28.8 %pad_slice_fusion.8 = (bf16[16,33,32,32]{3,2,0,1:T(8,128)(2,1)}, bf16[16,33,32,32]{3,2,0,1:T(8,128)(2,1)}, bf16[16,33,32,32]{3,2,0,1:T(8,128)(2,1)}, bf16[16,33,...) fusion(bf16[16,33,32,32]{3,2,0,1:T(8,128)(2,1)} %reshape.146), kind=kLoop, calls=%fused_computation.27 | loop fusion | bytes 9732096 | tf_op jit(solution)/shard_map/slice | solution.py:54
  538.4 34.7 %all-gather.5.cloned.1.call-done = bf16[16,132,1024]{2,0,1:T(8,128)(2,1)} async-done(((bf16[16,33,1024]{2,0,1:T(8,128)(2,1)}), bf16[16,132,1024]{2,0,1:T(8,128)(2,1)}) %all-gather.5.cloned.1.call-update) | async-done | bytes 4325392 | tf_op jit(solution)/shard_map/all_gather | solution.py:153
  596.2 37.5 %all-reduce.2 = (f32[157]{0:T(256)S(1)}, f32[157]{0:T(256)S(1)}, f32[33,3,3,33]{3,0,2,1:T(8,128)}) all-reduce(f32[157]{0:T(256)S(1)} %get-tuple-element.77, f32[157]{0:T(256)S(1)} %get-tuple-element.76, f32[33,3,3,33]{3,0,2,1:T(8,128)S(1)} %pad_maximum_fusion), channel_id=1, replica_groups=mesh['batch'=8,'chan'=4] {'batch'}, use_global_device_ids=true, to_apply=%region_17.18 | all-reduce | flops 10115 | bytes 80920 | tf_op jit(solution)/shard_map/psum | solution.py:157
  662.5 22.6 rev.7
  685.1 17.2 broadcast_select_fusion
  702.3 19.8 broadcast_in_dim.10
  722.1 1491.0 %while.3 = (s32[]{:T(128)}, f32[8,2,157,48,48]{4,3,2,1,0:T(8,128)}, s32[16,5]{1,0:T(8,128)}, f32[16,157,32,32]{1,3,2,0:T(8,128)}, s32[]{:T(128)}, /*index=5*/s32[5]{0:T(128)S(1)}, s32[]{:T(128)}) while((s32[]{:T(128)}, f32[8,2,157,48,48]{4,3,2,1,0:T(8,128)}, s32[16,5]{1,0:T(8,128)}, f32[16,157,32,32]{1,3,2,0:T(8,128)}, s32[]{:T(128)}, ...), condition=%wide.while_cond.1, body=%wide.while_body.1.sunk | while | flops 160789 | bytes 5787923 | solution.py:32
  737.8 77.5 %dynamic-update-slice.8 = f32[8,2,157,48,48]{4,3,2,1,0:T(8,128)} dynamic-update-slice(f32[8,2,157,48,48]{4,3,2,1,0:T(8,128)} %get-tuple-element.228, f32[1,1,157,32,32]{4,3,2,1,0:T(8,128)S(1)} %bitcast_select_fusion.2, s32[]{:T(128)} %bitcast.303, s32[]{:T(128)} %bitcast.304, s32[]{:T(128)} %constant.11.clone.1..sunk, s32[]{:T(128)} %bitcast.305, s32[]{:T(128)} %bitcast.306) | dynamic-update-slice | bytes 1286148 | tf_op jit(solution)/shard_map/vmap(vmap(vmap()))/scatter
  831.1 77.5 %dynamic-update-slice.8 = f32[8,2,157,48,48]{4,3,2,1,0:T(8,128)} dynamic-update-slice(f32[8,2,157,48,48]{4,3,2,1,0:T(8,128)} %get-tuple-element.228, f32[1,1,157,32,32]{4,3,2,1,0:T(8,128)S(1)} %bitcast_select_fusion.2, s32[]{:T(128)} %bitcast.303, s32[]{:T(128)} %bitcast.304, s32[]{:T(128)} %constant.11.clone.1..sunk, s32[]{:T(128)} %bitcast.305, s32[]{:T(128)} %bitcast.306) | dynamic-update-slice | bytes 1286148 | tf_op jit(solution)/shard_map/vmap(vmap(vmap()))/scatter
  924.3 77.5 %dynamic-update-slice.8 = f32[8,2,157,48,48]{4,3,2,1,0:T(8,128)} dynamic-update-slice(f32[8,2,157,48,48]{4,3,2,1,0:T(8,128)} %get-tuple-element.228, f32[1,1,157,32,32]{4,3,2,1,0:T(8,128)S(1)} %bitcast_select_fusion.2, s32[]{:T(128)} %bitcast.303, s32[]{:T(128)} %bitcast.304, s32[]{:T(128)} %constant.11.clone.1..sunk, s32[]{:T(128)} %bitcast.305, s32[]{:T(128)} %bitcast.306) | dynamic-update-slice | bytes 1286148 | tf_op jit(solution)/shard_map/vmap(vmap(vmap()))/scatter
  1017.5 77.5 %dynamic-update-slice.8 = f32[8,2,157,48,48]{4,3,2,1,0:T(8,128)} dynamic-update-slice(f32[8,2,157,48,48]{4,3,2,1,0:T(8,128)} %get-tuple-element.228, f32[1,1,157,32,32]{4,3,2,1,0:T(8,128)S(1)} %bitcast_select_fusion.2, s32[]{:T(128)} %bitcast.303, s32[]{:T(128)} %bitcast.304, s32[]{:T(128)} %constant.11.clone.1..sunk, s32[]{:T(128)} %bitcast.305, s32[]{:T(128)} %bitcast.306) | dynamic-update-slice | bytes 1286148 | tf_op jit(solution)/shard_map/vmap(vmap(vmap()))/scatter
  1110.7 77.5 %dynamic-update-slice.8 = f32[8,2,157,48,48]{4,3,2,1,0:T(8,128)} dynamic-update-slice(f32[8,2,157,48,48]{4,3,2,1,0:T(8,128)} %get-tuple-element.228, f32[1,1,157,32,32]{4,3,2,1,0:T(8,128)S(1)} %bitcast_select_fusion.2, s32[]{:T(128)} %bitcast.303, s32[]{:T(128)} %bitcast.304, s32[]{:T(128)} %constant.11.clone.1..sunk, s32[]{:T(128)} %bitcast.305, s32[]{:T(128)} %bitcast.306) | dynamic-update-slice | bytes 1286148 | tf_op jit(solution)/shard_map/vmap(vmap(vmap()))/scatter
  1203.9 77.5 %dynamic-update-slice.8 = f32[8,2,157,48,48]{4,3,2,1,0:T(8,128)} dynamic-update-slice(f32[8,2,157,48,48]{4,3,2,1,0:T(8,128)} %get-tuple-element.228, f32[1,1,157,32,32]{4,3,2,1,0:T(8,128)S(1)} %bitcast_select_fusion.2, s32[]{:T(128)} %bitcast.303, s32[]{:T(128)} %bitcast.304, s32[]{:T(128)} %constant.11.clone.1..sunk, s32[]{:T(128)} %bitcast.305, s32[]{:T(128)} %bitcast.306) | dynamic-update-slice | bytes 1286148 | tf_op jit(solution)/shard_map/vmap(vmap(vmap()))/scatter
  1297.1 77.5 %dynamic-update-slice.8 = f32[8,2,157,48,48]{4,3,2,1,0:T(8,128)} dynamic-update-slice(f32[8,2,157,48,48]{4,3,2,1,0:T(8,128)} %get-tuple-element.228, f32[1,1,157,32,32]{4,3,2,1,0:T(8,128)S(1)} %bitcast_select_fusion.2, s32[]{:T(128)} %bitcast.303, s32[]{:T(128)} %bitcast.304, s32[]{:T(128)} %constant.11.clone.1..sunk, s32[]{:T(128)} %bitcast.305, s32[]{:T(128)} %bitcast.306) | dynamic-update-slice | bytes 1286148 | tf_op jit(solution)/shard_map/vmap(vmap(vmap()))/scatter
  1390.3 77.5 %dynamic-update-slice.8 = f32[8,2,157,48,48]{4,3,2,1,0:T(8,128)} dynamic-update-slice(f32[8,2,157,48,48]{4,3,2,1,0:T(8,128)} %get-tuple-element.228, f32[1,1,157,32,32]{4,3,2,1,0:T(8,128)S(1)} %bitcast_select_fusion.2, s32[]{:T(128)} %bitcast.303, s32[]{:T(128)} %bitcast.304, s32[]{:T(128)} %constant.11.clone.1..sunk, s32[]{:T(128)} %bitcast.305, s32[]{:T(128)} %bitcast.306) | dynamic-update-slice | bytes 1286148 | tf_op jit(solution)/shard_map/vmap(vmap(vmap()))/scatter
  1483.5 77.5 %dynamic-update-slice.8 = f32[8,2,157,48,48]{4,3,2,1,0:T(8,128)} dynamic-update-slice(f32[8,2,157,48,48]{4,3,2,1,0:T(8,128)} %get-tuple-element.228, f32[1,1,157,32,32]{4,3,2,1,0:T(8,128)S(1)} %bitcast_select_fusion.2, s32[]{:T(128)} %bitcast.303, s32[]{:T(128)} %bitcast.304, s32[]{:T(128)} %constant.11.clone.1..sunk, s32[]{:T(128)} %bitcast.305, s32[]{:T(128)} %bitcast.306) | dynamic-update-slice | bytes 1286148 | tf_op jit(solution)/shard_map/vmap(vmap(vmap()))/scatter
  1576.7 77.5 %dynamic-update-slice.8 = f32[8,2,157,48,48]{4,3,2,1,0:T(8,128)} dynamic-update-slice(f32[8,2,157,48,48]{4,3,2,1,0:T(8,128)} %get-tuple-element.228, f32[1,1,157,32,32]{4,3,2,1,0:T(8,128)S(1)} %bitcast_select_fusion.2, s32[]{:T(128)} %bitcast.303, s32[]{:T(128)} %bitcast.304, s32[]{:T(128)} %constant.11.clone.1..sunk, s32[]{:T(128)} %bitcast.305, s32[]{:T(128)} %bitcast.306) | dynamic-update-slice | bytes 1286148 | tf_op jit(solution)/shard_map/vmap(vmap(vmap()))/scatter
  1670.0 77.5 %dynamic-update-slice.8 = f32[8,2,157,48,48]{4,3,2,1,0:T(8,128)} dynamic-update-slice(f32[8,2,157,48,48]{4,3,2,1,0:T(8,128)} %get-tuple-element.228, f32[1,1,157,32,32]{4,3,2,1,0:T(8,128)S(1)} %bitcast_select_fusion.2, s32[]{:T(128)} %bitcast.303, s32[]{:T(128)} %bitcast.304, s32[]{:T(128)} %constant.11.clone.1..sunk, s32[]{:T(128)} %bitcast.305, s32[]{:T(128)} %bitcast.306) | dynamic-update-slice | bytes 1286148 | tf_op jit(solution)/shard_map/vmap(vmap(vmap()))/scatter
  1763.0 77.5 %dynamic-update-slice.8 = f32[8,2,157,48,48]{4,3,2,1,0:T(8,128)} dynamic-update-slice(f32[8,2,157,48,48]{4,3,2,1,0:T(8,128)} %get-tuple-element.228, f32[1,1,157,32,32]{4,3,2,1,0:T(8,128)S(1)} %bitcast_select_fusion.2, s32[]{:T(128)} %bitcast.303, s32[]{:T(128)} %bitcast.304, s32[]{:T(128)} %constant.11.clone.1..sunk, s32[]{:T(128)} %bitcast.305, s32[]{:T(128)} %bitcast.306) | dynamic-update-slice | bytes 1286148 | tf_op jit(solution)/shard_map/vmap(vmap(vmap()))/scatter
  1856.2 77.5 %dynamic-update-slice.8 = f32[8,2,157,48,48]{4,3,2,1,0:T(8,128)} dynamic-update-slice(f32[8,2,157,48,48]{4,3,2,1,0:T(8,128)} %get-tuple-element.228, f32[1,1,157,32,32]{4,3,2,1,0:T(8,128)S(1)} %bitcast_select_fusion.2, s32[]{:T(128)} %bitcast.303, s32[]{:T(128)} %bitcast.304, s32[]{:T(128)} %constant.11.clone.1..sunk, s32[]{:T(128)} %bitcast.305, s32[]{:T(128)} %bitcast.306) | dynamic-update-slice | bytes 1286148 | tf_op jit(solution)/shard_map/vmap(vmap(vmap()))/scatter
  1949.4 77.5 %dynamic-update-slice.8 = f32[8,2,157,48,48]{4,3,2,1,0:T(8,128)} dynamic-update-slice(f32[8,2,157,48,48]{4,3,2,1,0:T(8,128)} %get-tuple-element.228, f32[1,1,157,32,32]{4,3,2,1,0:T(8,128)S(1)} %bitcast_select_fusion.2, s32[]{:T(128)} %bitcast.303, s32[]{:T(128)} %bitcast.304, s32[]{:T(128)} %constant.11.clone.1..sunk, s32[]{:T(128)} %bitcast.305, s32[]{:T(128)} %bitcast.306) | dynamic-update-slice | bytes 1286148 | tf_op jit(solution)/shard_map/vmap(vmap(vmap()))/scatter
  2042.4 77.5 %dynamic-update-slice.8 = f32[8,2,157,48,48]{4,3,2,1,0:T(8,128)} dynamic-update-slice(f32[8,2,157,48,48]{4,3,2,1,0:T(8,128)} %get-tuple-element.228, f32[1,1,157,32,32]{4,3,2,1,0:T(8,128)S(1)} %bitcast_select_fusion.2, s32[]{:T(128)} %bitcast.303, s32[]{:T(128)} %bitcast.304, s32[]{:T(128)} %constant.11.clone.1..sunk, s32[]{:T(128)} %bitcast.305, s32[]{:T(128)} %bitcast.306) | dynamic-update-slice | bytes 1286148 | tf_op jit(solution)/shard_map/vmap(vmap(vmap()))/scatter
  2135.6 77.5 %dynamic-update-slice.8 = f32[8,2,157,48,48]{4,3,2,1,0:T(8,128)} dynamic-update-slice(f32[8,2,157,48,48]{4,3,2,1,0:T(8,128)} %get-tuple-element.228, f32[1,1,157,32,32]{4,3,2,1,0:T(8,128)S(1)} %bitcast_select_fusion.2, s32[]{:T(128)} %bitcast.303, s32[]{:T(128)} %bitcast.304, s32[]{:T(128)} %constant.11.clone.1..sunk, s32[]{:T(128)} %bitcast.305, s32[]{:T(128)} %bitcast.306) | dynamic-update-slice | bytes 1286148 | tf_op jit(solution)/shard_map/vmap(vmap(vmap()))/scatter
  2213.1 35.5 %reduce_sum.89 = f32[8,157,48,48]{3,2,1,0:T(8,128)} reduce(f32[8,2,157,48,48]{4,3,2,1,0:T(8,128)} %get-tuple-element.22, f32[]{:T(128)} %constant.13.clone.1), dimensions={1}, to_apply=%region_19.20 | reduce | flops 2893824 | bytes 34725892 | tf_op jit(solution)/shard_map/reduce_sum | solution.py:35
  2248.6 26.4 %copy.161 = f32[8,157,48,48]{1,3,2,0:T(8,128)} copy(f32[8,157,48,48]{3,2,1,0:T(8,128)} %reduce_sum.89) | data formatting | bytes 23150592 | tf_op jit(solution)/shard_map/reduce_sum | solution.py:35
  (371 shorter events, 699.5 us)
Async XLA Ops:
  7.2 186.4 %copy-start = (bf16[157,132]{0,1:T(8,128)(2,1)S(1)}, bf16[157,132]{0,1:T(8,128)(2,1)}, u32[]{:S(2)}) copy-start(bf16[157,132]{0,1:T(8,128)(2,1)} %param.16) | copy-start | bytes 124348
  7.2 197.5 %all-gather.3.cloned.1.call-start = ((), (), s32[]{:S(2)}) async-start(), calls=%async_computation.4 | async-start | bytes 1638400 | tf_op jit(solution)/shard_map/all_gather | solution.py:122
  9.0 306.8 %reduce-scatter.3.cloned.1.call-start = ((), (), s32[]{:S(2)}) async-start(), calls=%async_computation.2 | async-start | bytes 10813440 | tf_op jit(solution)/shard_map/reduce_scatter | solution.py:124
  9.9 111.1 %copy-start.32 = (pred[8,2]{1,0:T(8,128)(4,1)}, pred[8,2]{1,0:T(8,128)(4,1)S(1)}, u32[]{:S(2)}) copy-start(pred[8,2]{1,0:T(8,128)(4,1)S(1)} %copy.108) | copy-start | bytes 52
  10.5 175.0 %copy-start.39 = (f32[157]{0:T(256)}, f32[157]{0:T(256)S(1)}, u32[]{:S(2)}) copy-start(f32[157]{0:T(256)S(1)} %convert_element_type.66) | copy-start | bytes 1888
  11.2 174.4 %copy-start.41 = (f32[157]{0:T(256)}, f32[157]{0:T(256)S(1)}, u32[]{:S(2)}) copy-start(f32[157]{0:T(256)S(1)} %convert_element_type.65) | copy-start | bytes 1888
  12.0 14.0 copy-start.28
  149.1 25.1 %copy-start.45 = (bf16[157]{0:T(256)(128)(2,1)S(1)}, bf16[157]{0:T(256)(128)(2,1)}, u32[]{:S(2)}) copy-start(bf16[157]{0:T(256)(128)(2,1)} %param.14) | copy-start | bytes 946
  204.0 332.3 %reduce-scatter.5.cloned.1.call-start = ((), (), s32[]{:S(2)}) async-start(), calls=%async_computation.3 | async-start | bytes 3276800 | tf_op jit(solution)/shard_map/reduce_scatter | solution.py:131
  204.7 151.9 %copy-start.37 = (f32[33]{0:T(128)}, f32[33]{0:T(128)S(1)}, u32[]{:S(2)}) copy-start(f32[33]{0:T(128)S(1)} %convert_element_type.69) | copy-start | bytes 400
  204.7 151.9 %copy-start.38 = (f32[33]{0:T(128)}, f32[33]{0:T(128)S(1)}, u32[]{:S(2)}) copy-start(f32[33]{0:T(128)S(1)} %convert_element_type.68) | copy-start | bytes 400
  288.9 7.2 copy-start.26
  315.8 20.2 copy-start.3
  336.0 31.2 %copy-start.31 = (f32[33]{0:T(128)}, f32[33]{0:T(128)S(1)}, u32[]{:S(2)}) copy-start(f32[33]{0:T(128)S(1)} %broadcast_multiply_fusion.3) | copy-start | bytes 400
  356.5 10.7 copy-start.30
  434.4 59.2 %copy-start.7 = (bf16[16,33,1024]{2,0,1:T(8,128)(2,1)}, bf16[16,33,1024]{2,0,1:T(8,128)(2,1)S(1)}, u32[]{:S(2)}) copy-start(bf16[16,33,1024]{2,0,1:T(8,128)(2,1)S(1)} %reshape.154) | copy-start | bytes 3244036
  441.2 51.6 %copy-start.8 = (bf16[16,33,1024]{2,0,1:T(8,128)(2,1)}, bf16[16,33,1024]{2,0,1:T(8,128)(2,1)S(1)}, u32[]{:S(2)}) copy-start(bf16[16,33,1024]{2,0,1:T(8,128)(2,1)S(1)} %reshape.148) | copy-start | bytes 3244036
  499.6 73.5 %all-gather.5.cloned.1.call-start = ((), (), s32[]{:S(2)}) async-start(), calls=%async_computation.5 | async-start | bytes 5406720 | tf_op jit(solution)/shard_map/all_gather | solution.py:153
  502.5 1789.5 %all-reduce.6.cloned.1.call-start = ((), (), s32[]{:S(2)}) async-start(), calls=%async_computation.6 | async-start | bytes 278528 | tf_op jit(solution)/shard_map/psum | solution.py:157
  502.6 12.6 copy-start.29
  502.6 12.6 copy-start.36
  502.6 12.6 copy-start.47
  502.6 13.3 copy-start.5
  515.9 4.4 copy-start.20
  538.4 44.5 %copy-start.40 = (f32[157]{0:T(256)S(1)}, f32[157]{0:T(256)}, u32[]{:S(2)}) copy-start(f32[157]{0:T(256)} %copy-done.39) | copy-start | bytes 1888
  538.4 44.5 %copy-start.42 = (f32[157]{0:T(256)S(1)}, f32[157]{0:T(256)}, u32[]{:S(2)}) copy-start(f32[157]{0:T(256)} %copy-done.41) | copy-start | bytes 1888
  583.0 50.7 %copy-start.34 = (f32[157]{0:T(256)S(1)}, f32[157]{0:T(256)}, u32[]{:S(2)}) copy-start(f32[157]{0:T(256)} %get-tuple-element.131) | copy-start | bytes 1888
  633.6 13.8 copy-start.43
  633.6 13.8 copy-start.44
  662.5 22.6 copy-start.33
  702.3 19.8 copy-start.49
  2275.0 18.6 copy-start.1
  (24 other events, 46.2 us)
Sparse Core Ops, SparseCore 0:
  10.2 19.3 all-gather.2
  204.1 75.1 reduce-scatter.2
  499.7 36.5 reduce-scatter.4
  537.8 35.2 all-gather.4
  583.1 68.8 all-reduce.5
where the time goes:
time: 2310 us; the launch traced here: 2300 us
  local copies, waits for them, and re-layouts  1810 us (78%)
  other arithmetic  219 us (9%)
  blocking collectives  129 us (6%)
  matrix products  84.1 us (4%)
  waiting for transfers between devices  41.1 us (2%)
    scatter x96, local copies, waits for them, and re-layouts  1370 us
    scatter x32, other arithmetic  115 us
    reshape x16, local copies, waits for them, and re-layouts, moved(): return window.reshape((values.shape[0], values.shape[1], H * W))  112 us
    gather x48, local copies, waits for them, and re-layouts  75.2 us
    slice x2, local copies, waits for them, and re-layouts, moved(): padded[:, :, 1 + row_step:1 + row_step + H, 1 + col_step:1 + col_step + W]  58.3 us
    unnamed x111, local copies, waits for them, and re-layouts  54.7 us
  transfers between devices with their start and end apart: 5, of which 2 were waited for; matrix products, arithmetic and copies ran while one was open for 86% of the time, Pallas kernels for 0%

commit v1 on v0

v1 whole, which is shorter than its diff:
```python
import functools

import jax
import jax.numpy as jnp
from jax import lax
from jax.experimental import pallas as pl
from jax.experimental.pallas import tpu as pltpu
from jax.sharding import PartitionSpec as P

H = 32
W = 32
MARGIN = 8
GRID = H + 2 * MARGIN
CELLS = H * W
EPS = 1e-05
CHUNK = 256
SPAN = 512
STRIDE = 8 * GRID
TAPS = 9
MID_PAD = 144
NEW_PAD = 48
F32 = jnp.float32
BF16 = jnp.bfloat16
MESH = pl.DeviceIdType.MESH
VMEM_LIMIT = 62 * 2**20


def dot(a, b):
    return jnp.dot(a, b, preferred_element_type=F32)


def dot_nt(a, b):
    return lax.dot_general(a, b, (((1,), (1,)), ((), ())), preferred_element_type=F32)


def iota(shape, axis):
    return lax.broadcasted_iota(jnp.int32, shape, axis)


def lane_fold(values):
    total = values[:, 0:128]
    for at in range(128, values.shape[1], 128):
        total = total + values[:, at : at + 128]
    return total


def cols_to_row(pad_ref, values):
    pad_ref[0 : values.shape[0], :] = values
    halves = [
        jnp.sum(jnp.transpose(pad_ref[at : at + 128, :]), axis=0, keepdims=True)
        for at in (0, 128)
    ]
    return jnp.concatenate(halves, axis=1)


def row_to_cols(out_ref, row):
    rows = out_ref.shape[0]
    for at in (0, 128):
        height = min(128, rows - at)
        square = jnp.broadcast_to(row[:, at : at + 128], (128, 128))
        out_ref[at : at + height, :] = jnp.transpose(square)[0:height, :]


def window_start(crops_ref, j, v):
    start = crops_ref[j, v, 0] * GRID + crops_ref[j, v, 1]
    base = jnp.minimum((start // 128) * 128, GRID * GRID - 3 * STRIDE - SPAN)
    return pl.multiple_of(base, 128), start - base


def chunk_target(offset, flip, cell):
    col = cell & (W - 1)
    row = cell >> 5
    return offset + row * GRID + jnp.where(flip > 0, W - 1 - col, col)


def crop_kernel(crops_ref, flips_ref, x_ref, views_ref, stats_ref, mean_ref, dev_ref, pad_ref):
    j = pl.program_id(0)
    count = 2 * CELLS
    total = None
    for v in range(2):
        base, offset = window_start(crops_ref, j, v)
        target = chunk_target(offset, flips_ref[j, v], iota((1, CHUNK), 1))
        select = (iota((SPAN, CHUNK), 0) == target).astype(BF16)
        for k in range(CELLS // CHUNK):
            span = x_ref[0, :, pl.ds(pl.multiple_of(base + STRIDE * k, 128), SPAN)]
            part = dot(span, select)
            views_ref[v, :, CHUNK * k : CHUNK * (k + 1)] = part.astype(BF16)
            folded = lane_fold(part)
            total = folded if total is None else total + folded
    mean = jnp.sum(total, axis=1, keepdims=True) / count
    squares = None
    for v in range(2):
        for k in range(CELLS // CHUNK):
            part = views_ref[v, :, CHUNK * k : CHUNK * (k + 1)].astype(F32) - mean
            folded = lane_fold(part * part)
            squares = folded if squares is None else squares + folded
    dev = jnp.sum(squares, axis=1, keepdims=True)

    @pl.when(j == 0)
    def _():
        mean_ref[...] = jnp.zeros_like(mean_ref)
        dev_ref[...] = jnp.zeros_like(dev_ref)
        pad_ref[...] = jnp.zeros_like(pad_ref)

    before = lax.convert_element_type(j, F32)
    old = mean_ref[...]
    delta = mean - old
    share = 1.0 / (before + 1.0)
    mean_ref[...] = old + delta * share
    dev_ref[...] = dev_ref[...] + dev + delta * delta * (count * before * share)

    @pl.when(j == pl.num_programs(0) - 1)
    def _():
        lane = iota(mean_ref.shape, 1)
        stats_ref[...] = jnp.zeros_like(stats_ref)
        stats_ref[0:1, :] = cols_to_row(pad_ref, jnp.where(lane == 0, mean_ref[...], 0.0))
        stats_ref[1:2, :] = cols_to_row(pad_ref, jnp.where(lane == 0, dev_ref[...], 0.0))


def crop_views(features, crops, flips):
    items, channels, cells = features.shape
    return pl.pallas_call(
        crop_kernel,
        grid=(items,),
        in_specs=[
            pl.BlockSpec(memory_space=pltpu.SMEM),
            pl.BlockSpec(memory_space=pltpu.SMEM),
            pl.BlockSpec((1, channels, cells), lambda j: (j, 0, 0)),
        ],
        out_specs=[
            pl.BlockSpec((2, channels, CELLS), lambda j: (j, 0, 0)),
            pl.BlockSpec((8, 256), lambda j: (0, 0)),
        ],
        out_shape=[
            jax.ShapeDtypeStruct((2 * items, channels, CELLS), BF16),
            jax.ShapeDtypeStruct((8, 256), F32),
        ],
        scratch_shapes=[
            pltpu.VMEM((channels, 128), F32),
            pltpu.VMEM((channels, 128), F32),
            pltpu.VMEM((256, 128), F32),
        ],
        compiler_params=pltpu.CompilerParams(vmem_limit_bytes=VMEM_LIMIT),
        name="crop_views",
    )(crops, flips, features)


def place_kernel(crops_ref, flips_ref, coef_ref, x_ref, dpre_ref, dpass_ref, out_ref):
    j = pl.program_id(0)
    coef = coef_ref[0 : x_ref.shape[1], :]
    mean, slant, level, gain = (coef[:, at : at + 1] for at in range(4))
    out_ref[...] = jnp.zeros_like(out_ref)
    for v in range(2):
        base, offset = window_start(crops_ref, j, v)
        target = chunk_target(offset, flips_ref[j, v], iota((CHUNK, 1), 0))
        select = (iota((CHUNK, SPAN), 1) == target).astype(BF16)
        for k in range(CELLS // CHUNK):
            cols = slice(CHUNK * k, CHUNK * (k + 1))
            x = x_ref[v, :, cols].astype(F32)
            grad = gain * dpre_ref[v, :, cols].astype(F32) + dpass_ref[v, :, cols].astype(F32)
            grad = grad + ((x - mean) * slant + level)
            span = pl.ds(pl.multiple_of(base + STRIDE * k, 128), SPAN)
            out_ref[0, :, span] += dot(grad.astype(BF16), select)


def place_views(crops, flips, coef, views, dpre, d_passed):
    items = crops.shape[0]
    channels = views.shape[1]
    pair = pl.BlockSpec((2, channels, CELLS), lambda j: (j, 0, 0))
    return pl.pallas_call(
        place_kernel,
        grid=(items,),
        in_specs=[
            pl.BlockSpec(memory_space=pltpu.SMEM),
            pl.BlockSpec(memory_space=pltpu.SMEM),
            pl.BlockSpec(coef.shape, lambda j: (0, 0)),
            pair,
            pair,
            pair,
        ],
        out_specs=pl.BlockSpec((1, channels, GRID * GRID), lambda j: (j, 0, 0)),
        out_shape=jax.ShapeDtypeStruct((items, channels, GRID * GRID), F32),
        compiler_params=pltpu.CompilerParams(vmem_limit_bytes=VMEM_LIMIT),
        name="place_views",
    )(crops, flips, coef, views, dpre, d_passed)


def sigmoid(v):
    return 0.5 * jnp.tanh(0.5 * v) + 0.5


def combine(parts, count):
    groups = parts.shape[0]
    mean = parts[0, 0:1, :]
    dev = parts[0, 1:2, :]
    for at in range(1, groups):
        mean = mean + parts[at, 0:1, :]
        dev = dev + parts[at, 1:2, :]
    mean = mean / groups
    spread = None
    for at in range(groups):
        off = parts[at, 0:1, :] - mean
        spread = off * off if spread is None else spread + off * off
    return mean, dev + spread * count


def layer_kernel(
    nb,
    views_hbm,
    stats_ref,
    params_ref,
    wr_in,
    wsp_in,
    dnew_hbm,
    dpre_hbm,
    coef_ref,
    new_ref,
    wrg_ref,
    wsg_ref,
    grads_ref,
    x_sc,
    act_sc,
    slope_sc,
    half_out,
    half_in,
    pair_sc,
    far_sc,
    d_sc,
    dcol_sc,
    mid_sc,
    actm_sc,
    dm_out,
    dm_in,
    t_sc,
    dn_sc,
    dnf_sc,
    par_sc,
    wsp_sc,
    wr_sc,
    wrt_sc,
    wb_sc,
    wf_sc,
    stat_sc,
    cstat_sc,
    msg_sc,
    cmsg_sc,
    col_sc,
    colm_sc,
    padc_sc,
    padm_sc,
    acc_sc,
    accm_sc,
    wg_sc,
    wsg_sc,
    wsgo_sc,
    wsgi_sc,
    rs_out,
    rs_in,
    ag_sc,
    newo_sc,
    newi_sc,
    load_sem,
    store_sem,
    half_s,
    half_r,
    far_s,
    far_r,
    dm_s,
    dm_r,
    bat_s,
    bat_r,
    chan_s,
    chan_r,
    own_sem,
):
    bi, ci = lax.axis_index("batch"), lax.axis_index("chan")
    y, c = ci // 2, lax.rem(ci, 2)
    n_views, n_in = x_sc.shape[0], x_sc.shape[1]
    quarter = n_views // 4
    local_count = float(n_views * CELLS)
    owned_count = float(quarter * CELLS)
    pixels = float(nb) * local_count
    mate = (bi, 2 * y + (1 - c))
    across = (bi, 2 * (1 - y) + c)

    def batch_peer(k):
        return (lax.rem(bi + k, nb), ci)

    def chan_peer(k):
        return (bi, lax.rem(ci + k, 4))

    barrier = pltpu.get_barrier_semaphore()

    def greet(k, carry):
        pl.semaphore_signal(barrier, inc=1, device_id=batch_peer(k), device_id_type=MESH)
        return carry

    lax.fori_loop(1, nb, greet, 0)
    for k in range(1, 4):
        pl.semaphore_signal(barrier, inc=1, device_id=chan_peer(k), device_id_type=MESH)
    pl.semaphore_wait(barrier, nb + 2)

    def batch_copy(kind, k, src, dst):
        return pltpu.make_async_remote_copy(
            src_ref=src,
            dst_ref=dst,
            send_sem=bat_s.at[kind, k],
            recv_sem=bat_r.at[kind, k],
            device_id=batch_peer(k),
            device_id_type=MESH,
        )

    def batch_send(kind, src_of, dst):
        def step(k, carry):
            batch_copy(kind, k, src_of(lax.rem(bi + k, nb)), dst.at[bi]).start()
            return carry

        lax.fori_loop(1, nb, step, 0)

    def batch_wait(kind, src_of, dst):
        def step(k, carry):
            other = lax.rem(bi + nb - k, nb)
            batch_copy(kind, k, src_of(lax.rem(bi + k, nb)), dst.at[other]).wait()
            return carry

        lax.fori_loop(1, nb, step, 0)

    def chan_copy(kind, k, src, dst):
        return pltpu.make_async_remote_copy(
            src_ref=src,
            dst_ref=dst,
            send_sem=chan_s.at[kind, k],
            recv_sem=chan_r.at[kind, k],
            device_id=chan_peer(k),
            device_id_type=MESH,
        )

    def chan_send(kind, src_of, dst):
        for k in range(1, 4):
            chan_copy(kind, k, src_of(lax.rem(ci + k, 4)), dst.at[ci]).start()

    def chan_wait(kind, src_of, dst):
        for k in range(1, 4):
            other = lax.rem(ci + 4 - k, 4)
            chan_copy(kind, k, src_of(lax.rem(ci + k, 4)), dst.at[other]).wait()

    def same(ref):
        return lambda other: ref

    def load(n):
        return pltpu.make_async_copy(views_hbm.at[n], x_sc.at[n], load_sem.at[n])

    def load_step(n, carry):
        load(n).start()
        return carry

    stat_sc[0, bi] = stats_ref[...]
    batch_send(0, same(stats_ref), stat_sc.at[0])
    lax.fori_loop(0, n_views, load_step, 0)
    par_sc[ci] = params_ref[...]
    chan_send(0, same(params_ref), par_sc)
    wsp_sc[ci] = wsp_in[...]
    chan_send(1, same(wsp_in), wsp_sc)
    own_new = pltpu.make_async_copy(dnew_hbm.at[:, c], dn_sc.at[ci], own_sem)
    own_new.start()
    dnew_of = lambda other: dnew_hbm.at[:, lax.rem(other, 2)]
    chan_send(2, dnew_of, dn_sc)

    padc_sc[...] = jnp.zeros_like(padc_sc)
    padm_sc[...] = jnp.zeros_like(padm_sc)
    acc_sc[...] = jnp.zeros_like(acc_sc)
    accm_sc[...] = jnp.zeros_like(accm_sc)
    wg_sc[...] = jnp.zeros_like(wg_sc)
    wsg_sc[...] = jnp.zeros_like(wsg_sc)
    dnf_sc[...] = jnp.zeros_like(dnf_sc)
    wr_sc[...] = jnp.zeros_like(wr_sc)
    wr_sc[:, 0 : wr_in.shape[1]] = wr_in[...]
    eye = (iota((MID_PAD, MID_PAD), 0) == iota((MID_PAD, MID_PAD), 1)).astype(BF16)
    wrt_sc[...] = dot_nt(eye, wr_sc[...]).astype(BF16)
    gain_row = params_ref[0:1, :]
    shift_row = params_ref[1:2, :]

    batch_wait(0, same(stats_ref), stat_sc.at[0])
    mean_row, dev_row = combine(stat_sc[0], local_count)
    rstd_row = lax.rsqrt(dev_row / pixels + EPS)
    row_to_cols(col_sc.at[0], mean_row)
    row_to_cols(col_sc.at[1], rstd_row)
    row_to_cols(col_sc.at[2], rstd_row * gain_row)
    row_to_cols(col_sc.at[3], shift_row)

    def wide(ref, at):
        col = ref[at]
        return jnp.concatenate([col, col], axis=1)

    def slot_view(i, core):
        h = jnp.where(i < quarter, 1 - y, y)
        return quarter * (2 * h + core) + lax.rem(i, quarter)

    def activate(n):
        mean, scale, shift = wide(col_sc, 0), wide(col_sc, 2), wide(col_sc, 3)
        for k in range(CELLS // CHUNK):
            cols = slice(CHUNK * k, CHUNK * (k + 1))
            pre = (x_sc[n, :, cols].astype(F32) - mean) * scale + shift
            s = sigmoid(pre)
            act = pre * s
            slope_sc[n, :, cols] = (s + act * (1.0 - s)).astype(BF16)
            act_sc[n, :, cols] = act.astype(BF16)

    def partial(n, k):
        return dot(wrt_sc[...], act_sc[n, :, CHUNK * k : CHUNK * (k + 1)])

    def half_copy(i):
        return pltpu.make_async_remote_copy(
            src_ref=half_out.at[i],
            dst_ref=half_in.at[i],
            send_sem=half_s.at[i],
            recv_sem=half_r.at[i],
            device_id=mate,
            device_id_type=MESH,
        )

    def far_copy(i):
        return pltpu.make_async_remote_copy(
            src_ref=pair_sc.at[i],
            dst_ref=far_sc.at[i],
            send_sem=far_s.at[i],
            recv_sem=far_r.at[i],
            device_id=across,
            device_id_type=MESH,
        )

    def forward(i, carry):
        theirs, mine = slot_view(i, 1 - c), slot_view(i, c)
        load(theirs).wait()
        activate(theirs)
        for k in range(CELLS // CHUNK):
            cols = slice(CHUNK * k, CHUNK * (k + 1))
            half_out[i, :, cols] = partial(theirs, k).astype(BF16)
        half_copy(i).start()
        load(mine).wait()
        activate(mine)
        half_copy(i).wait_recv()
        for k in range(CELLS // CHUNK):
            cols = slice(CHUNK * k, CHUNK * (k + 1))
            both = partial(mine, k) + half_in[i, :, cols].astype(F32)
            pair_sc[i, :, cols] = both.astype(BF16)
        far_copy(i).start()
        return carry

    lax.fori_loop(0, 2 * quarter, forward, 0)

    chan_wait(1, same(wsp_in), wsp_sc)
    stacked = wsp_sc[...].reshape(4 * NEW_PAD, TAPS * NEW_PAD)
    n_own = wsg_ref.shape[0]
    lane, row = iota((MID_PAD, 4 * NEW_PAD), 1), iota((MID_PAD, 4 * NEW_PAD), 0)
    hit = None
    for b in range(4):
        inner = lane - NEW_PAD * b
        one = (inner >= 0) & (inner < n_own) & (row == inner + n_own * b)
        hit = one if hit is None else hit | one
    wb_sc[...] = dot(hit.astype(BF16), stacked).astype(BF16)
    taps_eye = iota((TAPS * NEW_PAD, TAPS * NEW_PAD), 0) == iota((TAPS * NEW_PAD, TAPS * NEW_PAD), 1)
    wf_sc[...] = dot_nt(taps_eye.astype(BF16), wb_sc[...]).astype(BF16)

    cell = iota((1, CELLS), 1)
    col_at, row_at = cell & (W - 1), cell >> 5

    def inside(values, row_step, col_step):
        ok = None
        if col_step != 0:
            ok = (col_at + col_step >= 0) & (col_at + col_step < W)
        if row_step != 0:
            on = (row_at + row_step >= 0) & (row_at + row_step < H)
            ok = on if ok is None else ok & on
        return values if ok is None else jnp.where(ok, values, 0.0)

    def at_offset(values, row_step, col_step):
        move = (-(W * row_step + col_step)) % CELLS
        rolled = values if move == 0 else pltpu.roll(values, move, 1)
        return inside(rolled, row_step, col_step)

    own_new.wait()
    chan_wait(2, dnew_of, dn_sc)

    def back_slot(i, carry):
        h = jnp.where(i < quarter, 1 - y, y)
        keep = i
        for b in range(4):
            dnf_sc[0 : dn_sc.shape[3], CHUNK * b : CHUNK * (b + 1)] = dn_sc[b, h, lax.rem(i, quarter)].astype(F32)
        grad = dnf_sc[...]
        for b in range(3):
            moved = at_offset(grad, 0, 1 - b)
            for a in range(3):
                t = 3 * a + b
                tap = at_offset(moved, 1 - a, 0)
                dcol_sc[keep, NEW_PAD * t : NEW_PAD * (t + 1), :] = tap.astype(BF16)
        for k in range(CELLS // CHUNK):
            cols = slice(CHUNK * k, CHUNK * (k + 1))
            d_sc[i, :, cols] = dot(wb_sc[...], dcol_sc[keep, :, cols])
        return carry

    lax.fori_loop(0, 2 * quarter, back_slot, 0)

    chan_wait(0, same(params_ref), par_sc)

    def gathered(at):
        total = None
        for b in range(4):
            piece = jnp.where(iota((8, 256), 1) < n_own, par_sc[b], 0.0)
            piece = piece if b == 0 else pltpu.roll(piece, n_own * b, 1)
            total = piece if total is None else total + piece
        return total[at : at + 1, :]

    row_to_cols(colm_sc.at[2], gathered(2))
    row_to_cols(colm_sc.at[3], gathered(3))

    def middle_sum(q, carry):
        far_copy(q).wait_recv()
        total = None
        for k in range(CELLS // CHUNK):
            cols = slice(CHUNK * k, CHUNK * (k + 1))
            part = pair_sc[quarter + q, :, cols].astype(F32) + far_sc[q, :, cols].astype(F32)
            mid_sc[q, :, cols] = part
            folded = lane_fold(part)
            total = folded if total is None else total + folded
        accm_sc[0] += total
        return carry

    lax.fori_loop(0, quarter, middle_sum, 0)
    local_mean = jnp.sum(accm_sc[0], axis=1, keepdims=True) / owned_count

    def middle_dev(q, carry):
        total = None
        for k in range(CELLS // CHUNK):
            part = mid_sc[q, :, CHUNK * k : CHUNK * (k + 1)] - local_mean
            folded = lane_fold(part * part)
            total = folded if total is None else total + folded
        accm_sc[1] += total
        return carry

    lax.fori_loop(0, quarter, middle_dev, 0)
    cmsg_sc[0] = jnp.zeros_like(cmsg_sc[0])
    cmsg_sc[0, 0:1, :] = cols_to_row(padm_sc, accm_sc[0]) / owned_count
    cmsg_sc[0, 1:2, :] = cols_to_row(padm_sc, accm_sc[1])
    accm_sc[...] = jnp.zeros_like(accm_sc)
    cstat_sc[0, ci] = cmsg_sc[0]
    chan_send(3, same(cmsg_sc.at[0]), cstat_sc.at[0])
    chan_wait(3, same(cmsg_sc.at[0]), cstat_sc.at[0])
    group_mean, group_dev = combine(cstat_sc[0], owned_count)
    msg_sc[0] = jnp.zeros_like(msg_sc[0])
    msg_sc[0, 0:1, :] = group_mean
    msg_sc[0, 1:2, :] = group_dev
    stat_sc[1, bi] = msg_sc[0]
    batch_send(1, same(msg_sc.at[0]), stat_sc.at[1])
    batch_wait(1, same(msg_sc.at[0]), stat_sc.at[1])
    meanm_row, devm_row = combine(stat_sc[1], local_count)
    rstdm_row = lax.rsqrt(devm_row / pixels + EPS)
    row_to_cols(colm_sc.at[0], meanm_row)
    row_to_cols(colm_sc.at[1], rstdm_row)

    def mid_point(values):
        mean, rstd = wide(colm_sc, 0), wide(colm_sc, 1)
        norm = (values - mean) * rstd
        pre = norm * wide(colm_sc, 2) + wide(colm_sc, 3)
        s = sigmoid(pre)
        act = pre * s
        return norm, act, s + act * (1.0 - s)

    def mid_own(q, carry):
        first, second = None, None
        for k in range(CELLS // CHUNK):
            cols = slice(CHUNK * k, CHUNK * (k + 1))
            norm, act, slope = mid_point(mid_sc[q, :, cols])
            actm_sc[q, :, cols] = act.astype(BF16)
            grad = d_sc[quarter + q, :, cols] * slope
            d_sc[quarter + q, :, cols] = grad
            mid_sc[q, :, cols] = norm
            one, two = lane_fold(grad), lane_fold(grad * norm)
            first = one if first is None else first + one
            second = two if second is None else second + two
        accm_sc[0] += first
        accm_sc[1] += second
        return carry

    lax.fori_loop(0, quarter, mid_own, 0)
    cmsg_sc[1] = jnp.zeros_like(cmsg_sc[1])
    cmsg_sc[1, 0:1, :] = cols_to_row(padm_sc, accm_sc[0])
    cmsg_sc[1, 1:2, :] = cols_to_row(padm_sc, accm_sc[1])
    cstat_sc[1, ci] = cmsg_sc[1]
    chan_send(4, same(cmsg_sc.at[1]), cstat_sc.at[1])
    chan_wait(4, same(cmsg_sc.at[1]), cstat_sc.at[1])
    msg_sc[1] = (cstat_sc[1, 0] + cstat_sc[1, 1]) + (cstat_sc[1, 2] + cstat_sc[1, 3])
    stat_sc[2, bi] = msg_sc[1]
    batch_send(2, same(msg_sc.at[1]), stat_sc.at[2])

    def spread(q, carry):
        for k in range(CELLS // CHUNK):
            cols = slice(CHUNK * k, CHUNK * (k + 1))
            t_sc[:, cols] = dot(wf_sc[...], actm_sc[q, :, cols])
        total = None
        for b in range(3):
            column = None
            for a in range(3):
                t = 3 * a + b
                tap = at_offset(t_sc[NEW_PAD * t : NEW_PAD * t + 40, :], a - 1, 0)
                column = tap if column is None else column + tap
            column = at_offset(column, 0, b - 1)
            total = column if total is None else total + column
        for b in range(4):
            newo_sc[b, q] = total[0 : newo_sc.shape[2], CHUNK * b : CHUNK * (b + 1)].astype(BF16)
        wsg_sc[...] += dot_nt(actm_sc[q], dcol_sc[quarter + q])
        return carry

    lax.fori_loop(0, quarter, spread, 0)
    new_of = lambda other: newo_sc.at[other]
    newi_sc[ci] = newo_sc[ci]
    chan_send(5, new_of, newi_sc)
    for b in range(4):
        wsgo_sc[b] = wsg_sc[n_own * b : n_own * b + 40, :]
    wsgi_sc[ci] = wsgo_sc[ci]
    wsg_of = lambda other: wsgo_sc.at[other]
    chan_send(6, wsg_of, wsgi_sc)

    batch_wait(2, same(msg_sc.at[1]), stat_sc.at[2])
    total = stat_sc[2, 0]
    for at in range(1, nb):
        total = total + stat_sc[2, at]
    row_to_cols(colm_sc.at[4], total[0:1, :] / pixels)
    row_to_cols(colm_sc.at[5], total[1:2, :] / pixels)
    mid_sums = total
    gain_row_mid = gathered(2)
    row_to_cols(colm_sc.at[6], gain_row_mid * rstdm_row)

    def dm_copy(i):
        return pltpu.make_async_remote_copy(
            src_ref=dm_out.at[i],
            dst_ref=dm_in.at[i],
            send_sem=dm_s.at[i],
            recv_sem=dm_r.at[i],
            device_id=mate,
            device_id_type=MESH,
        )

    def store(n):
        return pltpu.make_async_copy(slope_sc.at[n], dpre_hbm.at[n], store_sem.at[n])

    def back_view(n, dm_ref):
        mean, rstd = wide(col_sc, 0), wide(col_sc, 1)
        first, second = None, None
        for k in range(CELLS // CHUNK):
            cols = slice(CHUNK * k, CHUNK * (k + 1))
            grad = dot(wr_sc[...], dm_ref[:, cols]) * slope_sc[n, :, cols].astype(F32)
            slope_sc[n, :, cols] = grad.astype(BF16)
            norm = (x_sc[n, :, cols].astype(F32) - mean) * rstd
            one, two = lane_fold(grad), lane_fold(grad * norm)
            first = one if first is None else first + one
            second = two if second is None else second + two
        acc_sc[0] += first
        acc_sc[1] += second
        wg_sc[0:n_in, :] += dot_nt(act_sc[n], dm_ref[...])
        store(n).start()

    def dm_own(q, carry):
        i = quarter + q
        for k in range(CELLS // CHUNK):
            cols = slice(CHUNK * k, CHUNK * (k + 1))
            grad = d_sc[i, :, cols] - wide(colm_sc, 4) - mid_sc[q, :, cols] * wide(colm_sc, 5)
            dm_out[i, :, cols] = (grad * wide(colm_sc, 6)).astype(BF16)
        dm_copy(i).start()
        return carry

    lax.fori_loop(0, quarter, dm_own, 0)

    def back_own(q, carry):
        i = quarter + q
        back_view(slot_view(i, c), dm_out.at[i])
        dm_copy(i).wait_recv()
        back_view(slot_view(i, 1 - c), dm_in.at[i])
        return carry

    lax.fori_loop(0, quarter, back_own, 0)

    rs_rows = rs_out.shape[2]
    chan_wait(6, wsg_of, wsgi_sc)
    wsg_total = (wsgi_sc[0] + wsgi_sc[1]) + (wsgi_sc[2] + wsgi_sc[3])
    wsg_tiles = [
        (r, l, min(128, TAPS * NEW_PAD - 128 * l)) for r in range(5) for l in range(4)
    ]

    def put_tiles(slot, values, tiles):
        for at, (r, l, width) in enumerate(tiles):
            rs_out[slot, at // rs_rows, at % rs_rows, :, 0:width] = values[
                8 * r : 8 * r + 8, 128 * l : 128 * l + width
            ]

    def scatter(slot, kind):
        rs_in[slot, bi] = rs_out[slot, bi]
        batch_send(kind, lambda other: rs_out.at[slot, other], rs_in.at[slot])

    def reduce_gather(slot, kind):
        batch_wait(kind, lambda other: rs_out.at[slot, other], rs_in.at[slot])
        total = rs_in[slot, 0]
        for at in range(1, nb):
            total = total + rs_in[slot, at]
        rs_out[slot, bi] = total
        ag_sc[slot, bi] = total
        batch_send(kind + 1, same(rs_out.at[slot, bi]), ag_sc.at[slot])

    def gather_wait(slot, kind):
        batch_wait(kind + 1, same(rs_out.at[slot, bi]), ag_sc.at[slot])

    rs_out[...] = jnp.zeros_like(rs_out)
    put_tiles(0, wsg_total, wsg_tiles)
    scatter(0, 4)

    def back_far(q, carry):
        far_copy(quarter + q).wait_recv()
        for k in range(CELLS // CHUNK):
            cols = slice(CHUNK * k, CHUNK * (k + 1))
            part = pair_sc[q, :, cols].astype(F32) + far_sc[quarter + q, :, cols].astype(F32)
            norm, act, slope = mid_point(part)
            grad = d_sc[q, :, cols] * slope - wide(colm_sc, 4) - norm * wide(colm_sc, 5)
            dm_out[q, :, cols] = (grad * wide(colm_sc, 6)).astype(BF16)
        dm_copy(q).start()
        back_view(slot_view(q, c), dm_out.at[q])
        dm_copy(q).wait_recv()
        back_view(slot_view(q, 1 - c), dm_in.at[q])
        return carry

    lax.fori_loop(0, quarter, back_far, 0)

    msg_sc[2] = jnp.zeros_like(msg_sc[2])
    msg_sc[2, 0:1, :] = cols_to_row(padc_sc, acc_sc[0])
    msg_sc[2, 1:2, :] = cols_to_row(padc_sc, acc_sc[1])
    stat_sc[3, bi] = msg_sc[2]
    batch_send(3, same(msg_sc.at[2]), stat_sc.at[3])
    wrg_tiles = [(r, l, 128 if l == 0 else MID_PAD - 128) for r in range(20) for l in range(2)]
    put_tiles(1, wg_sc, wrg_tiles)
    scatter(1, 6)
    reduce_gather(0, 4)
    reduce_gather(1, 6)

    chan_wait(5, new_of, newi_sc)
    for b in range(4):
        for q in range(quarter):
            new_ref[quarter * b + q] = newi_sc[b, q]

    batch_wait(3, same(msg_sc.at[2]), stat_sc.at[3])
    total = stat_sc[3, 0]
    for at in range(1, nb):
        total = total + stat_sc[3, at]
    gain_scale = gain_row * rstd_row
    row_to_cols(col_sc.at[4], -gain_scale * rstd_row * (total[1:2, :] / pixels))
    row_to_cols(col_sc.at[5], -gain_scale * (total[0:1, :] / pixels))
    row_to_cols(col_sc.at[6], gain_scale)
    lane = iota(coef_ref.shape, 1)
    coef = jnp.where(lane == 0, col_sc[0], 0.0)
    coef = jnp.where(lane == 1, col_sc[4], coef)
    coef = jnp.where(lane == 2, col_sc[5], coef)
    coef_ref[...] = jnp.where(lane == 3, col_sc[6], coef)

    grads_ref[...] = jnp.zeros_like(grads_ref)
    grads_ref[0:1, :] = total[1:2, :]
    grads_ref[1:2, :] = total[0:1, :]
    own_sums = mid_sums
    for b in range(1, 4):
        own_sums = jnp.where(ci == b, pltpu.roll(mid_sums, 256 - n_own * b, 1), own_sums)
    grads_ref[2:3, :] = own_sums[1:2, :]
    grads_ref[3:4, :] = own_sums[0:1, :]

    gather_wait(0, 4)
    for at, (r, l, width) in enumerate(wsg_tiles):
        height = min(8, wsg_ref.shape[0] - 8 * r)
        wsg_ref[8 * r : 8 * r + height, 128 * l : 128 * l + width] = ag_sc[
            0, at // rs_rows, at % rs_rows, 0:height, 0:width
        ]
    gather_wait(1, 6)
    for at, (r, l, width) in enumerate(wrg_tiles):
        height = min(8, wrg_ref.shape[0] - 8 * r)
        width = min(width, wrg_ref.shape[1] - 128 * l)
        wrg_ref[8 * r : 8 * r + height, 128 * l : 128 * l + width] = ag_sc[
            1, at // rs_rows, at % rs_rows, 0:height, 0:width
        ]

    def finish(n, carry):
        store(n).wait()
        return carry

    lax.fori_loop(0, n_views, finish, 0)

    def sent(i, carry):
        half_copy(i).wait_send()
        far_copy(i).wait_send()
        dm_copy(i).wait_send()
        return carry

    lax.fori_loop(0, 2 * quarter, sent, 0)


def layer(nb, views, stats, params, w_reduce, w_spread, d_new):
    n_views, n_in, _ = views.shape
    n_mid = w_reduce.shape[1]
    n_own = n_mid // 4
    quarter = n_views // 4
    n_new = d_new.shape[3]
    rs_rows = -(-40 // nb)
    n_cols = TAPS * NEW_PAD
    vmem = pl.BlockSpec(memory_space=pltpu.VMEM)
    anywhere = pl.BlockSpec(memory_space=pl.ANY)
    dma = pltpu.SemaphoreType.DMA
    slots = 2 * quarter
    return pl.pallas_call(
        functools.partial(layer_kernel, nb),
        in_specs=[anywhere, vmem, vmem, vmem, vmem, anywhere],
        out_specs=[anywhere, vmem, vmem, vmem, vmem, vmem],
        out_shape=[
            jax.ShapeDtypeStruct((n_views, n_in, CELLS), BF16),
            jax.ShapeDtypeStruct((n_in, 128), F32),
            jax.ShapeDtypeStruct((n_views, n_new, CHUNK), BF16),
            jax.ShapeDtypeStruct((n_in, n_mid), F32),
            jax.ShapeDtypeStruct((n_own, n_cols), F32),
            jax.ShapeDtypeStruct((8, 256), F32),
        ],
        scratch_shapes=[
            pltpu.VMEM((n_views, n_in, CELLS), BF16),
            pltpu.VMEM((n_views, n_in, CELLS), BF16),
            pltpu.VMEM((n_views, n_in, CELLS), BF16),
            pltpu.VMEM((slots, MID_PAD, CELLS), BF16),
            pltpu.VMEM((slots, MID_PAD, CELLS), BF16),
            pltpu.VMEM((slots, MID_PAD, CELLS), BF16),
            pltpu.VMEM((slots, MID_PAD, CELLS), BF16),
            pltpu.VMEM((slots, MID_PAD, CELLS), F32),
            pltpu.VMEM((slots, n_cols, CELLS), BF16),
            pltpu.VMEM((quarter, MID_PAD, CELLS), F32),
            pltpu.VMEM((quarter, MID_PAD, CELLS), BF16),
            pltpu.VMEM((slots, MID_PAD, CELLS), BF16),
            pltpu.VMEM((slots, MID_PAD, CELLS), BF16),
            pltpu.VMEM((n_cols, CELLS), F32),
            pltpu.VMEM((4, 2, quarter, n_new, CHUNK), BF16),
            pltpu.VMEM((NEW_PAD, CELLS), F32),
            pltpu.VMEM((4, 8, 256), F32),
            pltpu.VMEM((4, NEW_PAD, n_cols), BF16),
            pltpu.VMEM((n_in, MID_PAD), BF16),
            pltpu.VMEM((MID_PAD, n_in), BF16),
            pltpu.VMEM((MID_PAD, n_cols), BF16),
            pltpu.VMEM((n_cols, MID_PAD), BF16),
            pltpu.VMEM((4, nb, 8, 256), F32),
            pltpu.VMEM((2, 4, 8, 256), F32),
            pltpu.VMEM((3, 8, 256), F32),
            pltpu.VMEM((2, 8, 256), F32),
            pltpu.VMEM((7, n_in, 128), F32),
            pltpu.VMEM((7, MID_PAD, 128), F32),
            pltpu.VMEM((256, 128), F32),
            pltpu.VMEM((256, 128), F32),
            pltpu.VMEM((2, n_in, 128), F32),
            pltpu.VMEM((2, MID_PAD, 128), F32),
            pltpu.VMEM((160, MID_PAD), F32),
            pltpu.VMEM((MID_PAD, n_cols), F32),
            pltpu.VMEM((4, 40, n_cols), F32),
            pltpu.VMEM((4, 40, n_cols), F32),
            pltpu.VMEM((2, nb, rs_rows, 8, 128), F32),
            pltpu.VMEM((2, nb, rs_rows, 8, 128), F32),
            pltpu.VMEM((2, nb, rs_rows, 8, 128), F32),
            pltpu.VMEM((4, quarter, n_new, CHUNK), BF16),
            pltpu.VMEM((4, quarter, n_new, CHUNK), BF16),
            dma((n_views,)),
            dma((n_views,)),
            dma((slots,)),
            dma((slots,)),
            dma((slots,)),
            dma((slots,)),
            dma((slots,)),
            dma((slots,)),
            dma((8, nb)),
            dma((8, nb)),
            dma((7, 4)),
            dma((7, 4)),
            dma,
        ],
        compiler_params=pltpu.CompilerParams(
            collective_id=0, has_side_effects=True, vmem_limit_bytes=VMEM_LIMIT
        ),
        name="layer",
    )(views, stats, params, w_reduce, w_spread, d_new)


def solution(mesh):
    nb = mesh.shape["batch"]

    def on_device(features, crops, flips, gain_in, shift_in, w_reduce, gain_mid, shift_mid, w_spread, d_passed, d_new):
        n_in, n_mid = w_reduce.shape
        n_own, n_new = w_spread.shape[0], w_spread.shape[3]
        n_views = d_new.shape[0]

        def as_row(v):
            return jnp.pad(v.astype(F32), (0, 256 - v.shape[0]))

        params = jnp.stack([as_row(v) for v in (gain_in, shift_in, gain_mid, shift_mid)])
        params = jnp.pad(params, ((0, 4), (0, 0)))
        w9 = w_spread.reshape(n_own, TAPS, n_new)
        w9 = jnp.pad(w9, ((0, NEW_PAD - n_own), (0, 0), (0, NEW_PAD - n_new)))
        w9 = w9.reshape(NEW_PAD, TAPS * NEW_PAD)
        grads = d_new.reshape(2, 2, n_views // 4, n_new, d_new.shape[2])
        views, stats = crop_views(features, crops, flips)
        dpre, coef, new_maps, wr_grad, ws_grad, sums = layer(nb, views, stats, params, w_reduce, w9, grads)
        features_grad = place_views(crops, flips, coef, views, dpre, d_passed)
        ws_grad = ws_grad.reshape(n_own, TAPS, NEW_PAD)[:, :, :n_new].reshape(w_spread.shape)
        return (
            views,
            new_maps,
            features_grad,
            wr_grad,
            ws_grad,
            sums[0, :n_in],
            sums[1, :n_in],
            sums[2, :n_own],
            sums[3, :n_own],
        )

    return jax.shard_map(
        on_device,
        mesh=mesh,
        in_specs=(
            P("batch", "chan", None),
            P("batch", None, None),
            P("batch", None),
            P("chan"),
            P("chan"),
            P("chan", None),
            P("chan"),
            P("chan"),
            P("chan", None, None, None),
            P("batch", "chan", None),
            P("batch", None, "chan"),
        ),
        out_specs=(
            P("batch", "chan", None),
            P("batch", None, "chan"),
            P("batch", "chan", None),
            P("chan", None),
            P("chan", None, None, None),
            P("chan"),
            P("chan"),
            P("chan"),
            P("chan"),
        ),
        check_vma=False,
    )
```

time: 2310 us -> 189 us (0.08)
  the two profiles are of different devices: /device:TPU:24 before, /device:TPU:0 now
where the time goes in v1:
time: 189 us; the launch traced here: 188 us
  Pallas kernels  139 us (74%)
  local copies, waits for them, and re-layouts  47.4 us (25%)
    pallas_call x1, Pallas kernels, layer(): pl.pallas_call(functools.partial(layer_kernel, nb), in_specs=[anywhere, v...  114 us
    unnamed x30, local copies, waits for them, and re-layouts  43 us
    pallas_call x1, Pallas kernels, place_views(): pl.pallas_call(place_kernel, grid=(items,), in_specs=[pl.BlockSpec(memory...  14.6 us
    pallas_call x1, Pallas kernels, crop_views(): pl.pallas_call(crop_kernel, grid=(items,), in_specs=[pl.BlockSpec(memory_...  11.1 us

profile of v1, /device:TPU:0, one launch (start us, length us, event | category | flops | bytes accessed | tf_op | source)
XLA Modules:
  0.0 188.2 jit_solution(598117067405158261)
XLA Ops:
  0.6 1.4 copy.49.crops_ref
  2.0 1.3 copy.50.flips_ref
  3.3 6.3 %copy.51.x_ref = bf16[8,157,2304]{2,1,0:T(8,128)(2,1)} copy(bf16[8,157,2304]{2,0,1:T(8,128)(2,1)} %param.11) | data formatting | bytes 11575296 | tf_op args[0]
  9.7 0.0 copy-start.7
  9.7 0.0 copy-start.8
  9.7 0.0 copy-start.9
  9.7 11.1 %crop_views.1 = (bf16[16,157,1024]{2,1,0:T(8,128)(2,1)}, f32[8,256]{1,0:T(8,128)}) custom-call(s32[8,2,2]{2,1,0:T(2,128)} %copy.49.crops_ref, s32[8,2]{1,0:T(8,128)} %copy.50.flips_ref, bf16[8,157,2304]{2,1,0:T(8,128)(2,1)} %copy.51.x_ref), custom_call_target="tpu_custom_call" | custom-call | tf_op jit(solution)/shard_map/crop_views/pallas_call | solution.py:122
  20.8 0.0 copy-done.1
  20.8 0.8 copy.53
  21.6 0.0 copy-done.3
  21.6 0.2 copy.52
  21.8 0.7 copy.55.wsp_in
  22.5 0.0 copy-done.5
  22.5 0.7 copy.54.wr_in
  23.3 0.0 copy-done.6
  23.3 0.0 copy-done.7
  23.3 0.0 copy-done.8
  23.4 0.6 fusion.7.params_ref
  24.0 113.7 %layer.1 = (bf16[16,157,1024]{2,1,0:T(8,128)(2,1)}, f32[157,128]{1,0:T(8,128)}, bf16[16,33,256]{2,1,0:T(8,128)(2,1)}, f32[157,132]{1,0:T(8,128)}, f32[33,432]{1,0:T(8,128)}, /*index=5*/f32[8,256]{1,0:T(8,128)}) custom-call(bf16[16,157,1024]{2,1,0:T(8,128)(2,1)} %get-tuple-element.43.views_hbm.x_ref, f32[8,256]{1,0:T(8,128)} %get-tuple-element.18.stats_ref, ...), custom_call_target="tpu_custom_call" | custom-call | tf_op jit(solution)/shard_map/layer/pallas_call | solution.py:812
  137.7 7.7 %copy.58.dpass_ref = bf16[16,157,1024]{2,1,0:T(8,128)(2,1)} copy(bf16[16,157,1024]{2,0,1:T(8,128)(2,1)} %param.20) | data formatting | bytes 10289152 | tf_op args[9]
  145.4 14.6 %place_views.1 = f32[8,157,2304]{2,1,0:T(8,128)} custom-call(s32[8,2,2]{2,1,0:T(2,128)} %copy.49.crops_ref, s32[8,2]{1,0:T(8,128)} %copy.50.flips_ref, f32[157,128]{1,0:T(8,128)} %get-tuple-element.20.coef_ref, bf16[16,157,1024]{2,1,0:T(8,128)(2,1)} %get-tuple-element.43.views_hbm.x_ref, bf16[16,157,1024]{2,1,0:T(8,128)(2,1)} %get-tuple-element.21.dpre_ref, ...), custom_call_target="tpu_custom_call" | custom-call | tf_op jit(solution)/shard_map/place_views/pallas_call | solution.py:170
  160.0 0.0 copy-start.2
  160.0 15.6 %copy.62 = f32[8,157,2304]{2,0,1:T(8,128)} copy(f32[8,157,2304]{2,1,0:T(8,128)} %place_views.1) | data formatting | bytes 23150592
  175.6 1.3 fusion.8
  176.9 1.3 slice_bitcast_fusion
  178.2 0.1 reshape.36
  178.3 0.7 copy.59
  179.0 0.0 copy-done
  179.0 0.8 copy.61
  179.8 0.0 copy-done.2
  179.8 0.8 copy.63
  180.6 7.7 %copy.60 = bf16[16,157,1024]{2,0,1:T(8,128)(2,1)} copy(bf16[16,157,1024]{2,1,0:T(8,128)(2,1)} %get-tuple-element.43.views_hbm.x_ref) | data formatting | bytes 10289152
  (17 shorter events, 0.1 us)
Async XLA Ops:
  9.7 11.2 %copy-start.1 = (bf16[16,33,256]{2,0,1:T(8,128)(2,1)S(1)}, bf16[16,33,256]{2,0,1:T(8,128)(2,1)}, u32[]{:S(2)}) copy-start(bf16[16,33,256]{2,0,1:T(8,128)(2,1)} %param.21) | copy-start | bytes 811012
  9.7 12.0 %copy-start.3 = (bf16[33,3,3,33]{3,0,2,1:T(8,128)(2,1)S(1)}, bf16[33,3,3,33]{3,0,2,1:T(8,128)(2,1)}, u32[]{:S(2)}) copy-start(bf16[33,3,3,33]{3,0,2,1:T(8,128)(2,1)} %param.19) | copy-start | bytes 58810
  9.7 12.9 %copy-start.5 = (bf16[157,132]{0,1:T(8,128)(2,1)S(1)}, bf16[157,132]{0,1:T(8,128)(2,1)}, u32[]{:S(2)}) copy-start(bf16[157,132]{0,1:T(8,128)(2,1)} %param.16) | copy-start | bytes 124348
  9.7 13.6 %copy-start.6 = (bf16[157]{0:T(256)(128)(2,1)S(1)}, bf16[157]{0:T(256)(128)(2,1)}, u32[]{:S(2)}) copy-start(bf16[157]{0:T(256)(128)(2,1)} %param.14) | copy-start | bytes 946
  9.7 13.6 %copy-start.7 = (bf16[157]{0:T(256)(128)(2,1)S(1)}, bf16[157]{0:T(256)(128)(2,1)}, u32[]{:S(2)}) copy-start(bf16[157]{0:T(256)(128)(2,1)} %param.15) | copy-start | bytes 946
  9.7 13.6 %copy-start.8 = (bf16[33]{0:T(256)(128)(2,1)S(1)}, bf16[33]{0:T(256)(128)(2,1)}, u32[]{:S(2)}) copy-start(bf16[33]{0:T(256)(128)(2,1)} %param.17) | copy-start | bytes 202
  9.7 13.7 %copy-start.9 = (bf16[33]{0:T(256)(128)(2,1)S(1)}, bf16[33]{0:T(256)(128)(2,1)}, u32[]{:S(2)}) copy-start(bf16[33]{0:T(256)(128)(2,1)} %param.18) | copy-start | bytes 202
  160.0 18.2 %copy-start.4 = (f32[33,432]{1,0:T(8,128)S(1)}, f32[33,432]{1,0:T(8,128)}, u32[]{:S(2)}) copy-start(f32[33,432]{1,0:T(8,128)} %get-tuple-element.23) | copy-start | bytes 171076
  160.0 19.0 %copy-start = (bf16[16,33,256]{2,1,0:T(8,128)(2,1)S(1)}, bf16[16,33,256]{2,1,0:T(8,128)(2,1)}, u32[]{:S(2)}) copy-start(bf16[16,33,256]{2,1,0:T(8,128)(2,1)} %get-tuple-element.44) | copy-start | bytes 811012
  160.0 19.8 %copy-start.2 = (f32[157,132]{1,0:T(8,128)S(1)}, f32[157,132]{1,0:T(8,128)}, u32[]{:S(2)}) copy-start(f32[157,132]{1,0:T(8,128)} %get-tuple-element.46) | copy-start | bytes 248692

commit v2 on v1

v2 whole, which is shorter than its diff:
```python
import functools

import jax
import jax.numpy as jnp
from jax import lax
from jax.experimental import pallas as pl
from jax.experimental.pallas import tpu as pltpu
from jax.sharding import PartitionSpec as P

H = 32
W = 32
MARGIN = 8
GRID = H + 2 * MARGIN
CELLS = H * W
EPS = 1e-05
CHUNK = 256
SPAN = 512
STRIDE = 8 * GRID
TAPS = 9
MID_PAD = 144
NEW_PAD = 48
MAIN = 128
REST = 4
F32 = jnp.float32
BF16 = jnp.bfloat16
MESH = pl.DeviceIdType.MESH
VMEM_LIMIT = 63 * 2**20 + 800 * 2**10


def dot(a, b):
    return jnp.dot(a, b, preferred_element_type=F32)


def dot_nt(a, b):
    return lax.dot_general(a, b, (((1,), (1,)), ((), ())), preferred_element_type=F32)


def iota(shape, axis):
    return lax.broadcasted_iota(jnp.int32, shape, axis)


def lane_fold(values):
    total = values[:, 0:128]
    for at in range(128, values.shape[1], 128):
        total = total + values[:, at : at + 128]
    return total


def cols_to_row(pad_ref, values):
    if values is not None:
        pad_ref[0 : values.shape[0], :] = values
    halves = [
        jnp.sum(jnp.transpose(pad_ref[at : at + 128, :]), axis=0, keepdims=True)
        for at in (0, 128)
    ]
    return jnp.concatenate(halves, axis=0)


def two_rows(row):
    return jnp.concatenate([row[:, 0:128], row[:, 128:256]], axis=0)


def one_row(rows):
    return jnp.concatenate([rows[0:1, :], rows[1:2, :]], axis=1)


def row_to_cols(out_ref, row):
    rows = out_ref.shape[0]
    for h, at in enumerate((0, 128)):
        height = min(128, rows - at)
        square = jnp.broadcast_to(row[h : h + 1, :], (128, 128))
        out_ref[at : at + height, :] = jnp.transpose(square)[0:height, :]


def window_start(crops_ref, j, v):
    start = crops_ref[v, 0, j] * GRID + crops_ref[v, 1, j]
    base = jnp.minimum((start // 128) * 128, GRID * GRID - 3 * STRIDE - SPAN)
    return pl.multiple_of(base, 128), start - base


def chunk_target(offset, flip, cell):
    col = cell & (W - 1)
    row = cell >> 5
    return offset + row * GRID + jnp.where(flip > 0, W - 1 - col, col)


def crop_kernel(crops_ref, flips_ref, x_ref, views_ref, passed_ref, stats_ref, pick_sc, xf_sc, xi_sc, pf_sc, mean_sc, dev_sc):
    step = pl.program_id(0)
    rows, items, cells = x_ref.shape
    n_views = 2 * items

    @pl.when(step == 0)
    def _():
        def build(n, carry):
            j, v = n // 2, n % 2
            _, offset = window_start(crops_ref, j, v)
            target = chunk_target(offset, flips_ref[v, j], iota((1, CHUNK), 1))
            pick_sc[n] = (iota((SPAN, CHUNK), 0) == target).astype(BF16)
            return carry

        lax.fori_loop(0, n_views, build, 0)
        mean_sc[...] = jnp.zeros_like(mean_sc)
        dev_sc[...] = jnp.zeros_like(dev_sc)

    for l in range(cells // 128):
        at = slice(128 * l, 128 * (l + 1))
        wide_x = x_ref[:, :, at].astype(F32)
        for ch in range(rows):
            xf_sc[l, (items + 1) * ch : (items + 1) * ch + items, :] = wide_x[ch]

    total = jnp.zeros((rows, 128), F32)
    squares = jnp.zeros((rows, 128), F32)
    pivot = None
    for j in range(items):
        for l in range(cells // 128):
            xi_sc[j, :, 128 * l : 128 * (l + 1)] = xf_sc[l, pl.ds(j, rows, stride=items + 1), :].astype(BF16)
        for v in range(2):
            n = 2 * j + v
            base, _ = window_start(crops_ref, j, v)
            spans = [xi_sc[j, :, pl.ds(pl.multiple_of(base + STRIDE * k, 128), SPAN)] for k in range(CELLS // CHUNK)]
            parts = dot(jnp.concatenate(spans, axis=0), pick_sc[n])
            for k in range(CELLS // CHUNK):
                cols = slice(CHUNK * k, CHUNK * (k + 1))
                part = parts[rows * k : rows * (k + 1), :]
                views_ref[n, :, cols] = part.astype(BF16)
                for l in range(2):
                    pf_sc[2 * k + l, pl.ds(n, rows, stride=n_views + 1), :] = part[:, 128 * l : 128 * (l + 1)]
                if pivot is None:
                    pivot = jnp.sum(lane_fold(part), axis=1, keepdims=True) / CHUNK
                off = part - pivot
                total = total + lane_fold(off)
                squares = squares + lane_fold(off * off)
    for l in range(CELLS // 128):
        at = slice(128 * l, 128 * (l + 1))
        for ch in range(rows):
            first = (n_views + 1) * ch
            passed_ref[ch, :, at] = pf_sc[l, first : first + n_views, :].astype(BF16)
    count = n_views * CELLS
    shift = jnp.sum(total, axis=1, keepdims=True) / count
    mean = pivot + shift
    first = pl.multiple_of(step * rows, 8)
    lane = iota((rows, 128), 1)
    mean_sc[pl.ds(first, rows), :] = jnp.where(lane == 0, mean, 0.0)
    dev_sc[pl.ds(first, rows), :] = squares - jnp.where(lane == 0, shift * shift * count, 0.0)

    @pl.when(step == pl.num_programs(0) - 1)
    def _():
        stats_ref[...] = jnp.zeros_like(stats_ref)
        stats_ref[0:2, :] = cols_to_row(mean_sc, None)
        stats_ref[2:4, :] = cols_to_row(dev_sc, None)


def crop_views(features, crops, flips):
    channels, items, cells = features.shape
    rows = 80
    return pl.pallas_call(
        crop_kernel,
        grid=(-(-channels // rows),),
        in_specs=[
            pl.BlockSpec(memory_space=pltpu.SMEM),
            pl.BlockSpec(memory_space=pltpu.SMEM),
            pl.BlockSpec((rows, items, cells), lambda s: (s, 0, 0)),
        ],
        out_specs=[
            pl.BlockSpec((2 * items, rows, CELLS), lambda s: (0, s, 0)),
            pl.BlockSpec((rows, 2 * items, CELLS), lambda s: (s, 0, 0)),
            pl.BlockSpec((8, 128), lambda s: (0, 0)),
        ],
        out_shape=[
            jax.ShapeDtypeStruct((2 * items, channels, CELLS), BF16),
            jax.ShapeDtypeStruct((channels, 2 * items, CELLS), BF16),
            jax.ShapeDtypeStruct((8, 128), F32),
        ],
        scratch_shapes=[
            pltpu.VMEM((2 * items, SPAN, CHUNK), BF16),
            pltpu.VMEM((cells // 128, rows * (items + 1), 128), F32),
            pltpu.VMEM((items, rows, cells), BF16),
            pltpu.VMEM((CELLS // 128, rows * (2 * items + 1), 128), F32),
            pltpu.VMEM((256, 128), F32),
            pltpu.VMEM((256, 128), F32),
        ],
        compiler_params=pltpu.CompilerParams(vmem_limit_bytes=VMEM_LIMIT),
        name="crop_views",
    )(crops, flips, features)


def place_kernel(crops_ref, flips_ref, dv_ref, new_ref, wrg_ref, wsg_ref, sums_ref, out_ref, newo_ref, wrgo_ref, wsgo_ref, gi_ref, si_ref, gm_ref, sm_ref, pick_sc, sum_sc, flat_sc, new_sc):
    step = pl.program_id(0)
    rows, items, cells = out_ref.shape
    n_views = 2 * items

    @pl.when(step == 0)
    def _():
        def build(n, carry):
            j, v = n // 2, n % 2
            _, offset = window_start(crops_ref, j, v)
            target = chunk_target(offset, flips_ref[v, j], iota((CHUNK, 1), 0))
            pick_sc[n] = (iota((CHUNK, SPAN), 1) == target).astype(BF16)
            return carry

        lax.fori_loop(0, n_views, build, 0)
        n_new = new_ref.shape[1]
        for n in range(n_views):
            for l in range(2):
                piece = new_ref[n, :, 128 * l : 128 * (l + 1)]
                new_sc[l, pl.ds(n, n_new, stride=n_views), :] = piece.astype(F32)
        for l in range(2):
            newo_ref[:, :, 128 * l : 128 * (l + 1)] = new_sc[l].reshape(n_new, n_views, 128).astype(BF16)
        wrgo_ref[...] = wrg_ref[...]
        for t in range(TAPS):
            wsgo_ref[t] = wsg_ref[:, NEW_PAD * t : NEW_PAD * t + wsgo_ref.shape[2]]
        for at, ref in enumerate((gi_ref, si_ref, gm_ref, sm_ref)):
            ref[...] = sums_ref[at, 0 : ref.shape[0]]

    for j in range(items):
        sum_sc[j] = jnp.zeros_like(sum_sc[j])
        for v in range(2):
            n = 2 * j + v
            base, _ = window_start(crops_ref, j, v)
            parts = [dv_ref[n, :, CHUNK * k : CHUNK * (k + 1)] for k in range(CELLS // CHUNK)]
            spans = dot(jnp.concatenate(parts, axis=0), pick_sc[n])
            spans = [spans[rows * k : rows * (k + 1), :] for k in range(CELLS // CHUNK)]
            pieces = [spans[0][:, 0:STRIDE]]
            for k in range(1, CELLS // CHUNK):
                pieces.append(spans[k - 1][:, STRIDE:SPAN] + spans[k][:, 0 : SPAN - STRIDE])
                pieces.append(spans[k][:, SPAN - STRIDE : STRIDE])
            pieces.append(spans[-1][:, STRIDE:SPAN])
            window = jnp.concatenate(pieces, axis=1)
            span = pl.ds(base, window.shape[1])
            if v == 0:
                sum_sc[j, :, span] = window
            else:
                sum_sc[j, :, span] += window
        for l in range(cells // 128):
            flat_sc[l, pl.ds(j, rows, stride=items + 1), :] = sum_sc[j, :, 128 * l : 128 * (l + 1)]
    for l in range(cells // 128):
        for ch in range(rows):
            first = (items + 1) * ch
            out_ref[ch, :, 128 * l : 128 * (l + 1)] = flat_sc[l, first : first + items, :]


def place_views(crops, flips, dv, new_maps, wr_grad, ws_grad, sums):
    items = crops.shape[2]
    n_views, channels, _ = dv.shape
    n_new, n_own = new_maps.shape[1], ws_grad.shape[0]
    rows = 80
    whole = lambda shape: pl.BlockSpec(shape, lambda s: (0,) * len(shape))
    small = [
        ((n_new, n_views, CHUNK), BF16),
        (wr_grad.shape, F32),
        ((TAPS, n_own, n_new), F32),
        ((channels,), F32),
        ((channels,), F32),
        ((n_own,), F32),
        ((n_own,), F32),
    ]
    return pl.pallas_call(
        place_kernel,
        grid=(-(-channels // rows),),
        in_specs=[
            pl.BlockSpec(memory_space=pltpu.SMEM),
            pl.BlockSpec(memory_space=pltpu.SMEM),
            pl.BlockSpec((n_views, rows, CELLS), lambda s: (0, s, 0)),
        ]
        + [whole(v.shape) for v in (new_maps, wr_grad, ws_grad, sums)],
        out_specs=[pl.BlockSpec((rows, items, GRID * GRID), lambda s: (s, 0, 0))]
        + [whole(shape) for shape, _ in small],
        out_shape=[jax.ShapeDtypeStruct((channels, items, GRID * GRID), F32)]
        + [jax.ShapeDtypeStruct(shape, kind) for shape, kind in small],
        scratch_shapes=[
            pltpu.VMEM((n_views, CHUNK, SPAN), BF16),
            pltpu.VMEM((items, rows, GRID * GRID), F32),
            pltpu.VMEM((GRID * GRID // 128, rows * (items + 1), 128), F32),
            pltpu.VMEM((2, n_new * n_views, 128), F32),
        ],
        compiler_params=pltpu.CompilerParams(vmem_limit_bytes=VMEM_LIMIT),
        name="place_views",
    )(crops, flips, dv, new_maps, wr_grad, ws_grad, sums)


def sigmoid(v):
    return 0.5 * jnp.tanh(0.5 * v) + 0.5


def combine(parts, count):
    groups = parts.shape[0]
    mean = parts[0, 0:2, :]
    dev = parts[0, 2:4, :]
    for at in range(1, groups):
        mean = mean + parts[at, 0:2, :]
        dev = dev + parts[at, 2:4, :]
    mean = mean / groups
    spread = None
    for at in range(groups):
        off = parts[at, 0:2, :] - mean
        spread = off * off if spread is None else spread + off * off
    return mean, dev + spread * count


def layer_kernel(
    nb,
    views_hbm,
    stats_ref,
    gain_in_ref,
    shift_in_ref,
    gain_mid_ref,
    shift_mid_ref,
    wr_in,
    wsp_in,
    dnew_ref,
    dpass_hbm,
    dv_hbm,
    new_ref,
    wrg_ref,
    wsg_ref,
    sums_ref,
    x_sc,
    act_sc,
    slope_sc,
    dp_sc,
    half_out,
    half_in,
    pair_sc,
    far_sc,
    pair_rest,
    far_rest,
    pack_sc,
    ext_sc,
    d_sc,
    dcol_sc,
    mid_sc,
    actm_sc,
    dm_out,
    dm_in,
    dno_sc,
    dn_sc,
    dnf_sc,
    dpn_sc,
    flat_sc,
    own_par,
    par_sc,
    wsp_sc,
    wr_sc,
    wrt_sc,
    wb_sc,
    wf_sc,
    stat_sc,
    cstat_sc,
    msg_sc,
    cmsg_sc,
    col_sc,
    colm_sc,
    padc_sc,
    padm_sc,
    acc_sc,
    accm_sc,
    wg_sc,
    wsg_sc,
    wsgi_sc,
    ws_out,
    ws_in,
    ws_all,
    wr_out,
    wr_back,
    wr_all,
    newo_sc,
    newi_sc,
    load_sem,
    store_sem,
    half_s,
    half_r,
    far_s,
    far_r,
    rest_s,
    rest_r,
    dm_s,
    dm_r,
    bat_s,
    bat_r,
    chan_s,
    chan_r,
    dp_sem,
):
    bi, ci = lax.axis_index("batch"), lax.axis_index("chan")
    y, c = ci // 2, lax.rem(ci, 2)
    n_views, n_in = x_sc.shape[0], x_sc.shape[1]
    quarter = n_views // 4
    n_own, n_new = wsg_ref.shape[0], dnew_ref.shape[0]
    local_count = float(n_views * CELLS)
    owned_count = float(quarter * CELLS)
    pixels = float(nb) * local_count
    mate = (bi, 2 * y + (1 - c))
    across = (bi, 2 * (1 - y) + c)

    def batch_peer(k):
        return (lax.rem(bi + k, nb), ci)

    def chan_peer(k):
        return (bi, lax.rem(ci + k, 4))

    barrier = pltpu.get_barrier_semaphore()

    def greet(k, carry):
        pl.semaphore_signal(barrier, inc=1, device_id=batch_peer(k), device_id_type=MESH)
        return carry

    lax.fori_loop(1, nb, greet, 0)
    for k in range(1, 4):
        pl.semaphore_signal(barrier, inc=1, device_id=chan_peer(k), device_id_type=MESH)

    def load(n):
        return pltpu.make_async_copy(views_hbm.at[n], x_sc.at[n], load_sem.at[n])

    def load_step(i, carry):
        load(slot_view(i, 1 - c)).start()
        load(slot_view(i, c)).start()
        return carry

    def slot_view(i, core):
        h = jnp.where(i < quarter, 1 - y, y)
        return quarter * (2 * h + core) + lax.rem(i, quarter)

    lax.fori_loop(0, 2 * quarter, load_step, 0)
    pl.semaphore_wait(barrier, nb + 2)

    def batch_copy(kind, k, src, dst):
        return pltpu.make_async_remote_copy(
            src_ref=src,
            dst_ref=dst,
            send_sem=bat_s.at[kind, k],
            recv_sem=bat_r.at[kind, k],
            device_id=batch_peer(k),
            device_id_type=MESH,
        )

    def batch_send(kind, src_of, dst):
        def step(k, carry):
            batch_copy(kind, k, src_of(lax.rem(bi + k, nb)), dst.at[bi]).start()
            return carry

        lax.fori_loop(1, nb, step, 0)

    def batch_wait(kind, src_of, dst):
        def step(k, carry):
            other = lax.rem(bi + nb - k, nb)
            batch_copy(kind, k, src_of(lax.rem(bi + k, nb)), dst.at[other]).wait()
            return carry

        lax.fori_loop(1, nb, step, 0)

    def chan_copy(kind, k, src, dst):
        return pltpu.make_async_remote_copy(
            src_ref=src,
            dst_ref=dst,
            send_sem=chan_s.at[kind, k],
            recv_sem=chan_r.at[kind, k],
            device_id=chan_peer(k),
            device_id_type=MESH,
        )

    def chan_send(kind, src_of, dst):
        for k in range(1, 4):
            chan_copy(kind, k, src_of(lax.rem(ci + k, 4)), dst.at[ci]).start()

    def chan_wait(kind, src_of, dst):
        for k in range(1, 4):
            other = lax.rem(ci + 4 - k, 4)
            chan_copy(kind, k, src_of(lax.rem(ci + k, 4)), dst.at[other]).wait()

    def same(ref):
        return lambda other: ref

    stat_sc[0, bi] = stats_ref[...]
    batch_send(0, same(stats_ref), stat_sc.at[0])
    own_par[...] = jnp.zeros_like(own_par)
    for at, ref in enumerate((gain_in_ref, shift_in_ref, gain_mid_ref, shift_mid_ref)):
        own_par[at : at + 1, 0 : ref.shape[0]] = ref[...].astype(F32).reshape(1, ref.shape[0])
    par_sc[ci] = own_par[...]
    chan_send(0, same(own_par), par_sc)
    dnf_sc[...] = jnp.zeros_like(dnf_sc)
    for t in range(TAPS):
        dnf_sc[0:n_own, NEW_PAD * t : NEW_PAD * t + n_new] = wsp_in[t].astype(F32)
    wsp_sc[ci] = dnf_sc[:, 0 : TAPS * NEW_PAD].astype(BF16)
    wsp_own = same(wsp_sc.at[ci])
    chan_send(1, wsp_own, wsp_sc)

    for l in range(2):
        at = slice(128 * l, 128 * (l + 1))
        flat_sc[l, 0 : n_new * n_views, :] = dnew_ref[:, :, at].astype(F32).reshape(n_new * n_views, 128)
        for n in range(n_views):
            by_view = flat_sc[l, pl.ds(n, n_new, stride=n_views), :].astype(BF16)
            block, q = n // quarter, n % quarter
            dno_sc[block % 2, block // 2, q, :, at] = by_view
    dn_sc[0, ci] = dno_sc[c, y]
    dn_sc[1, ci] = dno_sc[c, 1 - y]
    dnew_of = lambda other: dno_sc.at[lax.rem(other, 2), other // 2]
    dfar_of = lambda other: dno_sc.at[lax.rem(other, 2), 1 - other // 2]
    chan_send(2, dnew_of, dn_sc.at[0])

    padc_sc[...] = jnp.zeros_like(padc_sc)
    padm_sc[...] = jnp.zeros_like(padm_sc)
    acc_sc[...] = jnp.zeros_like(acc_sc)
    accm_sc[...] = jnp.zeros_like(accm_sc)
    wg_sc[...] = jnp.zeros_like(wg_sc)
    wsg_sc[...] = jnp.zeros_like(wsg_sc)
    ext_sc[...] = jnp.zeros_like(ext_sc)
    ws_out[...] = jnp.zeros_like(ws_out)
    wr_out[...] = jnp.zeros_like(wr_out)
    wrt_sc[...] = jnp.zeros_like(wrt_sc)
    wrt_sc[0 : wr_in.shape[0], :] = wr_in[...]
    eye = (iota((n_in, n_in), 0) == iota((n_in, n_in), 1)).astype(BF16)
    wr_sc[...] = dot_nt(eye, wrt_sc[...]).astype(BF16)
    gain_row = two_rows(own_par[0:1, :])
    shift_row = two_rows(own_par[1:2, :])

    batch_wait(0, same(stats_ref), stat_sc.at[0])
    mean_row, dev_row = combine(stat_sc[0], local_count)
    rstd_row = lax.rsqrt(dev_row / pixels + EPS)
    row_to_cols(col_sc.at[0], mean_row)
    row_to_cols(col_sc.at[1], rstd_row)
    row_to_cols(col_sc.at[2], rstd_row * gain_row)
    row_to_cols(col_sc.at[3], shift_row)

    def wide(ref, at):
        col = ref[at]
        return jnp.concatenate([col, col], axis=1)

    def chunks(start=0, count=CELLS // CHUNK):
        if isinstance(start, int):
            return [slice(start + CHUNK * k, start + CHUNK * (k + 1)) for k in range(count)]
        return [pl.ds(pl.multiple_of(start + CHUNK * k, CHUNK), CHUNK) for k in range(count)]

    half = CELLS // 2

    def half_cols(h):
        return pl.ds(h * half if isinstance(h, int) else pl.multiple_of(h * half, half), half)

    def activate(n):
        mean, scale, shift = wide(col_sc, 0), wide(col_sc, 2), wide(col_sc, 3)
        for cols in chunks():
            pre = (x_sc[n, :, cols].astype(F32) - mean) * scale + shift
            s = sigmoid(pre)
            act = pre * s
            slope_sc[n, :, cols] = (s + act * (1.0 - s)).astype(BF16)
            act_sc[n, :, cols] = act.astype(BF16)

    def partial(n, cols):
        return dot(wrt_sc[...], act_sc[n, :, cols])

    def half_copy(i):
        return pltpu.make_async_remote_copy(
            src_ref=half_out.at[i],
            dst_ref=half_in.at[i],
            send_sem=half_s.at[i],
            recv_sem=half_r.at[i],
            device_id=mate,
            device_id_type=MESH,
        )

    def rest_copy(i):
        return pltpu.make_async_remote_copy(
            src_ref=pair_rest.at[i],
            dst_ref=far_rest.at[i],
            send_sem=rest_s.at[i],
            recv_sem=rest_r.at[i],
            device_id=across,
            device_id_type=MESH,
        )

    def unpack_rest(values):
        for k in range(CELLS // CHUNK):
            ext_sc[k, 0:REST, :] = values[REST * k : REST * (k + 1), :]

    def with_rest(main, k):
        return jnp.concatenate([main, ext_sc[k], jnp.zeros((8, CHUNK), F32)], axis=0)

    def far_start(i):
        rest_copy(i).start()
        far_copy(i, 0).start()
        far_copy(i, 1).start()

    def far_copy(i, h):
        return pltpu.make_async_remote_copy(
            src_ref=pair_sc.at[i, :, half_cols(h)],
            dst_ref=far_sc.at[i, :, half_cols(h)],
            send_sem=far_s.at[i, h],
            recv_sem=far_r.at[i, h],
            device_id=across,
            device_id_type=MESH,
        )

    def to_mate(i):
        theirs = slot_view(i, 1 - c)
        load(theirs).wait()
        activate(theirs)
        for cols in chunks():
            half_out[i, :, cols] = partial(theirs, cols)
        half_copy(i).start()

    def forward(i, carry):
        @pl.when(i < 2 * quarter - 1)
        def _():
            to_mate(i + 1)

        mine = slot_view(i, c)
        load(mine).wait()
        activate(mine)
        half_copy(i).wait_recv()
        for k, cols in enumerate(chunks()):
            both = partial(mine, cols) + half_in[i, :, cols]
            pair_sc[i, :, cols] = both[0:MAIN, :].astype(BF16)
            pack_sc[REST * k : REST * (k + 1), :] = both[MAIN : MAIN + REST, :]

            @pl.when(i >= quarter)
            def _():
                mid_sc[i - quarter, :, cols] = both

        pair_rest[i] = pack_sc[...].astype(BF16)

        @pl.when(i < quarter)
        def _():
            far_start(i)

        return carry

    to_mate(0)
    lax.fori_loop(0, 2 * quarter, forward, 0)

    chan_wait(1, wsp_own, wsp_sc)
    stacked = wsp_sc[...].reshape(4 * NEW_PAD, TAPS * NEW_PAD)
    lane, row = iota((MID_PAD, 4 * NEW_PAD), 1), iota((MID_PAD, 4 * NEW_PAD), 0)
    hit = None
    for b in range(4):
        inner = lane - NEW_PAD * b
        one = (inner >= 0) & (inner < n_own) & (row == inner + n_own * b)
        hit = one if hit is None else hit | one
    wb_sc[...] = dot(hit.astype(BF16), stacked).astype(BF16)
    taps_eye = iota((TAPS * NEW_PAD, TAPS * NEW_PAD), 0) == iota((TAPS * NEW_PAD, TAPS * NEW_PAD), 1)
    wf_sc[...] = dot_nt(taps_eye.astype(BF16), wb_sc[...]).astype(BF16)

    cell = iota((1, CELLS), 1)
    col_at, row_at = cell & (W - 1), cell >> 5

    def inside(values, row_step, col_step):
        ok = None
        if col_step != 0:
            ok = (col_at + col_step >= 0) & (col_at + col_step < W)
        if row_step != 0:
            on = (row_at + row_step >= 0) & (row_at + row_step < H)
            ok = on if ok is None else ok & on
        return values if ok is None else jnp.where(ok, values, 0.0)

    def at_offset(values, row_step, col_step):
        move = (-(W * row_step + col_step)) % CELLS
        rolled = values if move == 0 else pltpu.roll(values, move, 1)
        return inside(rolled, row_step, col_step)

    chan_wait(2, dnew_of, dn_sc.at[0])

    def back_slot(i, carry):
        far = jnp.where(i < quarter, 1, 0)
        keep = jnp.where(i < quarter, quarter, i - quarter)
        for b in range(4):
            dnf_sc[0:n_new, CHUNK * b : CHUNK * (b + 1)] = dn_sc[far, b, lax.rem(i, quarter)].astype(F32)
        grad = dnf_sc[...]
        for b in range(3):
            moved = at_offset(grad, 0, 1 - b)
            for a in range(3):
                t = 3 * a + b
                tap = at_offset(moved, 1 - a, 0)
                dcol_sc[keep, NEW_PAD * t : NEW_PAD * (t + 1), :] = tap.astype(BF16)
        for cols in chunks():
            d_sc[i, :, cols] = dot(wb_sc[...], dcol_sc[keep, :, cols])
        return carry

    lax.fori_loop(quarter, 2 * quarter, back_slot, 0)

    group = dpn_sc.shape[1]
    full = n_in // group

    def dp_load(k, rows):
        return pltpu.make_async_copy(
            dpass_hbm.at[pl.ds(k * group, rows)],
            dpn_sc.at[lax.rem(k, 2), pl.ds(0, rows)],
            dp_sem.at[lax.rem(k, 2)],
        )

    def dp_split(k, rows):
        first = k * group if isinstance(k, int) else pl.multiple_of(k * group, group)
        for l in range(CELLS // 128):
            at = slice(128 * l, 128 * (l + 1))
            native = dpn_sc[lax.rem(k, 2), 0:rows, :, at].astype(F32)
            for ch in range(rows):
                flat_sc[l, (n_views + 1) * ch : (n_views + 1) * ch + n_views, :] = native[ch]
            for n in range(n_views):
                by_view = flat_sc[l, pl.ds(n, rows, stride=n_views + 1), :]
                dp_sc[n, pl.ds(first, rows), at] = by_view.astype(BF16)

    left = n_in - full * group

    def dp_step(k, carry):
        @pl.when(k < full - 1)
        def _():
            dp_load(k + 1, group).start()

        dp_load(k, group).wait()
        dp_split(k, group)
        return carry

    dp_load(0, group).start()
    lax.fori_loop(0, full, dp_step, 0)
    if left > 0:
        dp_load(full, left).start()
        dp_load(full, left).wait()
        dp_split(full, left)

    chan_wait(0, same(own_par), par_sc)

    def gathered(at):
        total = None
        for b in range(4):
            piece = jnp.where(iota((8, 256), 1) < n_own, par_sc[b], 0.0)
            piece = piece if b == 0 else pltpu.roll(piece, n_own * b, 1)
            total = piece if total is None else total + piece
        return two_rows(total[at : at + 1, :])

    row_to_cols(colm_sc.at[2], gathered(2))
    row_to_cols(colm_sc.at[3], gathered(3))

    def middle_view(q):
        rest_copy(q).wait_recv()
        far_copy(q, 0).wait_recv()
        far_copy(q, 1).wait_recv()
        unpack_rest(far_rest[q].astype(F32))
        for k, cols in enumerate(chunks()):
            mid_sc[q, :, cols] = mid_sc[q, :, cols] + with_rest(far_sc[q, :, cols].astype(F32), k)

    def middle_sums(q, carry):
        @pl.when(q > 0)
        def _():
            middle_view(q)

        first, second = None, None
        for cols in chunks():
            part = mid_sc[q, :, cols] - wide(colm_sc, 7)
            one, two = lane_fold(part), lane_fold(part * part)
            first = one if first is None else first + one
            second = two if second is None else second + two
        accm_sc[0] += first
        accm_sc[1] += second
        return carry

    middle_view(0)
    pivot = sum(lane_fold(mid_sc[0, :, cols]) for cols in chunks())
    colm_sc[7] = jnp.broadcast_to(jnp.sum(pivot, axis=1, keepdims=True) / CELLS, colm_sc.shape[1:])
    pivot_row = cols_to_row(padm_sc, pivot) / CELLS
    lax.fori_loop(0, quarter, middle_sums, 0)
    off_row = cols_to_row(padm_sc, accm_sc[0]) / owned_count
    cmsg_sc[0] = jnp.zeros_like(cmsg_sc[0])
    cmsg_sc[0, 0:2, :] = pivot_row + off_row
    cmsg_sc[0, 2:4, :] = cols_to_row(padm_sc, accm_sc[1]) - off_row * off_row * owned_count
    accm_sc[...] = jnp.zeros_like(accm_sc)
    cstat_sc[0, ci] = cmsg_sc[0]
    chan_send(3, same(cmsg_sc.at[0]), cstat_sc.at[0])
    chan_send(7, dfar_of, dn_sc.at[1])
    far_start(quarter)
    chan_wait(3, same(cmsg_sc.at[0]), cstat_sc.at[0])
    group_mean, group_dev = combine(cstat_sc[0], owned_count)
    msg_sc[0] = jnp.zeros_like(msg_sc[0])
    msg_sc[0, 0:2, :] = group_mean
    msg_sc[0, 2:4, :] = group_dev
    stat_sc[1, bi] = msg_sc[0]
    batch_send(1, same(msg_sc.at[0]), stat_sc.at[1])
    chan_wait(7, dfar_of, dn_sc.at[1])
    lax.fori_loop(0, quarter, back_slot, 0)
    batch_wait(1, same(msg_sc.at[0]), stat_sc.at[1])
    meanm_row, devm_row = combine(stat_sc[1], local_count)
    rstdm_row = lax.rsqrt(devm_row / pixels + EPS)
    row_to_cols(colm_sc.at[0], meanm_row)
    row_to_cols(colm_sc.at[1], rstdm_row)

    def mid_point(values):
        mean, rstd = wide(colm_sc, 0), wide(colm_sc, 1)
        norm = (values - mean) * rstd
        pre = norm * wide(colm_sc, 2) + wide(colm_sc, 3)
        s = sigmoid(pre)
        act = pre * s
        return norm, act, s + act * (1.0 - s)

    def mid_own(q, carry):
        first, second = None, None
        for cols in chunks():
            norm, act, slope = mid_point(mid_sc[q, :, cols])
            actm_sc[q, :, cols] = act.astype(BF16)
            grad = d_sc[quarter + q, :, cols] * slope
            d_sc[quarter + q, :, cols] = grad
            mid_sc[q, :, cols] = norm
            one, two = lane_fold(grad), lane_fold(grad * norm)
            first = one if first is None else first + one
            second = two if second is None else second + two
        accm_sc[0] += first
        accm_sc[1] += second
        return carry

    lax.fori_loop(0, quarter, mid_own, 0)
    cmsg_sc[1] = jnp.zeros_like(cmsg_sc[1])
    cmsg_sc[1, 0:2, :] = cols_to_row(padm_sc, accm_sc[0])
    cmsg_sc[1, 2:4, :] = cols_to_row(padm_sc, accm_sc[1])
    cstat_sc[1, ci] = cmsg_sc[1]
    chan_send(4, same(cmsg_sc.at[1]), cstat_sc.at[1])
    for q in range(1, quarter):
        far_start(quarter + q)

    def tiles_of(ref):
        rows, cols = ref.shape
        return [(r, l, min(128, cols - 128 * l)) for r in range(rows // 16) for l in range(-(-cols // 128))]

    def scatter(refs, kind, values):
        out, back, _ = refs
        per = out.shape[1]
        for at, (r, l, width) in enumerate(tiles_of(values)):
            tile = values[16 * r : 16 * r + 16, 128 * l : 128 * l + width]
            out[at // per, at % per, :, 0:width] = tile.astype(BF16)
        back[bi] = out[bi]
        batch_send(kind, lambda other: out.at[other], back)

    def reduce_gather(refs, kind):
        out, back, whole = refs
        batch_wait(kind, lambda other: out.at[other], back)
        total = back[0].astype(F32)
        for at in range(1, nb):
            total = total + back[at].astype(F32)
        out[bi] = total.astype(BF16)
        whole[bi] = total.astype(BF16)
        batch_send(kind + 1, same(out.at[bi]), whole)

    def gather(refs, kind, ref):
        out, _, whole = refs
        per = out.shape[1]
        batch_wait(kind + 1, same(out.at[bi]), whole)
        for at, (r, l, width) in enumerate(tiles_of(ref)):
            tile = whole[at // per, at % per, :, 0:width]
            ref[16 * r : 16 * r + 16, 128 * l : 128 * l + width] = tile.astype(F32)

    spread_refs, reduce_refs = (ws_out, ws_in, ws_all), (wr_out, wr_back, wr_all)

    def spread_grad(q, carry):
        wsg_sc[...] += dot_nt(actm_sc[q], dcol_sc[q])
        return carry

    lax.fori_loop(0, quarter, spread_grad, 0)
    scatter(spread_refs, 4, wsg_sc)
    chan_wait(4, same(cmsg_sc.at[1]), cstat_sc.at[1])
    msg_sc[1] = (cstat_sc[1, 0] + cstat_sc[1, 1]) + (cstat_sc[1, 2] + cstat_sc[1, 3])
    stat_sc[2, bi] = msg_sc[1]
    batch_send(2, same(msg_sc.at[1]), stat_sc.at[2])
    def spread(q, carry):
        for k, cols in enumerate(chunks()):
            taps = dot(wf_sc[...], actm_sc[q, :, cols])
            for l in range(2):
                flat_sc[2 * k + l, 0 : TAPS * NEW_PAD, :] = taps[:, 128 * l : 128 * (l + 1)]
        total = None
        for b in range(3):
            column = None
            for a in range(3):
                t = 3 * a + b
                tap = [flat_sc[l, NEW_PAD * t : NEW_PAD * t + 40, :] for l in range(CELLS // 128)]
                tap = at_offset(jnp.concatenate(tap, axis=1), a - 1, 0)
                column = tap if column is None else column + tap
            column = at_offset(column, 0, b - 1)
            total = column if total is None else total + column
        for b in range(4):
            newo_sc[b, q] = total[0:n_new, CHUNK * b : CHUNK * (b + 1)].astype(BF16)
        return carry

    lax.fori_loop(0, quarter, spread, 0)
    new_of = lambda other: newo_sc.at[other]
    newi_sc[ci] = newo_sc[ci]
    reduce_gather(spread_refs, 4)
    batch_wait(2, same(msg_sc.at[1]), stat_sc.at[2])
    mid_sums = stat_sc[2, 0]
    for at in range(1, nb):
        mid_sums = mid_sums + stat_sc[2, at]
    row_to_cols(colm_sc.at[4], mid_sums[0:2, :] / pixels)
    row_to_cols(colm_sc.at[5], mid_sums[2:4, :] / pixels)
    row_to_cols(colm_sc.at[6], gathered(2) * rstdm_row)

    def dm_copy(i, h):
        return pltpu.make_async_remote_copy(
            src_ref=dm_out.at[i, :, half_cols(h)],
            dst_ref=dm_in.at[i, :, half_cols(h)],
            send_sem=dm_s.at[i, h],
            recv_sem=dm_r.at[i, h],
            device_id=mate,
            device_id_type=MESH,
        )

    def store(n):
        return pltpu.make_async_copy(slope_sc.at[n], dv_hbm.at[n], store_sem.at[n])

    def back_part(n, dm_ref, h):
        mean, rstd, scale = wide(col_sc, 0), wide(col_sc, 1), wide(col_sc, 2)
        first, second = None, None
        for cols in chunks(h * half, half // CHUNK):
            grad = dot(wr_sc[...], dm_ref[:, cols]) * slope_sc[n, :, cols].astype(F32)
            slope_sc[n, :, cols] = (grad * scale + dp_sc[n, :, cols].astype(F32)).astype(BF16)
            norm = (x_sc[n, :, cols].astype(F32) - mean) * rstd
            one, two = lane_fold(grad), lane_fold(grad * norm)
            first = one if first is None else first + one
            second = two if second is None else second + two
        acc_sc[0] += first
        acc_sc[1] += second
        cols = half_cols(h)
        wg_sc[:, 0:n_in] += dot_nt(dm_ref[:, cols], act_sc[n, :, cols])

    def dm_own(q, carry):
        i = quarter + q
        for cols in chunks():
            grad = d_sc[i, :, cols] - wide(colm_sc, 4) - mid_sc[q, :, cols] * wide(colm_sc, 5)
            dm_out[i, :, cols] = (grad * wide(colm_sc, 6)).astype(BF16)
        dm_copy(i, 0).start()
        dm_copy(i, 1).start()
        return carry

    lax.fori_loop(0, quarter, dm_own, 0)

    def back_mate(i, h):
        dm_copy(i, h).wait_recv()
        back_part(slot_view(i, 1 - c), dm_in.at[i], h)

    def back_own(t, carry):
        i, h = quarter + t // 2, lax.rem(t, 2)
        back_part(slot_view(i, c), dm_out.at[i], h)
        back_mate(i, h)
        return carry

    lax.fori_loop(0, 2 * quarter, back_own, 0)

    def back_far(t, carry):
        q, h = t // 2, lax.rem(t, 2)
        @pl.when(h == 0)
        def _():
            rest_copy(quarter + q).wait_recv()
            unpack_rest(pair_rest[q].astype(F32) + far_rest[quarter + q].astype(F32))

        far_copy(quarter + q, h).wait_recv()
        for k, cols in enumerate(chunks(h * half, half // CHUNK)):
            part = pair_sc[q, :, cols].astype(F32) + far_sc[quarter + q, :, cols].astype(F32)
            part = with_rest(part, half // CHUNK * h + k)
            norm, act, slope = mid_point(part)
            grad = d_sc[q, :, cols] * slope - wide(colm_sc, 4) - norm * wide(colm_sc, 5)
            dm_out[q, :, cols] = (grad * wide(colm_sc, 6)).astype(BF16)
        dm_copy(q, h).start()
        back_part(slot_view(q, c), dm_out.at[q], h)

        @pl.when(t > 0)
        def _():
            back_mate((t - 1) // 2, lax.rem(t + 1, 2))

        return carry

    lax.fori_loop(0, quarter, back_far, 0)
    gather(spread_refs, 4, wsg_sc)
    for b in range(4):
        wsp_sc[b, 0:40, :] = wsg_sc[n_own * b : n_own * b + 40, :].astype(BF16)
    wsgi_sc[ci] = wsp_sc[ci]
    wsg_of = lambda other: wsp_sc.at[other]
    chan_send(6, wsg_of, wsgi_sc)
    chan_send(5, new_of, newi_sc)
    lax.fori_loop(quarter, 2 * quarter, back_far, 0)
    back_mate(quarter - 1, 1)

    msg_sc[2] = jnp.zeros_like(msg_sc[2])
    msg_sc[2, 0:2, :] = cols_to_row(padc_sc, acc_sc[0])
    msg_sc[2, 2:4, :] = cols_to_row(padc_sc, acc_sc[1])
    stat_sc[3, bi] = msg_sc[2]
    batch_send(3, same(msg_sc.at[2]), stat_sc.at[3])
    scatter(reduce_refs, 6, wg_sc)
    batch_wait(3, same(msg_sc.at[2]), stat_sc.at[3])
    total = stat_sc[3, 0]
    for at in range(1, nb):
        total = total + stat_sc[3, at]
    gain_scale = gain_row * rstd_row
    row_to_cols(col_sc.at[4], -gain_scale * rstd_row * (total[2:4, :] / pixels))
    row_to_cols(col_sc.at[5], -gain_scale * (total[0:2, :] / pixels))
    reduce_gather(reduce_refs, 6)

    def finish(n, carry):
        mean, slant, level = wide(col_sc, 0), wide(col_sc, 4), wide(col_sc, 5)
        for cols in chunks():
            rest = (x_sc[n, :, cols].astype(F32) - mean) * slant + level
            slope_sc[n, :, cols] = (slope_sc[n, :, cols].astype(F32) + rest).astype(BF16)
        store(n).start()
        return carry

    lax.fori_loop(0, n_views, finish, 0)

    sums_ref[...] = jnp.zeros_like(sums_ref)
    sums_ref[0:1, :] = one_row(total[2:4, :])
    sums_ref[1:2, :] = one_row(total[0:2, :])
    all_sums = jnp.concatenate([one_row(mid_sums[2:4, :]), one_row(mid_sums[0:2, :]), jnp.zeros((6, 256), F32)], axis=0)
    own_sums = all_sums
    for b in range(1, 4):
        own_sums = jnp.where(ci == b, pltpu.roll(all_sums, 256 - n_own * b, 1), own_sums)
    sums_ref[2:4, :] = own_sums[0:2, :]

    chan_wait(5, new_of, newi_sc)
    for b in range(4):
        for q in range(quarter):
            new_ref[quarter * b + q] = newi_sc[b, q]
    chan_wait(6, wsg_of, wsgi_sc)
    wsg_total = (wsgi_sc[0].astype(F32) + wsgi_sc[1].astype(F32)) + (
        wsgi_sc[2].astype(F32) + wsgi_sc[3].astype(F32)
    )
    wsg_ref[...] = wsg_total[0:n_own, :]
    gather(reduce_refs, 6, wg_sc)
    wrg_ref[...] = wg_sc[0 : wrg_ref.shape[0], 0:n_in]

    def stored(n, carry):
        store(n).wait()
        return carry

    lax.fori_loop(0, n_views, stored, 0)

    def sent(i, carry):
        half_copy(i).wait_send()
        rest_copy(i).wait_send()
        for h in range(2):
            far_copy(i, h).wait_send()
            dm_copy(i, h).wait_send()
        return carry

    lax.fori_loop(0, 2 * quarter, sent, 0)


def layer(nb, views, stats, vectors, wr_t, w_spread, d_new, d_passed):
    n_views, n_in, _ = views.shape
    n_mid = wr_t.shape[0]
    n_own = n_mid // 4
    quarter = n_views // 4
    n_new = d_new.shape[0]
    n_cols = TAPS * NEW_PAD
    in_pad = -(-n_in // 16) * 16
    ws_tiles = -(-(MID_PAD // 16 * -(-n_cols // 128)) // nb)
    wr_tiles = -(-(MID_PAD // 16 * -(-in_pad // 128)) // nb)
    group = 16
    vmem = pl.BlockSpec(memory_space=pltpu.VMEM)
    anywhere = pl.BlockSpec(memory_space=pl.ANY)
    dma = pltpu.SemaphoreType.DMA
    slots = 2 * quarter
    return pl.pallas_call(
        functools.partial(layer_kernel, nb),
        in_specs=[anywhere] + [vmem] * 8 + [anywhere],
        out_specs=[anywhere, vmem, vmem, vmem, vmem],
        out_shape=[
            jax.ShapeDtypeStruct((n_views, n_in, CELLS), BF16),
            jax.ShapeDtypeStruct((n_views, n_new, CHUNK), BF16),
            jax.ShapeDtypeStruct((n_mid, n_in), F32),
            jax.ShapeDtypeStruct((n_own, n_cols), F32),
            jax.ShapeDtypeStruct((8, 256), F32),
        ],
        scratch_shapes=[
            pltpu.VMEM((n_views, n_in, CELLS), BF16),
            pltpu.VMEM((n_views, n_in, CELLS), BF16),
            pltpu.VMEM((n_views, n_in, CELLS), BF16),
            pltpu.VMEM((n_views, n_in, CELLS), BF16),
            pltpu.VMEM((slots, MID_PAD, CELLS), F32),
            pltpu.VMEM((slots, MID_PAD, CELLS), F32),
            pltpu.VMEM((slots, MAIN, CELLS), BF16),
            pltpu.VMEM((slots, MAIN, CELLS), BF16),
            pltpu.VMEM((slots, 16, CHUNK), BF16),
            pltpu.VMEM((slots, 16, CHUNK), BF16),
            pltpu.VMEM((16, CHUNK), F32),
            pltpu.VMEM((CELLS // CHUNK, 8, CHUNK), F32),
            pltpu.VMEM((slots, MID_PAD, CELLS), F32),
            pltpu.VMEM((quarter + 1, n_cols, CELLS), BF16),
            pltpu.VMEM((quarter, MID_PAD, CELLS), F32),
            pltpu.VMEM((quarter, MID_PAD, CELLS), BF16),
            pltpu.VMEM((slots, MID_PAD, CELLS), BF16),
            pltpu.VMEM((slots, MID_PAD, CELLS), BF16),
            pltpu.VMEM((2, 2, quarter, n_new, CHUNK), BF16),
            pltpu.VMEM((2, 4, quarter, n_new, CHUNK), BF16),
            pltpu.VMEM((NEW_PAD, CELLS), F32),
            pltpu.VMEM((2, group, n_views, CELLS), BF16),
            pltpu.VMEM((CELLS // 128, max(max(group, n_new) * n_views, n_cols), 128), F32),
            pltpu.VMEM((8, 256), F32),
            pltpu.VMEM((4, 8, 256), F32),
            pltpu.VMEM((4, NEW_PAD, n_cols), BF16),
            pltpu.VMEM((n_in, MID_PAD), BF16),
            pltpu.VMEM((MID_PAD, n_in), BF16),
            pltpu.VMEM((MID_PAD, n_cols), BF16),
            pltpu.VMEM((n_cols, MID_PAD), BF16),
            pltpu.VMEM((4, nb, 8, 128), F32),
            pltpu.VMEM((2, 4, 8, 128), F32),
            pltpu.VMEM((3, 8, 128), F32),
            pltpu.VMEM((2, 8, 128), F32),
            pltpu.VMEM((6, n_in, 128), F32),
            pltpu.VMEM((8, MID_PAD, 128), F32),
            pltpu.VMEM((256, 128), F32),
            pltpu.VMEM((256, 128), F32),
            pltpu.VMEM((2, n_in, 128), F32),
            pltpu.VMEM((2, MID_PAD, 128), F32),
            pltpu.VMEM((MID_PAD, in_pad), F32),
            pltpu.VMEM((MID_PAD, n_cols), F32),
            pltpu.VMEM((4, NEW_PAD, n_cols), BF16),
            pltpu.VMEM((nb, ws_tiles, 16, 128), BF16),
            pltpu.VMEM((nb, ws_tiles, 16, 128), BF16),
            pltpu.VMEM((nb, ws_tiles, 16, 128), BF16),
            pltpu.VMEM((nb, wr_tiles, 16, 128), BF16),
            pltpu.VMEM((nb, wr_tiles, 16, 128), BF16),
            pltpu.VMEM((nb, wr_tiles, 16, 128), BF16),
            pltpu.VMEM((4, quarter, n_new, CHUNK), BF16),
            pltpu.VMEM((4, quarter, n_new, CHUNK), BF16),
            dma((n_views,)),
            dma((n_views,)),
            dma((slots,)),
            dma((slots,)),
            dma((slots, 2)),
            dma((slots, 2)),
            dma((slots,)),
            dma((slots,)),
            dma((slots, 2)),
            dma((slots, 2)),
            dma((8, nb)),
            dma((8, nb)),
            dma((8, 4)),
            dma((8, 4)),
            dma((2,)),
        ],
        compiler_params=pltpu.CompilerParams(
            collective_id=0, has_side_effects=True, vmem_limit_bytes=VMEM_LIMIT
        ),
        name="layer",
    )(views, stats, *vectors, wr_t, w_spread, d_new, d_passed)


def solution(mesh):
    nb = mesh.shape["batch"]

    def on_device(features, crops, flips, gain_in, shift_in, w_reduce, gain_mid, shift_mid, w_spread, d_passed, d_new):
        n_own, n_new = w_spread.shape[0], w_spread.shape[3]

        w9 = jnp.transpose(w_spread, (1, 2, 0, 3)).reshape(TAPS, n_own, n_new)
        crops_t, flips_t = jnp.transpose(crops, (1, 2, 0)), jnp.transpose(flips)
        swap = lambda v: jnp.transpose(v, (1, 0, 2))
        views, passed, stats = crop_views(swap(features), crops_t, flips_t)
        dv, new_maps, wr_grad, ws_grad, sums = layer(
            nb, views, stats, (gain_in, shift_in, gain_mid, shift_mid), jnp.transpose(w_reduce), w9, swap(d_new), swap(d_passed)
        )
        features_grad, new_maps, wr_grad, ws_grad, *grads = place_views(
            crops_t, flips_t, dv, new_maps, wr_grad, ws_grad, sums
        )
        ws_grad = jnp.transpose(ws_grad.reshape(3, 3, n_own, n_new), (2, 0, 1, 3))
        return (swap(passed), swap(new_maps), swap(features_grad), jnp.transpose(wr_grad), ws_grad, *grads)

    return jax.shard_map(
        on_device,
        mesh=mesh,
        in_specs=(
            P("batch", "chan", None),
            P("batch", None, None),
            P("batch", None),
            P("chan"),
            P("chan"),
            P("chan", None),
            P("chan"),
            P("chan"),
            P("chan", None, None, None),
            P("batch", "chan", None),
            P("batch", None, "chan"),
        ),
        out_specs=(
            P("batch", "chan", None),
            P("batch", None, "chan"),
            P("batch", "chan", None),
            P("chan", None),
            P("chan", None, None, None),
            P("chan"),
            P("chan"),
            P("chan"),
            P("chan"),
        ),
        check_vma=False,
    )
```

time: 189 us -> 112 us (0.59)
  local copies, waits for them, and re-layouts: 47.4 us -> 0 us
  Pallas kernels: 139 us -> 111 us
    unnamed x30 -> x0, local copies, waits for them, and re-layouts: 43 us -> none
    pallas_call x3, Pallas kernels: 139 us -> 111 us  [the longest x1 84.6 us: layer(): pl.pallas_call(functools.partial(layer_kernel, nb), in_specs=[anywhere] +...]
    slice x2 -> x0, local copies, waits for them, and re-layouts: 2.06 us -> none  [the longest x1 1.34 us: on_device(): sums[1, :n_in]]
where the time goes in v2:
time: 112 us; the launch traced here: 111 us
  Pallas kernels  111 us (99%)
    pallas_call x1, Pallas kernels, layer(): pl.pallas_call(functools.partial(layer_kernel, nb), in_specs=[anywhere] +...  84.6 us
    pallas_call x1, Pallas kernels, place_views(): pl.pallas_call(place_kernel, grid=(-(-channels // rows),), in_specs=[pl.B...  13.5 us
    pallas_call x1, Pallas kernels, crop_views(): pl.pallas_call(crop_kernel, grid=(-(-channels // rows),), in_specs=[pl.Bl...  12.4 us

profile of v2, /device:TPU:0, one launch (start us, length us, event | category | flops | bytes accessed | tf_op | source)
XLA Modules:
  0.0 111.3 jit_solution(7203942732182555409)
XLA Ops:
  0.6 12.4 %crop_views.1 = (bf16[16,157,1024]{2,1,0:T(8,128)(2,1)}, bf16[157,16,1024]{2,1,0:T(8,128)(2,1)}, f32[8,128]{1,0:T(8,128)}) custom-call(s32[2,2,8]{2,1,0:T(2,128)} %bitcast.21, s32[2,8]{1,0:T(2,128)} %bitcast.23, bf16[157,8,2304]{2,1,0:T(8,128)(2,1)} %bitcast.16), custom_call_target="tpu_custom_call" | custom-call | tf_op jit(solution)/shard_map/crop_views/pallas_call | solution.py:156
  13.0 84.6 %layer.1 = (bf16[16,157,1024]{2,1,0:T(8,128)(2,1)}, bf16[16,33,256]{2,1,0:T(8,128)(2,1)}, f32[132,157]{1,0:T(8,128)}, f32[33,432]{1,0:T(8,128)}, f32[8,256]{1,0:T(8,128)}) custom-call(bf16[16,157,1024]{2,1,0:T(8,128)(2,1)} %get-tuple-element.26.views_hbm, f32[8,128]{1,0:T(8,128)} %get-tuple-element.27.stats_ref, bf16[157]{0:T(256)(128)(2,1)} %gain_in_ref.1, ...), custom_call_target="tpu_custom_call" | custom-call | tf_op jit(solution)/shard_map/layer/pallas_call | solution.py:1051
  97.7 13.5 %place_views.1 = (f32[157,8,2304]{2,1,0:T(8,128)}, bf16[33,16,256]{2,1,0:T(8,128)(2,1)}, f32[132,157]{1,0:T(8,128)}, f32[9,33,33]{2,1,0:T(8,128)}, f32[157]{0:T(...) custom-call(s32[2,2,8]{2,1,0:T(2,128)} %bitcast.22, s32[2,8]{1,0:T(2,128)} %bitcast.24, ...), custom_call_target="tpu_custom_call" | custom-call | tf_op jit(solution)/shard_map/place_views/pallas_call | solution.py:257

commit v3 on v2

--- a/solution.py
+++ b/solution.py
@@ -17,6 +17,7 @@
 SPAN = 512
 STRIDE = 8 * GRID
 TAPS = 9
+BLOCK = 80
 MID_PAD = 144
 NEW_PAD = 48
 MAIN = 128
@@ -84,167 +85,248 @@
     return offset + row * GRID + jnp.where(flip > 0, W - 1 - col, col)
 
 
-def crop_kernel(crops_ref, flips_ref, x_ref, views_ref, passed_ref, stats_ref, pick_sc, xf_sc, xi_sc, pf_sc, mean_sc, dev_sc):
-    step = pl.program_id(0)
-    rows, items, cells = x_ref.shape
-    n_views = 2 * items
-
-    @pl.when(step == 0)
-    def _():
-        def build(n, carry):
-            j, v = n // 2, n % 2
-            _, offset = window_start(crops_ref, j, v)
-            target = chunk_target(offset, flips_ref[v, j], iota((1, CHUNK), 1))
-            pick_sc[n] = (iota((SPAN, CHUNK), 0) == target).astype(BF16)
-            return carry
-
-        lax.fori_loop(0, n_views, build, 0)
-        mean_sc[...] = jnp.zeros_like(mean_sc)
-        dev_sc[...] = jnp.zeros_like(dev_sc)
-
-    for l in range(cells // 128):
-        at = slice(128 * l, 128 * (l + 1))
-        wide_x = x_ref[:, :, at].astype(F32)
-        for ch in range(rows):
-            xf_sc[l, (items + 1) * ch : (items + 1) * ch + items, :] = wide_x[ch]
-
-    total = jnp.zeros((rows, 128), F32)
-    squares = jnp.zeros((rows, 128), F32)
-    pivot = None
-    for j in range(items):
+def blocks_of(channels):
+    return [(at, min(BLOCK, channels - at)) for at in range(0, channels, BLOCK)]
+
+
+def crop_kernel(crops_ref, flips_ref, x_hbm, views_hbm, passed_hbm, stats_ref, pick_sc, xn_sc, xf_sc, xi_sc, vw_sc, pf_sc, pn_sc, mean_sc, dev_sc, x_sem, vw_sem, pn_sem):
+    channels, items, cells = x_hbm.shape
+    n_views, rows, part_rows = 2 * items, BLOCK, 16
+    blocks = blocks_of(channels)
+
+    def load(at):
+        first, size = blocks[at]
+        return pltpu.make_async_copy(x_hbm.at[pl.ds(first, size)], xn_sc.at[at, pl.ds(0, size)], x_sem.at[at])
+
+    def view_out(at, n):
+        first = pl.multiple_of(at * rows, rows)
+        return pltpu.make_async_copy(vw_sc.at[at, n], views_hbm.at[n, pl.ds(first, rows)], vw_sem.at[at, n])
+
+    def passed_out(at, u):
+        first, size = blocks[at]
+        size = min(part_rows, size - part_rows * u)
+        return pltpu.make_async_copy(
+            pn_sc.at[at, pl.ds(part_rows * u, size)],
+            passed_hbm.at[pl.ds(first + part_rows * u, size)],
+            pn_sem.at[at, u],
+        )
+
+    for at in range(len(blocks)):
+        load(at).start()
+
+    def build(n, carry):
+        j, v = n // 2, n % 2
+        _, offset = window_start(crops_ref, j, v)
+        target = chunk_target(offset, flips_ref[v, j], iota((1, CHUNK), 1))
+        pick_sc[n] = (iota((SPAN, CHUNK), 0) == target).astype(BF16)
+        return carry
+
+    lax.fori_loop(0, n_views, build, 0)
+    mean_sc[...] = jnp.zeros_like(mean_sc)
+    dev_sc[...] = jnp.zeros_like(dev_sc)
+
+    def block(b, carry):
+        for at in range(len(blocks)):
+
+            @pl.when(b == at)
+            def _(at=at):
+                load(at).wait()
+
         for l in range(cells // 128):
-            xi_sc[j, :, 128 * l : 128 * (l + 1)] = xf_sc[l, pl.ds(j, rows, stride=items + 1), :].astype(BF16)
-        for v in range(2):
-            n = 2 * j + v
-            base, _ = window_start(crops_ref, j, v)
-            spans = [xi_sc[j, :, pl.ds(pl.multiple_of(base + STRIDE * k, 128), SPAN)] for k in range(CELLS // CHUNK)]
-            parts = dot(jnp.concatenate(spans, axis=0), pick_sc[n])
-            for k in range(CELLS // CHUNK):
-                cols = slice(CHUNK * k, CHUNK * (k + 1))
-                part = parts[rows * k : rows * (k + 1), :]
-                views_ref[n, :, cols] = part.astype(BF16)
-                for l in range(2):
-                    pf_sc[2 * k + l, pl.ds(n, rows, stride=n_views + 1), :] = part[:, 128 * l : 128 * (l + 1)]
-                if pivot is None:
-                    pivot = jnp.sum(lane_fold(part), axis=1, keepdims=True) / CHUNK
-                off = part - pivot
-                total = total + lane_fold(off)
-                squares = squares + lane_fold(off * off)
-    for l in range(CELLS // 128):
-        at = slice(128 * l, 128 * (l + 1))
-        for ch in range(rows):
-            first = (n_views + 1) * ch
-            passed_ref[ch, :, at] = pf_sc[l, first : first + n_views, :].astype(BF16)
-    count = n_views * CELLS
-    shift = jnp.sum(total, axis=1, keepdims=True) / count
-    mean = pivot + shift
-    first = pl.multiple_of(step * rows, 8)
-    lane = iota((rows, 128), 1)
-    mean_sc[pl.ds(first, rows), :] = jnp.where(lane == 0, mean, 0.0)
-    dev_sc[pl.ds(first, rows), :] = squares - jnp.where(lane == 0, shift * shift * count, 0.0)
-
-    @pl.when(step == pl.num_programs(0) - 1)
-    def _():
-        stats_ref[...] = jnp.zeros_like(stats_ref)
-        stats_ref[0:2, :] = cols_to_row(mean_sc, None)
-        stats_ref[2:4, :] = cols_to_row(dev_sc, None)
+            at = slice(128 * l, 128 * (l + 1))
+            wide_x = xn_sc[b, :, :, at].astype(F32)
+            for ch in range(rows):
+                xf_sc[l, (items + 1) * ch : (items + 1) * ch + items, :] = wide_x[ch]
+
+        total = jnp.zeros((rows, 128), F32)
+        squares = jnp.zeros((rows, 128), F32)
+        pivot = None
+        for j in range(items):
+            for l in range(cells // 128):
+                xi_sc[j, :, 128 * l : 128 * (l + 1)] = xf_sc[l, pl.ds(j, rows, stride=items + 1), :].astype(BF16)
+            for v in range(2):
+                n = 2 * j + v
+                base, _ = window_start(crops_ref, j, v)
+                spans = [xi_sc[j, :, pl.ds(pl.multiple_of(base + STRIDE * k, 128), SPAN)] for k in range(CELLS // CHUNK)]
+                parts = dot(jnp.concatenate(spans, axis=0), pick_sc[n])
+                for k in range(CELLS // CHUNK):
+                    part = parts[rows * k : rows * (k + 1), :]
+                    vw_sc[b, n, :, CHUNK * k : CHUNK * (k + 1)] = part.astype(BF16)
+                    for l in range(2):
+                        pf_sc[2 * k + l, pl.ds(n, rows, stride=n_views + 1), :] = part[:, 128 * l : 128 * (l + 1)]
+                    if pivot is None:
+                        pivot = jnp.sum(lane_fold(part), axis=1, keepdims=True) / CHUNK
+                    off = part - pivot
+                    total = total + lane_fold(off)
+                    squares = squares + lane_fold(off * off)
+                view_out(b, n).start()
+        for u in range(rows // part_rows):
+            for l in range(CELLS // 128):
+                at = slice(128 * l, 128 * (l + 1))
+                for ch in range(part_rows * u, part_rows * (u + 1)):
+                    first = (n_views + 1) * ch
+                    pn_sc[b, ch, :, at] = pf_sc[l, first : first + n_views, :].astype(BF16)
+            for at in range(len(blocks)):
+
+                @pl.when(b == at)
+                def _(at=at):
+                    passed_out(at, u).start()
+
+        count = n_views * CELLS
+        shift = jnp.sum(total, axis=1, keepdims=True) / count
+        first = pl.multiple_of(b * rows, 8)
+        lane = iota((rows, 128), 1)
+        mean_sc[pl.ds(first, rows), :] = jnp.where(lane == 0, pivot + shift, 0.0)
+        dev_sc[pl.ds(first, rows), :] = squares - jnp.where(lane == 0, shift * shift * count, 0.0)
+        return carry
+
+    lax.fori_loop(0, len(blocks), block, 0)
+    stats_ref[...] = jnp.zeros_like(stats_ref)
+    stats_ref[0:2, :] = cols_to_row(mean_sc, None)
+    stats_ref[2:4, :] = cols_to_row(dev_sc, None)
+    for at in range(len(blocks)):
+        for n in range(n_views):
+            view_out(at, n).wait()
+        for u in range(rows // part_rows):
+            passed_out(at, u).wait()
 
 
 def crop_views(features, crops, flips):
     channels, items, cells = features.shape
-    rows = 80
+    n_blocks = len(blocks_of(channels))
+    anywhere = pl.BlockSpec(memory_space=pl.ANY)
+    smem = pl.BlockSpec(memory_space=pltpu.SMEM)
+    dma = pltpu.SemaphoreType.DMA
     return pl.pallas_call(
         crop_kernel,
-        grid=(-(-channels // rows),),
-        in_specs=[
-            pl.BlockSpec(memory_space=pltpu.SMEM),
-            pl.BlockSpec(memory_space=pltpu.SMEM),
-            pl.BlockSpec((rows, items, cells), lambda s: (s, 0, 0)),
-        ],
-        out_specs=[
-            pl.BlockSpec((2 * items, rows, CELLS), lambda s: (0, s, 0)),
-            pl.BlockSpec((rows, 2 * items, CELLS), lambda s: (s, 0, 0)),
-            pl.BlockSpec((8, 128), lambda s: (0, 0)),
-        ],
+        in_specs=[smem, smem, anywhere],
+        out_specs=[anywhere, anywhere, pl.BlockSpec(memory_space=pltpu.VMEM)],
         out_shape=[
-            jax.ShapeDtypeStruct((2 * items, channels, CELLS), BF16),
+            jax.ShapeDtypeStruct((2 * items, n_blocks * BLOCK, CELLS), BF16),
             jax.ShapeDtypeStruct((channels, 2 * items, CELLS), BF16),
             jax.ShapeDtypeStruct((8, 128), F32),
         ],
         scratch_shapes=[
             pltpu.VMEM((2 * items, SPAN, CHUNK), BF16),
-            pltpu.VMEM((cells // 128, rows * (items + 1), 128), F32),
-            pltpu.VMEM((items, rows, cells), BF16),
-            pltpu.VMEM((CELLS // 128, rows * (2 * items + 1), 128), F32),
+            pltpu.VMEM((n_blocks, BLOCK, items, cells), BF16),
+            pltpu.VMEM((cells // 128, BLOCK * (items + 1), 128), F32),
+            pltpu.VMEM((items, BLOCK, cells), BF16),
+            pltpu.VMEM((n_blocks, 2 * items, BLOCK, CELLS), BF16),
+            pltpu.VMEM((CELLS // 128, BLOCK * (2 * items + 1), 128), F32),
+            pltpu.VMEM((n_blocks, BLOCK, 2 * items, CELLS), BF16),
             pltpu.VMEM((256, 128), F32),
             pltpu.VMEM((256, 128), F32),
+            dma((n_blocks,)),
+            dma((n_blocks, 2 * items)),
+            dma((n_blocks, BLOCK // 16)),
         ],
         compiler_params=pltpu.CompilerParams(vmem_limit_bytes=VMEM_LIMIT),
         name="crop_views",
     )(crops, flips, features)
 
 
-def place_kernel(crops_ref, flips_ref, dv_ref, new_ref, wrg_ref, wsg_ref, sums_ref, out_ref, newo_ref, wrgo_ref, wsgo_ref, gi_ref, si_ref, gm_ref, sm_ref, pick_sc, sum_sc, flat_sc, new_sc):
-    step = pl.program_id(0)
-    rows, items, cells = out_ref.shape
-    n_views = 2 * items
-
-    @pl.when(step == 0)
-    def _():
-        def build(n, carry):
-            j, v = n // 2, n % 2
-            _, offset = window_start(crops_ref, j, v)
-            target = chunk_target(offset, flips_ref[v, j], iota((CHUNK, 1), 0))
-            pick_sc[n] = (iota((CHUNK, SPAN), 1) == target).astype(BF16)
+def place_kernel(crops_ref, flips_ref, dv_hbm, new_ref, wrg_ref, wsg_ref, sums_ref, out_hbm, newo_ref, wrgo_ref, wsgo_ref, gi_ref, si_ref, gm_ref, sm_ref, pick_sc, dv_sc, flat_sc, out_sc, new_sc, dv_sem, out_sem):
+    channels, items, cells = out_hbm.shape
+    n_views, rows, part_rows = 2 * items, BLOCK, 16
+    blocks = blocks_of(channels)
+
+    def load(at):
+        first = at * rows if isinstance(at, int) else pl.multiple_of(at * rows, rows)
+        return pltpu.make_async_copy(dv_hbm.at[:, pl.ds(first, rows)], dv_sc.at[at], dv_sem.at[at])
+
+    def out(at, u):
+        first, size = blocks[at]
+        size = min(part_rows, size - part_rows * u)
+        return pltpu.make_async_copy(
+            out_sc.at[at, pl.ds(part_rows * u, size)],
+            out_hbm.at[pl.ds(first + part_rows * u, size)],
+            out_sem.at[at, u],
+        )
+
+    for at in range(len(blocks)):
+        load(at).start()
+
+    def build(n, carry):
+        j, v = n // 2, n % 2
+        _, offset = window_start(crops_ref, j, v)
+        target = chunk_target(offset, flips_ref[v, j], iota((CHUNK, 1), 0))
+        pick_sc[n] = (iota((CHUNK, SPAN), 1) == target).astype(BF16)
+        return carry
+
+    lax.fori_loop(0, n_views, build, 0)
+
+    def block(b, carry):
+        load(b).wait()
+        flat_sc[...] = jnp.zeros_like(flat_sc)
+
+        def place_item(j):
+            for v in range(2):
+                n = 2 * j + v
+                base, _ = window_start(crops_ref, j, v)
+                tile = base // 128
+                parts = [dv_sc[b, n, :, CHUNK * k : CHUNK * (k + 1)] for k in range(CELLS // CHUNK)]
+                spans = dot(jnp.concatenate(parts, axis=0), pick_sc[n])
+                spans = [spans[rows * k : rows * (k + 1), :] for k in range(CELLS // CHUNK)]
+                pieces = [spans[0][:, 0:STRIDE]]
+                for k in range(1, CELLS // CHUNK):
+                    pieces.append(spans[k - 1][:, STRIDE:SPAN] + spans[k][:, 0 : SPAN - STRIDE])
+                    pieces.append(spans[k][:, SPAN - STRIDE : STRIDE])
+                pieces.append(spans[-1][:, STRIDE:SPAN])
+                window = jnp.concatenate(pieces, axis=1)
+                of_item = pl.ds(j, rows, stride=items + 1)
+                for t in range(window.shape[1] // 128):
+                    piece = window[:, 128 * t : 128 * (t + 1)]
+                    if v == 1:
+                        piece = piece + flat_sc[tile + t, of_item, :]
+                    flat_sc[tile + t, of_item, :] = piece
+
+        def place_some(group, carry):
+            for inner in range(4):
+                place_item(4 * group + inner)
             return carry
 
-        lax.fori_loop(0, n_views, build, 0)
-        n_new = new_ref.shape[1]
-        for n in range(n_views):
-            for l in range(2):
-                piece = new_ref[n, :, 128 * l : 128 * (l + 1)]
-                new_sc[l, pl.ds(n, n_new, stride=n_views), :] = piece.astype(F32)
+        lax.fori_loop(0, items // 4, place_some, 0)
+        for u in range(rows // part_rows):
+            for l in range(cells // 128):
+                for ch in range(part_rows * u, part_rows * (u + 1)):
+                    first = (items + 1) * ch
+                    out_sc[b, ch, :, 128 * l : 128 * (l + 1)] = flat_sc[l, first : first + items, :]
+            for at in range(len(blocks)):
+
+                @pl.when(b == at)
+                def _(at=at):
+                    out(at, u).start()
+
+        return carry
+
+    lax.fori_loop(0, len(blocks), block, 0)
+
+    n_new = new_ref.shape[1]
+    for n in range(n_views):
         for l in range(2):
-            newo_ref[:, :, 128 * l : 128 * (l + 1)] = new_sc[l].reshape(n_new, n_views, 128).astype(BF16)
-        wrgo_ref[...] = wrg_ref[...]
-        for t in range(TAPS):
-            wsgo_ref[t] = wsg_ref[:, NEW_PAD * t : NEW_PAD * t + wsgo_ref.shape[2]]
-        for at, ref in enumerate((gi_ref, si_ref, gm_ref, sm_ref)):
-            ref[...] = sums_ref[at, 0 : ref.shape[0]]
-
-    for j in range(items):
-        sum_sc[j] = jnp.zeros_like(sum_sc[j])
-        for v in range(2):
-            n = 2 * j + v
-            base, _ = window_start(crops_ref, j, v)
-            parts = [dv_ref[n, :, CHUNK * k : CHUNK * (k + 1)] for k in range(CELLS // CHUNK)]
-            spans = dot(jnp.concatenate(parts, axis=0), pick_sc[n])
-            spans = [spans[rows * k : rows * (k + 1), :] for k in range(CELLS // CHUNK)]
-            pieces = [spans[0][:, 0:STRIDE]]
-            for k in range(1, CELLS // CHUNK):
-                pieces.append(spans[k - 1][:, STRIDE:SPAN] + spans[k][:, 0 : SPAN - STRIDE])
-                pieces.append(spans[k][:, SPAN - STRIDE : STRIDE])
-            pieces.append(spans[-1][:, STRIDE:SPAN])
-            window = jnp.concatenate(pieces, axis=1)
-            span = pl.ds(base, window.shape[1])
-            if v == 0:
-                sum_sc[j, :, span] = window
-            else:
-                sum_sc[j, :, span] += window
-        for l in range(cells // 128):
-            flat_sc[l, pl.ds(j, rows, stride=items + 1), :] = sum_sc[j, :, 128 * l : 128 * (l + 1)]
-    for l in range(cells // 128):
-        for ch in range(rows):
-            first = (items + 1) * ch
-            out_ref[ch, :, 128 * l : 128 * (l + 1)] = flat_sc[l, first : first + items, :]
+            piece = new_ref[n, :, 128 * l : 128 * (l + 1)]
+            new_sc[l, pl.ds(n, n_new, stride=n_views), :] = piece.astype(F32)
+    for l in range(2):
+        newo_ref[:, :, 128 * l : 128 * (l + 1)] = new_sc[l].reshape(n_new, n_views, 128).astype(BF16)
+    wrgo_ref[...] = wrg_ref[...]
+    for t in range(TAPS):
+        wsgo_ref[t] = wsg_ref[:, NEW_PAD * t : NEW_PAD * t + wsgo_ref.shape[2]]
+    for at, ref in enumerate((gi_ref, si_ref, gm_ref, sm_ref)):
+        ref[...] = sums_ref[at, 0 : ref.shape[0]]
+    for at in range(len(blocks)):
+        for u in range(rows // part_rows):
+            out(at, u).wait()
 
 
 def place_views(crops, flips, dv, new_maps, wr_grad, ws_grad, sums):
-    items = crops.shape[2]
-    n_views, channels, _ = dv.shape
+    items, channels = crops.shape[2], wr_grad.shape[1]
+    n_views, n_blocks = dv.shape[0], dv.shape[1] // BLOCK
     n_new, n_own = new_maps.shape[1], ws_grad.shape[0]
-    rows = 80
-    whole = lambda shape: pl.BlockSpec(shape, lambda s: (0,) * len(shape))
+    cells = GRID * GRID
+    anywhere = pl.BlockSpec(memory_space=pl.ANY)
+    vmem = pl.BlockSpec(memory_space=pltpu.VMEM)
+    smem = pl.BlockSpec(memory_space=pltpu.SMEM)
+    dma = pltpu.SemaphoreType.DMA
     small = [
         ((n_new, n_views, CHUNK), BF16),
         (wr_grad.shape, F32),
@@ -256,22 +338,18 @@
     ]
     return pl.pallas_call(
         place_kernel,
-        grid=(-(-channels // rows),),
-        in_specs=[
-            pl.BlockSpec(memory_space=pltpu.SMEM),
-            pl.BlockSpec(memory_space=pltpu.SMEM),
-            pl.BlockSpec((n_views, rows, CELLS), lambda s: (0, s, 0)),
-        ]
-        + [whole(v.shape) for v in (new_maps, wr_grad, ws_grad, sums)],
-        out_specs=[pl.BlockSpec((rows, items, GRID * GRID), lambda s: (s, 0, 0))]
-        + [whole(shape) for shape, _ in small],
-        out_shape=[jax.ShapeDtypeStruct((channels, items, GRID * GRID), F32)]
+        in_specs=[smem, smem, anywhere] + [vmem] * 4,
+        out_specs=[anywhere] + [vmem] * len(small),
+        out_shape=[jax.ShapeDtypeStruct((channels, items, cells), F32)]
         + [jax.ShapeDtypeStruct(shape, kind) for shape, kind in small],
         scratch_shapes=[
             pltpu.VMEM((n_views, CHUNK, SPAN), BF16),
-            pltpu.VMEM((items, rows, GRID * GRID), F32),
-            pltpu.VMEM((GRID * GRID // 128, rows * (items + 1), 128), F32),
+            pltpu.VMEM((n_blocks, n_views, BLOCK, CELLS), BF16),
+            pltpu.VMEM((cells // 128, BLOCK * (items + 1), 128), F32),
+            pltpu.VMEM((n_blocks, BLOCK, items, cells), F32),
             pltpu.VMEM((2, n_new * n_views, 128), F32),
+            dma((n_blocks,)),
+            dma((n_blocks, BLOCK // 16)),
         ],
         compiler_params=pltpu.CompilerParams(vmem_limit_bytes=VMEM_LIMIT),
         name="place_views",
@@ -299,6 +377,8 @@
 
 def layer_kernel(
     nb,
+    crops_ref,
+    flips_ref,
     views_hbm,
     stats_ref,
     gain_in_ref,
@@ -326,6 +406,9 @@
     far_rest,
     pack_sc,
     ext_sc,
+    packed_sc,
+    find_sc,
+    join_sc,
     d_sc,
     dcol_sc,
     mid_sc,
@@ -334,6 +417,7 @@
     dm_in,
     dno_sc,
     dn_sc,
+    pack_dn,
     dnf_sc,
     dpn_sc,
     flat_sc,
@@ -383,7 +467,7 @@
 ):
     bi, ci = lax.axis_index("batch"), lax.axis_index("chan")
     y, c = ci // 2, lax.rem(ci, 2)
-    n_views, n_in = x_sc.shape[0], x_sc.shape[1]
+    n_views, n_in = x_sc.shape[0], act_sc.shape[1]
     quarter = n_views // 4
     n_own, n_new = wsg_ref.shape[0], dnew_ref.shape[0]
     local_count = float(n_views * CELLS)
@@ -466,6 +550,10 @@
         for k in range(1, 4):
             other = lax.rem(ci + 4 - k, 4)
             chan_copy(kind, k, src_of(lax.rem(ci + k, 4)), dst.at[other]).wait()
+
+    def wide(ref, at):
+        col = ref[at]
+        return jnp.concatenate([col, col], axis=1)
 
     def same(ref):
         return lambda other: ref
@@ -484,13 +572,17 @@
     wsp_own = same(wsp_sc.at[ci])
     chan_send(1, wsp_own, wsp_sc)
 
+    pack_dn[...] = jnp.zeros_like(pack_dn)
     for l in range(2):
         at = slice(128 * l, 128 * (l + 1))
-        flat_sc[l, 0 : n_new * n_views, :] = dnew_ref[:, :, at].astype(F32).reshape(n_new * n_views, 128)
-        for n in range(n_views):
-            by_view = flat_sc[l, pl.ds(n, n_new, stride=n_views), :].astype(BF16)
-            block, q = n // quarter, n % quarter
-            dno_sc[block % 2, block // 2, q, :, at] = by_view
+        native = dnew_ref[:, :, at].astype(F32)
+        for ch in range(n_new):
+            flat_sc[l, (n_views + 1) * ch : (n_views + 1) * ch + n_views, :] = native[ch]
+        for block in range(4):
+            for q in range(quarter):
+                by_view = flat_sc[l, pl.ds(quarter * block + q, n_new, stride=n_views + 1), :]
+                pack_dn[n_new * q : n_new * (q + 1), :] = by_view
+            dno_sc[block % 2, block // 2, :, at] = pack_dn[...].astype(BF16)
     dn_sc[0, ci] = dno_sc[c, y]
     dn_sc[1, ci] = dno_sc[c, 1 - y]
     dnew_of = lambda other: dno_sc.at[lax.rem(other, 2), other // 2]
@@ -504,6 +596,9 @@
     wg_sc[...] = jnp.zeros_like(wg_sc)
     wsg_sc[...] = jnp.zeros_like(wsg_sc)
     ext_sc[...] = jnp.zeros_like(ext_sc)
+    piece, place = iota((CELLS // 2, CELLS // 2), 0), iota((CELLS // 2, CELLS // 2), 1)
+    joined_at = ((piece & 255) >> 4) * W + (piece >> 8) * 16 + (piece & 15)
+    join_sc[...] = (joined_at == place).astype(BF16)
     ws_out[...] = jnp.zeros_like(ws_out)
     wr_out[...] = jnp.zeros_like(wr_out)
     wrt_sc[...] = jnp.zeros_like(wrt_sc)
@@ -513,6 +608,14 @@
     gain_row = two_rows(own_par[0:1, :])
     shift_row = two_rows(own_par[1:2, :])
 
+    gain_col, shift_col = (jnp.transpose(jnp.broadcast_to(one_row(v), (256, 256)))[0:n_in, 0:128] for v in (gain_row, shift_row))
+    guess = None
+    for weight, offset in ((2 / 3, 0.0), (1 / 6, 3.0**0.5), (1 / 6, -(3.0**0.5))):
+        pre = shift_col + offset * gain_col
+        part = weight * pre * sigmoid(pre)
+        guess = part if guess is None else guess + part
+    colm_sc[7] = dot(wrt_sc[...], guess.astype(BF16))
+
     batch_wait(0, same(stats_ref), stat_sc.at[0])
     mean_row, dev_row = combine(stat_sc[0], local_count)
     rstd_row = lax.rsqrt(dev_row / pixels + EPS)
@@ -521,10 +624,6 @@
     row_to_cols(col_sc.at[2], rstd_row * gain_row)
     row_to_cols(col_sc.at[3], shift_row)
 
-    def wide(ref, at):
-        col = ref[at]
-        return jnp.concatenate([col, col], axis=1)
-
     def chunks(start=0, count=CELLS // CHUNK):
         if isinstance(start, int):
             return [slice(start + CHUNK * k, start + CHUNK * (k + 1)) for k in range(count)]
@@ -538,14 +637,14 @@
     def activate(n):
         mean, scale, shift = wide(col_sc, 0), wide(col_sc, 2), wide(col_sc, 3)
         for cols in chunks():
-            pre = (x_sc[n, :, cols].astype(F32) - mean) * scale + shift
+            pre = (x_sc[n, 0:n_in, cols].astype(F32) - mean) * scale + shift
             s = sigmoid(pre)
             act = pre * s
-            slope_sc[n, :, cols] = (s + act * (1.0 - s)).astype(BF16)
+            slope_sc[n, 0:n_in, cols] = (s + act * (1.0 - s)).astype(BF16)
             act_sc[n, :, cols] = act.astype(BF16)
 
     def partial(n, cols):
-        return dot(wrt_sc[...], act_sc[n, :, cols])
+        return dot(wrt_sc[...], act_sc[n, :, cols]) - wide(colm_sc, 7)
 
     def half_copy(i):
         return pltpu.make_async_remote_copy(
@@ -574,15 +673,62 @@
     def with_rest(main, k):
         return jnp.concatenate([main, ext_sc[k], jnp.zeros((8, CHUNK), F32)], axis=0)
 
-    def far_start(i):
-        rest_copy(i).start()
-        far_copy(i, 0).start()
-        far_copy(i, 1).start()
-
-    def far_copy(i, h):
+    def quarter_of(i):
+        j = slot_view(i, c) // 2
+        row_half = jnp.where(crops_ref[1, 0, j] >= crops_ref[0, 0, j], 0, 1)
+        col_half = jnp.where(crops_ref[1, 1, j] >= crops_ref[0, 1, j], 0, 1)
+        return j, row_half, jnp.where(flips_ref[1, j] > 0, 1 - col_half, col_half)
+
+    def arriving(m):
+        return lax.rem(2 * m + quarter, 2 * quarter)
+
+    def find_quarter(m, carry):
+        j, row_half, col_half = quarter_of(arriving(m))
+        cell = iota((1, CHUNK), 1)
+        row, col = (cell >> 4) + 16 * row_half, (cell & 15) + 16 * col_half
+        col = jnp.where(flips_ref[1, j] > 0, W - 1 - col, col)
+        row = row + crops_ref[1, 0, j] - crops_ref[0, 0, j]
+        col = col + crops_ref[1, 1, j] - crops_ref[0, 1, j]
+        col = jnp.where(flips_ref[0, j] > 0, W - 1 - col, col)
+        find_sc[m] = (iota((CELLS, CHUNK), 0) == row * W + col).astype(BF16)
+        return carry
+
+    def pack_second(m):
+        _, row_half, col_half = quarter_of(2 * m)
+        low, high = pair_sc[2 * m + 1, :, 0:half], pair_sc[2 * m + 1, :, half:CELLS]
+        columns = dot_nt(jnp.where(row_half == 0, low, high), join_sc[...])
+        kept = jnp.where(col_half == 0, columns[:, CHUNK:half], columns[:, 0:CHUNK])
+        packed_sc[m, :, 0:half] = jnp.where(row_half == 0, high, low)
+        packed_sc[m, :, half : half + CHUNK] = kept.astype(BF16)
+
+    def unpack_second(m):
+        far_copy(m, 1, 0).wait_recv()
+        far_copy(m, 1, 1).wait_recv()
+        _, row_half, col_half = quarter_of(arriving(m))
+        whole = far_sc[2 * m + 1, :, 0:half]
+        kept = far_sc[2 * m + 1, :, half : half + CHUNK]
+        found = dot(far_sc[2 * m], find_sc[m]).astype(BF16)
+        left, right = jnp.where(col_half == 0, found, kept), jnp.where(col_half == 0, kept, found)
+        joined = dot(jnp.concatenate([left, right], axis=1), join_sc[...]).astype(BF16)
+        far_sc[2 * m + 1, :, 0:half] = jnp.where(row_half == 0, joined, whole)
+        far_sc[2 * m + 1, :, half:CELLS] = jnp.where(row_half == 0, whole, joined)
+
+    def far_start(m, v):
+        rest_copy(2 * m + v).start()
+        far_copy(m, v, 0).start()
+        far_copy(m, v, 1).start()
+
+    def far_copy(m, v, h):
+        i = 2 * m + v
+        if v == 0:
+            cols = half_cols(h)
+            src = pair_sc.at[i, :, cols]
+        else:
+            cols = pl.ds(half * h, half if h == 0 else CHUNK)
+            src = packed_sc.at[m, :, cols]
         return pltpu.make_async_remote_copy(
-            src_ref=pair_sc.at[i, :, half_cols(h)],
-            dst_ref=far_sc.at[i, :, half_cols(h)],
+            src_ref=src,
+            dst_ref=far_sc.at[i, :, cols],
             send_sem=far_s.at[i, h],
             recv_sem=far_r.at[i, h],
             device_id=across,
@@ -594,37 +740,43 @@
         load(theirs).wait()
         activate(theirs)
         for cols in chunks():
-            half_out[i, :, cols] = partial(theirs, cols)
+            half_out[i, :, cols] = partial(theirs, cols).astype(BF16)
         half_copy(i).start()
 
-    def forward(i, carry):
-        @pl.when(i < 2 * quarter - 1)
-        def _():
-            to_mate(i + 1)
-
-        mine = slot_view(i, c)
-        load(mine).wait()
-        activate(mine)
-        half_copy(i).wait_recv()
-        for k, cols in enumerate(chunks()):
-            both = partial(mine, cols) + half_in[i, :, cols]
-            pair_sc[i, :, cols] = both[0:MAIN, :].astype(BF16)
-            pack_sc[REST * k : REST * (k + 1), :] = both[MAIN : MAIN + REST, :]
-
-            @pl.when(i >= quarter)
+    def forward(m, carry):
+        for v in range(2):
+            i = 2 * m + v
+
+            @pl.when(i < 2 * quarter - 1)
             def _():
-                mid_sc[i - quarter, :, cols] = both
-
-        pair_rest[i] = pack_sc[...].astype(BF16)
-
-        @pl.when(i < quarter)
-        def _():
-            far_start(i)
+                to_mate(i + 1)
+
+            mine = slot_view(i, c)
+            load(mine).wait()
+            activate(mine)
+            half_copy(i).wait_recv()
+            for k, cols in enumerate(chunks()):
+                both = partial(mine, cols) + half_in[i, :, cols].astype(F32)
+                pair_sc[i, :, cols] = both[0:MAIN, :].astype(BF16)
+                pack_sc[REST * k : REST * (k + 1), :] = both[MAIN : MAIN + REST, :]
+
+                @pl.when(i >= quarter)
+                def _():
+                    mid_sc[i - quarter, :, cols] = both
+
+            pair_rest[i] = pack_sc[...].astype(BF16)
+            if v == 1:
+                pack_second(m)
+
+            @pl.when(i < quarter)
+            def _():
+                far_start(m, v)
 
         return carry
 
     to_mate(0)
-    lax.fori_loop(0, 2 * quarter, forward, 0)
+    lax.fori_loop(0, quarter, forward, 0)
+    lax.fori_loop(0, quarter, find_quarter, 0)
 
     chan_wait(1, wsp_own, wsp_sc)
     stacked = wsp_sc[...].reshape(4 * NEW_PAD, TAPS * NEW_PAD)
@@ -661,7 +813,10 @@
         far = jnp.where(i < quarter, 1, 0)
         keep = jnp.where(i < quarter, quarter, i - quarter)
         for b in range(4):
-            dnf_sc[0:n_new, CHUNK * b : CHUNK * (b + 1)] = dn_sc[far, b, lax.rem(i, quarter)].astype(F32)
+            for l in range(2):
+                pack_dn[...] = dn_sc[far, b, :, 128 * l : 128 * (l + 1)].astype(F32)
+                at = CHUNK * b + 128 * l
+                dnf_sc[0:n_new, at : at + 128] = pack_dn[pl.ds(n_new * lax.rem(i, quarter), n_new), :]
         grad = dnf_sc[...]
         for b in range(3):
             moved = at_offset(grad, 0, 1 - b)
@@ -707,12 +862,12 @@
         dp_split(k, group)
         return carry
 
+    def dp_some(first, last):
+        lax.fori_loop(first, last, dp_step, 0)
+
+    early = full - 2
     dp_load(0, group).start()
-    lax.fori_loop(0, full, dp_step, 0)
-    if left > 0:
-        dp_load(full, left).start()
-        dp_load(full, left).wait()
-        dp_split(full, left)
+    dp_some(0, early)
 
     chan_wait(0, same(own_par), par_sc)
 
@@ -727,10 +882,22 @@
     row_to_cols(colm_sc.at[2], gathered(2))
     row_to_cols(colm_sc.at[3], gathered(3))
 
-    def middle_view(q):
+    def middle_view(q, first):
         rest_copy(q).wait_recv()
-        far_copy(q, 0).wait_recv()
-        far_copy(q, 1).wait_recv()
+
+        def arrive_first():
+            far_copy(q // 2, 0, 0).wait_recv()
+            far_copy(q // 2, 0, 1).wait_recv()
+
+        if first:
+            arrive_first()
+        else:
+            pl.when(lax.rem(q, 2) == 0)(arrive_first)
+
+            @pl.when(lax.rem(q, 2) == 1)
+            def _():
+                unpack_second(q // 2)
+
         unpack_rest(far_rest[q].astype(F32))
         for k, cols in enumerate(chunks()):
             mid_sc[q, :, cols] = mid_sc[q, :, cols] + with_rest(far_sc[q, :, cols].astype(F32), k)
@@ -738,11 +905,11 @@
     def middle_sums(q, carry):
         @pl.when(q > 0)
         def _():
-            middle_view(q)
+            middle_view(q, False)
 
         first, second = None, None
         for cols in chunks():
-            part = mid_sc[q, :, cols] - wide(colm_sc, 7)
+            part = mid_sc[q, :, cols] - wide(colm_sc, 8)
             one, two = lane_fold(part), lane_fold(part * part)
             first = one if first is None else first + one
             second = two if second is None else second + two
@@ -750,9 +917,9 @@
         accm_sc[1] += second
         return carry
 
-    middle_view(0)
+    middle_view(0, True)
     pivot = sum(lane_fold(mid_sc[0, :, cols]) for cols in chunks())
-    colm_sc[7] = jnp.broadcast_to(jnp.sum(pivot, axis=1, keepdims=True) / CELLS, colm_sc.shape[1:])
+    colm_sc[8] = jnp.broadcast_to(jnp.sum(pivot, axis=1, keepdims=True) / CELLS, colm_sc.shape[1:])
     pivot_row = cols_to_row(padm_sc, pivot) / CELLS
     lax.fori_loop(0, quarter, middle_sums, 0)
     off_row = cols_to_row(padm_sc, accm_sc[0]) / owned_count
@@ -763,7 +930,12 @@
     cstat_sc[0, ci] = cmsg_sc[0]
     chan_send(3, same(cmsg_sc.at[0]), cstat_sc.at[0])
     chan_send(7, dfar_of, dn_sc.at[1])
-    far_start(quarter)
+    far_start(quarter // 2, 0)
+    dp_some(early, full)
+    if left > 0:
+        dp_load(full, left).start()
+        dp_load(full, left).wait()
+        dp_split(full, left)
     chan_wait(3, same(cmsg_sc.at[0]), cstat_sc.at[0])
     group_mean, group_dev = combine(cstat_sc[0], owned_count)
     msg_sc[0] = jnp.zeros_like(msg_sc[0])
@@ -809,7 +981,7 @@
     cstat_sc[1, ci] = cmsg_sc[1]
     chan_send(4, same(cmsg_sc.at[1]), cstat_sc.at[1])
     for q in range(1, quarter):
-        far_start(quarter + q)
+        far_start((quarter + q) // 2, q % 2)
 
     def tiles_of(ref):
         rows, cols = ref.shape
@@ -898,20 +1070,19 @@
     def store(n):
         return pltpu.make_async_copy(slope_sc.at[n], dv_hbm.at[n], store_sem.at[n])
 
-    def back_part(n, dm_ref, h):
+    def back_view(n, dm_ref):
         mean, rstd, scale = wide(col_sc, 0), wide(col_sc, 1), wide(col_sc, 2)
         first, second = None, None
-        for cols in chunks(h * half, half // CHUNK):
-            grad = dot(wr_sc[...], dm_ref[:, cols]) * slope_sc[n, :, cols].astype(F32)
-            slope_sc[n, :, cols] = (grad * scale + dp_sc[n, :, cols].astype(F32)).astype(BF16)
-            norm = (x_sc[n, :, cols].astype(F32) - mean) * rstd
+        for cols in chunks():
+            grad = dot(wr_sc[...], dm_ref[:, cols]) * slope_sc[n, 0:n_in, cols].astype(F32)
+            slope_sc[n, 0:n_in, cols] = (grad * scale + dp_sc[n, :, cols].astype(F32)).astype(BF16)
+            norm = (x_sc[n, 0:n_in, cols].astype(F32) - mean) * rstd
             one, two = lane_fold(grad), lane_fold(grad * norm)
             first = one if first is None else first + one
             second = two if second is None else second + two
         acc_sc[0] += first
         acc_sc[1] += second
-        cols = half_cols(h)
-        wg_sc[:, 0:n_in] += dot_nt(dm_ref[:, cols], act_sc[n, :, cols])
+        wg_sc[:, 0:n_in] += dot_nt(dm_ref[...], act_sc[n])
 
     def dm_own(q, carry):
         i = quarter + q
@@ -924,42 +1095,53 @@
 
     lax.fori_loop(0, quarter, dm_own, 0)
 
-    def back_mate(i, h):
-        dm_copy(i, h).wait_recv()
-        back_part(slot_view(i, 1 - c), dm_in.at[i], h)
-
-    def back_own(t, carry):
-        i, h = quarter + t // 2, lax.rem(t, 2)
-        back_part(slot_view(i, c), dm_out.at[i], h)
-        back_mate(i, h)
-        return carry
-
-    lax.fori_loop(0, 2 * quarter, back_own, 0)
-
-    def back_far(t, carry):
-        q, h = t // 2, lax.rem(t, 2)
-        @pl.when(h == 0)
+    def back_mate(i):
+        dm_copy(i, 0).wait_recv()
+        dm_copy(i, 1).wait_recv()
+        back_view(slot_view(i, 1 - c), dm_in.at[i])
+
+    def back_own(q, carry):
+        back_view(slot_view(quarter + q, c), dm_out.at[quarter + q])
+
+        @pl.when(q > 0)
         def _():
-            rest_copy(quarter + q).wait_recv()
-            unpack_rest(pair_rest[q].astype(F32) + far_rest[quarter + q].astype(F32))
-
-        far_copy(quarter + q, h).wait_recv()
-        for k, cols in enumerate(chunks(h * half, half // CHUNK)):
+            back_mate(quarter + q - 1)
+
+        return carry
+
+    lax.fori_loop(0, quarter, back_own, 0)
+    back_mate(2 * quarter - 1)
+
+    def back_far(q, carry):
+        m = quarter // 2 + q // 2
+        rest_copy(quarter + q).wait_recv()
+        unpack_rest(pair_rest[q].astype(F32) + far_rest[quarter + q].astype(F32))
+
+        @pl.when(lax.rem(q, 2) == 0)
+        def _():
+            far_copy(m, 0, 0).wait_recv()
+            far_copy(m, 0, 1).wait_recv()
+
+        @pl.when(lax.rem(q, 2) == 1)
+        def _():
+            unpack_second(m)
+
+        for k, cols in enumerate(chunks()):
             part = pair_sc[q, :, cols].astype(F32) + far_sc[quarter + q, :, cols].astype(F32)
-            part = with_rest(part, half // CHUNK * h + k)
-            norm, act, slope = mid_point(part)
+            norm, act, slope = mid_point(with_rest(part, k))
             grad = d_sc[q, :, cols] * slope - wide(colm_sc, 4) - norm * wide(colm_sc, 5)
             dm_out[q, :, cols] = (grad * wide(colm_sc, 6)).astype(BF16)
-        dm_copy(q, h).start()
-        back_part(slot_view(q, c), dm_out.at[q], h)
-
-        @pl.when(t > 0)
+            if k % 2 == 1:
+                dm_copy(q, k // 2).start()
+        back_view(slot_view(q, c), dm_out.at[q])
+
+        @pl.when(q > 0)
         def _():
-            back_mate((t - 1) // 2, lax.rem(t + 1, 2))
-
-        return carry
-
-    lax.fori_loop(0, quarter, back_far, 0)
+            back_mate(q - 1)
+
+        return carry
+
+    lax.fori_loop(0, quarter // 2, back_far, 0)
     gather(spread_refs, 4, wsg_sc)
     for b in range(4):
         wsp_sc[b, 0:40, :] = wsg_sc[n_own * b : n_own * b + 40, :].astype(BF16)
@@ -967,15 +1149,15 @@
     wsg_of = lambda other: wsp_sc.at[other]
     chan_send(6, wsg_of, wsgi_sc)
     chan_send(5, new_of, newi_sc)
-    lax.fori_loop(quarter, 2 * quarter, back_far, 0)
-    back_mate(quarter - 1, 1)
-
+    lax.fori_loop(quarter // 2, quarter, back_far, 0)
+    back_mate(quarter - 1)
+
+    scatter(reduce_refs, 6, wg_sc)
     msg_sc[2] = jnp.zeros_like(msg_sc[2])
     msg_sc[2, 0:2, :] = cols_to_row(padc_sc, acc_sc[0])
     msg_sc[2, 2:4, :] = cols_to_row(padc_sc, acc_sc[1])
     stat_sc[3, bi] = msg_sc[2]
     batch_send(3, same(msg_sc.at[2]), stat_sc.at[3])
-    scatter(reduce_refs, 6, wg_sc)
     batch_wait(3, same(msg_sc.at[2]), stat_sc.at[3])
     total = stat_sc[3, 0]
     for at in range(1, nb):
@@ -988,8 +1170,8 @@
     def finish(n, carry):
         mean, slant, level = wide(col_sc, 0), wide(col_sc, 4), wide(col_sc, 5)
         for cols in chunks():
-            rest = (x_sc[n, :, cols].astype(F32) - mean) * slant + level
-            slope_sc[n, :, cols] = (slope_sc[n, :, cols].astype(F32) + rest).astype(BF16)
+            rest = (x_sc[n, 0:n_in, cols].astype(F32) - mean) * slant + level
+            slope_sc[n, 0:n_in, cols] = (slope_sc[n, 0:n_in, cols].astype(F32) + rest).astype(BF16)
         store(n).start()
         return carry
 
@@ -1026,63 +1208,76 @@
         half_copy(i).wait_send()
         rest_copy(i).wait_send()
         for h in range(2):
-            far_copy(i, h).wait_send()
             dm_copy(i, h).wait_send()
         return carry
 
     lax.fori_loop(0, 2 * quarter, sent, 0)
 
-
-def layer(nb, views, stats, vectors, wr_t, w_spread, d_new, d_passed):
-    n_views, n_in, _ = views.shape
-    n_mid = wr_t.shape[0]
+    def sent_far(m, carry):
+        for v in range(2):
+            for h in range(2):
+                far_copy(m, v, h).wait_send()
+        return carry
+
+    lax.fori_loop(0, quarter, sent_far, 0)
+
+
+def layer(nb, crops, flips, views, stats, vectors, wr_t, w_spread, d_new, d_passed):
+    n_views, n_rows, _ = views.shape
+    n_mid, n_in = wr_t.shape
     n_own = n_mid // 4
     quarter = n_views // 4
     n_new = d_new.shape[0]
     n_cols = TAPS * NEW_PAD
+    together = -(-quarter * n_new // 16) * 16
     in_pad = -(-n_in // 16) * 16
     ws_tiles = -(-(MID_PAD // 16 * -(-n_cols // 128)) // nb)
     wr_tiles = -(-(MID_PAD // 16 * -(-in_pad // 128)) // nb)
     group = 16
     vmem = pl.BlockSpec(memory_space=pltpu.VMEM)
     anywhere = pl.BlockSpec(memory_space=pl.ANY)
+    smem = pl.BlockSpec(memory_space=pltpu.SMEM)
     dma = pltpu.SemaphoreType.DMA
     slots = 2 * quarter
     return pl.pallas_call(
         functools.partial(layer_kernel, nb),
-        in_specs=[anywhere] + [vmem] * 8 + [anywhere],
+        in_specs=[smem, smem, anywhere] + [vmem] * 8 + [anywhere],
         out_specs=[anywhere, vmem, vmem, vmem, vmem],
         out_shape=[
-            jax.ShapeDtypeStruct((n_views, n_in, CELLS), BF16),
+            jax.ShapeDtypeStruct((n_views, n_rows, CELLS), BF16),
             jax.ShapeDtypeStruct((n_views, n_new, CHUNK), BF16),
             jax.ShapeDtypeStruct((n_mid, n_in), F32),
             jax.ShapeDtypeStruct((n_own, n_cols), F32),
             jax.ShapeDtypeStruct((8, 256), F32),
         ],
         scratch_shapes=[
+            pltpu.VMEM((n_views, n_rows, CELLS), BF16),
             pltpu.VMEM((n_views, n_in, CELLS), BF16),
+            pltpu.VMEM((n_views, n_rows, CELLS), BF16),
             pltpu.VMEM((n_views, n_in, CELLS), BF16),
-            pltpu.VMEM((n_views, n_in, CELLS), BF16),
-            pltpu.VMEM((n_views, n_in, CELLS), BF16),
-            pltpu.VMEM((slots, MID_PAD, CELLS), F32),
-            pltpu.VMEM((slots, MID_PAD, CELLS), F32),
+            pltpu.VMEM((slots, MID_PAD, CELLS), BF16),
+            pltpu.VMEM((slots, MID_PAD, CELLS), BF16),
             pltpu.VMEM((slots, MAIN, CELLS), BF16),
             pltpu.VMEM((slots, MAIN, CELLS), BF16),
             pltpu.VMEM((slots, 16, CHUNK), BF16),
             pltpu.VMEM((slots, 16, CHUNK), BF16),
             pltpu.VMEM((16, CHUNK), F32),
             pltpu.VMEM((CELLS // CHUNK, 8, CHUNK), F32),
+            pltpu.VMEM((quarter, MAIN, CELLS // 2 + CHUNK), BF16),
+            pltpu.VMEM((quarter, CELLS, CHUNK), BF16),
+            pltpu.VMEM((CELLS // 2, CELLS // 2), BF16),
             pltpu.VMEM((slots, MID_PAD, CELLS), F32),
             pltpu.VMEM((quarter + 1, n_cols, CELLS), BF16),
             pltpu.VMEM((quarter, MID_PAD, CELLS), F32),
             pltpu.VMEM((quarter, MID_PAD, CELLS), BF16),
             pltpu.VMEM((slots, MID_PAD, CELLS), BF16),
             pltpu.VMEM((slots, MID_PAD, CELLS), BF16),
-            pltpu.VMEM((2, 2, quarter, n_new, CHUNK), BF16),
-            pltpu.VMEM((2, 4, quarter, n_new, CHUNK), BF16),
+            pltpu.VMEM((2, 2, together, CHUNK), BF16),
+            pltpu.VMEM((2, 4, together, CHUNK), BF16),
+            pltpu.VMEM((together, 128), F32),
             pltpu.VMEM((NEW_PAD, CELLS), F32),
             pltpu.VMEM((2, group, n_views, CELLS), BF16),
-            pltpu.VMEM((CELLS // 128, max(max(group, n_new) * n_views, n_cols), 128), F32),
+            pltpu.VMEM((CELLS // 128, max(max(group, n_new) * (n_views + 1), n_cols), 128), F32),
             pltpu.VMEM((8, 256), F32),
             pltpu.VMEM((4, 8, 256), F32),
             pltpu.VMEM((4, NEW_PAD, n_cols), BF16),
@@ -1095,7 +1290,7 @@
             pltpu.VMEM((3, 8, 128), F32),
             pltpu.VMEM((2, 8, 128), F32),
             pltpu.VMEM((6, n_in, 128), F32),
-            pltpu.VMEM((8, MID_PAD, 128), F32),
+            pltpu.VMEM((9, MID_PAD, 128), F32),
             pltpu.VMEM((256, 128), F32),
             pltpu.VMEM((256, 128), F32),
             pltpu.VMEM((2, n_in, 128), F32),
@@ -1131,7 +1326,7 @@
             collective_id=0, has_side_effects=True, vmem_limit_bytes=VMEM_LIMIT
         ),
         name="layer",
-    )(views, stats, *vectors, wr_t, w_spread, d_new, d_passed)
+    )(crops, flips, views, stats, *vectors, wr_t, w_spread, d_new, d_passed)
 
 
 def solution(mesh):
@@ -1145,7 +1340,7 @@
         swap = lambda v: jnp.transpose(v, (1, 0, 2))
         views, passed, stats = crop_views(swap(features), crops_t, flips_t)
         dv, new_maps, wr_grad, ws_grad, sums = layer(
-            nb, views, stats, (gain_in, shift_in, gain_mid, shift_mid), jnp.transpose(w_reduce), w9, swap(d_new), swap(d_passed)
+            nb, crops_t, flips_t, views, stats, (gain_in, shift_in, gain_mid, shift_mid), jnp.transpose(w_reduce), w9, swap(d_new), swap(d_passed)
         )
         features_grad, new_maps, wr_grad, ws_grad, *grads = place_views(
             crops_t, flips_t, dv, new_maps, wr_grad, ws_grad, sums

time: 112 us -> 103 us (0.920)
  Pallas kernels: 111 us -> 102 us
    pallas_call x3, Pallas kernels: 111 us -> 102 us  [the longest x1 79.2 us: layer(): pl.pallas_call(functools.partial(layer_kernel, nb), in_specs=[smem, smem,...]
where the time goes in v3:
time: 103 us
  Pallas kernels  102 us (99%)
    pallas_call x1, Pallas kernels, layer(): pl.pallas_call(functools.partial(layer_kernel, nb), in_specs=[smem, smem,...  79.2 us
    pallas_call x1, Pallas kernels, crop_views(): pl.pallas_call(crop_kernel, in_specs=[smem, smem, anywhere], out_specs=[a...  12.1 us
    pallas_call x1, Pallas kernels, place_views(): pl.pallas_call(place_kernel, in_specs=[smem, smem, anywhere] + [vmem] * 4...  10.8 us

profile of v3, /device:TPU:0, one launch (start us, length us, event | category | flops | bytes accessed | tf_op | source)
XLA Modules:
  0.0 102.9 jit_solution(13296918596885563516)
XLA Ops:
  0.6 12.1 %crop_views.1 = (bf16[16,160,1024]{2,1,0:T(8,128)(2,1)}, bf16[157,16,1024]{2,1,0:T(8,128)(2,1)}, f32[8,128]{1,0:T(8,128)}) custom-call(s32[2,2,8]{2,1,0:T(2,128)} %bitcast.21, s32[2,8]{1,0:T(2,128)} %bitcast.24, bf16[157,8,2304]{2,1,0:T(8,128)(2,1)} %bitcast.16), custom_call_target="tpu_custom_call" | custom-call | tf_op jit(solution)/shard_map/crop_views/pallas_call | solution.py:200
  12.8 79.2 %layer.1 = (bf16[16,160,1024]{2,1,0:T(8,128)(2,1)}, bf16[16,33,256]{2,1,0:T(8,128)(2,1)}, f32[132,157]{1,0:T(8,128)}, f32[33,432]{1,0:T(8,128)}, f32[8,256]{1,0:T(8,128)}) custom-call(s32[2,2,8]{2,1,0:T(2,128)} %bitcast.22, s32[2,8]{1,0:T(2,128)} %bitcast.25, bf16[16,160,1024]{2,1,0:T(8,128)(2,1)} %get-tuple-element.26.views_hbm, ...), custom_call_target="tpu_custom_call" | custom-call | tf_op jit(solution)/shard_map/layer/pallas_call | solution.py:1242
  91.9 10.8 %place_views.1 = (f32[157,8,2304]{2,1,0:T(8,128)}, bf16[33,16,256]{2,1,0:T(8,128)(2,1)}, f32[132,157]{1,0:T(8,128)}, f32[9,33,33]{2,1,0:T(8,128)}, f32[157]{0:T(...) custom-call(s32[2,2,8]{2,1,0:T(2,128)} %bitcast.23, s32[2,8]{1,0:T(2,128)} %bitcast.26, ...), custom_call_target="tpu_custom_call" | custom-call | tf_op jit(solution)/shard_map/place_views/pallas_call | solution.py:339

commit v4 on v3

--- a/solution.py
+++ b/solution.py
@@ -570,7 +570,6 @@
         dnf_sc[0:n_own, NEW_PAD * t : NEW_PAD * t + n_new] = wsp_in[t].astype(F32)
     wsp_sc[ci] = dnf_sc[:, 0 : TAPS * NEW_PAD].astype(BF16)
     wsp_own = same(wsp_sc.at[ci])
-    chan_send(1, wsp_own, wsp_sc)
 
     pack_dn[...] = jnp.zeros_like(pack_dn)
     for l in range(2):
@@ -588,6 +587,7 @@
     dnew_of = lambda other: dno_sc.at[lax.rem(other, 2), other // 2]
     dfar_of = lambda other: dno_sc.at[lax.rem(other, 2), 1 - other // 2]
     chan_send(2, dnew_of, dn_sc.at[0])
+    chan_send(1, wsp_own, wsp_sc)
 
     padc_sc[...] = jnp.zeros_like(padc_sc)
     padm_sc[...] = jnp.zeros_like(padm_sc)
@@ -646,12 +646,12 @@
     def partial(n, cols):
         return dot(wrt_sc[...], act_sc[n, :, cols]) - wide(colm_sc, 7)
 
-    def half_copy(i):
+    def half_copy(i, h):
         return pltpu.make_async_remote_copy(
-            src_ref=half_out.at[i],
-            dst_ref=half_in.at[i],
-            send_sem=half_s.at[i],
-            recv_sem=half_r.at[i],
+            src_ref=half_out.at[i, :, half_cols(h)],
+            dst_ref=half_in.at[i, :, half_cols(h)],
+            send_sem=half_s.at[i, h],
+            recv_sem=half_r.at[i, h],
             device_id=mate,
             device_id_type=MESH,
         )
@@ -739,9 +739,10 @@
         theirs = slot_view(i, 1 - c)
         load(theirs).wait()
         activate(theirs)
-        for cols in chunks():
+        for k, cols in enumerate(chunks()):
             half_out[i, :, cols] = partial(theirs, cols).astype(BF16)
-        half_copy(i).start()
+            if k % 2 == 1:
+                half_copy(i, k // 2).start()
 
     def forward(m, carry):
         for v in range(2):
@@ -754,8 +755,9 @@
             mine = slot_view(i, c)
             load(mine).wait()
             activate(mine)
-            half_copy(i).wait_recv()
             for k, cols in enumerate(chunks()):
+                if k % 2 == 0:
+                    half_copy(i, k // 2).wait_recv()
                 both = partial(mine, cols) + half_in[i, :, cols].astype(F32)
                 pair_sc[i, :, cols] = both[0:MAIN, :].astype(BF16)
                 pack_sc[REST * k : REST * (k + 1), :] = both[MAIN : MAIN + REST, :]
@@ -764,19 +766,30 @@
                 def _():
                     mid_sc[i - quarter, :, cols] = both
 
+                if v == 0 and k % 2 == 1:
+
+                    @pl.when(i < quarter)
+                    def _(h=k // 2):
+                        far_copy(m, 0, h).start()
+
             pair_rest[i] = pack_sc[...].astype(BF16)
             if v == 1:
                 pack_second(m)
 
             @pl.when(i < quarter)
             def _():
-                far_start(m, v)
+                rest_copy(i).start()
+                if v == 1:
+                    far_copy(m, 1, 0).start()
+                    far_copy(m, 1, 1).start()
 
         return carry
 
     to_mate(0)
     lax.fori_loop(0, quarter, forward, 0)
     lax.fori_loop(0, quarter, find_quarter, 0)
+
+    chan_send(7, dfar_of, dn_sc.at[1])
 
     chan_wait(1, wsp_own, wsp_sc)
     stacked = wsp_sc[...].reshape(4 * NEW_PAD, TAPS * NEW_PAD)
@@ -929,8 +942,8 @@
     accm_sc[...] = jnp.zeros_like(accm_sc)
     cstat_sc[0, ci] = cmsg_sc[0]
     chan_send(3, same(cmsg_sc.at[0]), cstat_sc.at[0])
-    chan_send(7, dfar_of, dn_sc.at[1])
     far_start(quarter // 2, 0)
+    far_start(quarter // 2, 1)
     dp_some(early, full)
     if left > 0:
         dp_load(full, left).start()
@@ -980,7 +993,7 @@
     cmsg_sc[1, 2:4, :] = cols_to_row(padm_sc, accm_sc[1])
     cstat_sc[1, ci] = cmsg_sc[1]
     chan_send(4, same(cmsg_sc.at[1]), cstat_sc.at[1])
-    for q in range(1, quarter):
+    for q in range(2, quarter):
         far_start((quarter + q) // 2, q % 2)
 
     def tiles_of(ref):
@@ -1071,13 +1084,13 @@
         return pltpu.make_async_copy(slope_sc.at[n], dv_hbm.at[n], store_sem.at[n])
 
     def back_view(n, dm_ref):
-        mean, rstd, scale = wide(col_sc, 0), wide(col_sc, 1), wide(col_sc, 2)
+        mean, scale = wide(col_sc, 0), wide(col_sc, 2)
         first, second = None, None
         for cols in chunks():
             grad = dot(wr_sc[...], dm_ref[:, cols]) * slope_sc[n, 0:n_in, cols].astype(F32)
             slope_sc[n, 0:n_in, cols] = (grad * scale + dp_sc[n, :, cols].astype(F32)).astype(BF16)
-            norm = (x_sc[n, 0:n_in, cols].astype(F32) - mean) * rstd
-            one, two = lane_fold(grad), lane_fold(grad * norm)
+            off = x_sc[n, 0:n_in, cols].astype(F32) - mean
+            one, two = lane_fold(grad), lane_fold(grad * off)
             first = one if first is None else first + one
             second = two if second is None else second + two
         acc_sc[0] += first
@@ -1155,9 +1168,10 @@
     scatter(reduce_refs, 6, wg_sc)
     msg_sc[2] = jnp.zeros_like(msg_sc[2])
     msg_sc[2, 0:2, :] = cols_to_row(padc_sc, acc_sc[0])
-    msg_sc[2, 2:4, :] = cols_to_row(padc_sc, acc_sc[1])
+    msg_sc[2, 2:4, :] = cols_to_row(padc_sc, acc_sc[1]) * rstd_row
     stat_sc[3, bi] = msg_sc[2]
     batch_send(3, same(msg_sc.at[2]), stat_sc.at[3])
+    reduce_gather(reduce_refs, 6)
     batch_wait(3, same(msg_sc.at[2]), stat_sc.at[3])
     total = stat_sc[3, 0]
     for at in range(1, nb):
@@ -1165,7 +1179,6 @@
     gain_scale = gain_row * rstd_row
     row_to_cols(col_sc.at[4], -gain_scale * rstd_row * (total[2:4, :] / pixels))
     row_to_cols(col_sc.at[5], -gain_scale * (total[0:2, :] / pixels))
-    reduce_gather(reduce_refs, 6)
 
     def finish(n, carry):
         mean, slant, level = wide(col_sc, 0), wide(col_sc, 4), wide(col_sc, 5)
@@ -1205,9 +1218,9 @@
     lax.fori_loop(0, n_views, stored, 0)
 
     def sent(i, carry):
-        half_copy(i).wait_send()
         rest_copy(i).wait_send()
         for h in range(2):
+            half_copy(i, h).wait_send()
             dm_copy(i, h).wait_send()
         return carry
 
@@ -1308,8 +1321,8 @@
             pltpu.VMEM((4, quarter, n_new, CHUNK), BF16),
             dma((n_views,)),
             dma((n_views,)),
-            dma((slots,)),
-            dma((slots,)),
+            dma((slots, 2)),
+            dma((slots, 2)),
             dma((slots, 2)),
             dma((slots, 2)),
             dma((slots,)),

time: 103 us -> 102 us (level)
    pallas_call x1, Pallas kernels: 79.2 us -> 78.1 us  [layer(): pl.pallas_call(functools.partial(layer_kernel, nb), in_specs=[smem, smem,...]
where the time goes in v4:
time: 102 us
  Pallas kernels  101 us (99%)
    pallas_call x1, Pallas kernels, layer(): pl.pallas_call(functools.partial(layer_kernel, nb), in_specs=[smem, smem,...  78.1 us
    pallas_call x1, Pallas kernels, crop_views(): pl.pallas_call(crop_kernel, in_specs=[smem, smem, anywhere], out_specs=[a...  12.1 us
    pallas_call x1, Pallas kernels, place_views(): pl.pallas_call(place_kernel, in_specs=[smem, smem, anywhere] + [vmem] * 4...  10.8 us

profile of v4, /device:TPU:0, one launch (start us, length us, event | category | flops | bytes accessed | tf_op | source)
XLA Modules:
  0.0 101.8 jit_solution(7374461340570472228)
XLA Ops:
  0.6 12.1 %crop_views.1 = (bf16[16,160,1024]{2,1,0:T(8,128)(2,1)}, bf16[157,16,1024]{2,1,0:T(8,128)(2,1)}, f32[8,128]{1,0:T(8,128)}) custom-call(s32[2,2,8]{2,1,0:T(2,128)} %bitcast.21, s32[2,8]{1,0:T(2,128)} %bitcast.24, bf16[157,8,2304]{2,1,0:T(8,128)(2,1)} %bitcast.16), custom_call_target="tpu_custom_call" | custom-call | tf_op jit(solution)/shard_map/crop_views/pallas_call | solution.py:200
  12.8 78.1 %layer.1 = (bf16[16,160,1024]{2,1,0:T(8,128)(2,1)}, bf16[16,33,256]{2,1,0:T(8,128)(2,1)}, f32[132,157]{1,0:T(8,128)}, f32[33,432]{1,0:T(8,128)}, f32[8,256]{1,0:T(8,128)}) custom-call(s32[2,2,8]{2,1,0:T(2,128)} %bitcast.22, s32[2,8]{1,0:T(2,128)} %bitcast.25, bf16[16,160,1024]{2,1,0:T(8,128)(2,1)} %get-tuple-element.26.views_hbm, ...), custom_call_target="tpu_custom_call" | custom-call | tf_op jit(solution)/shard_map/layer/pallas_call | solution.py:1255
  90.9 10.8 %place_views.1 = (f32[157,8,2304]{2,1,0:T(8,128)}, bf16[33,16,256]{2,1,0:T(8,128)(2,1)}, f32[132,157]{1,0:T(8,128)}, f32[9,33,33]{2,1,0:T(8,128)}, f32[157]{0:T(...) custom-call(s32[2,2,8]{2,1,0:T(2,128)} %bitcast.23, s32[2,8]{1,0:T(2,128)} %bitcast.26, ...), custom_call_target="tpu_custom_call" | custom-call | tf_op jit(solution)/shard_map/place_views/pallas_call | solution.py:339

commit v5 on v4

--- a/solution.py
+++ b/solution.py
@@ -1039,6 +1039,129 @@
     msg_sc[1] = (cstat_sc[1, 0] + cstat_sc[1, 1]) + (cstat_sc[1, 2] + cstat_sc[1, 3])
     stat_sc[2, bi] = msg_sc[1]
     batch_send(2, same(msg_sc.at[1]), stat_sc.at[2])
+    ready = quarter // 2
+
+    def far_point(q, carry):
+        m = quarter // 2 + q // 2
+        rest_copy(quarter + q).wait_recv()
+        unpack_rest(pair_rest[q].astype(F32) + far_rest[quarter + q].astype(F32))
+
+        @pl.when(lax.rem(q, 2) == 0)
+        def _():
+            far_copy(m, 0, 0).wait_recv()
+            far_copy(m, 0, 1).wait_recv()
+
+        @pl.when(lax.rem(q, 2) == 1)
+        def _():
+            unpack_second(m)
+
+        for k, cols in enumerate(chunks()):
+            part = pair_sc[q, :, cols].astype(F32) + far_sc[quarter + q, :, cols].astype(F32)
+            norm, act, slope = mid_point(with_rest(part, k))
+            d_sc[q, :, cols] = d_sc[q, :, cols] * slope
+            half_in[q, :, cols] = norm.astype(BF16)
+        return carry
+
+    lax.fori_loop(0, ready, far_point, 0)
+    reduce_gather(spread_refs, 4)
+    batch_wait(2, same(msg_sc.at[1]), stat_sc.at[2])
+    mid_sums = stat_sc[2, 0]
+    for at in range(1, nb):
+        mid_sums = mid_sums + stat_sc[2, at]
+    row_to_cols(colm_sc.at[4], mid_sums[0:2, :] / pixels)
+    row_to_cols(colm_sc.at[5], mid_sums[2:4, :] / pixels)
+    row_to_cols(colm_sc.at[6], gathered(2) * rstdm_row)
+
+    def dm_copy(i, h):
+        return pltpu.make_async_remote_copy(
+            src_ref=dm_out.at[i, :, half_cols(h)],
+            dst_ref=dm_in.at[i, :, half_cols(h)],
+            send_sem=dm_s.at[i, h],
+            recv_sem=dm_r.at[i, h],
+            device_id=mate,
+            device_id_type=MESH,
+        )
+
+    def store(n):
+        return pltpu.make_async_copy(slope_sc.at[n], dv_hbm.at[n], store_sem.at[n])
+
+    def back_view(n, dm_ref):
+        mean, scale = wide(col_sc, 0), wide(col_sc, 2)
+        first, second = None, None
+        for cols in chunks():
+            grad = dot(wr_sc[...], dm_ref[:, cols]) * slope_sc[n, 0:n_in, cols].astype(F32)
+            slope_sc[n, 0:n_in, cols] = (grad * scale + dp_sc[n, :, cols].astype(F32)).astype(BF16)
+            off = x_sc[n, 0:n_in, cols].astype(F32) - mean
+            one, two = lane_fold(grad), lane_fold(grad * off)
+            first = one if first is None else first + one
+            second = two if second is None else second + two
+        acc_sc[0] += first
+        acc_sc[1] += second
+        wg_sc[:, 0:n_in] += dot_nt(dm_ref[...], act_sc[n])
+
+    def dm_own(q, carry):
+        i = quarter + q
+        for cols in chunks():
+            grad = d_sc[i, :, cols] - wide(colm_sc, 4) - mid_sc[q, :, cols] * wide(colm_sc, 5)
+            dm_out[i, :, cols] = (grad * wide(colm_sc, 6)).astype(BF16)
+        dm_copy(i, 0).start()
+        dm_copy(i, 1).start()
+        return carry
+
+    lax.fori_loop(0, quarter, dm_own, 0)
+
+    def back_mate(i):
+        dm_copy(i, 0).wait_recv()
+        dm_copy(i, 1).wait_recv()
+        back_view(slot_view(i, 1 - c), dm_in.at[i])
+
+    def back_own(q, carry):
+        back_view(slot_view(quarter + q, c), dm_out.at[quarter + q])
+
+        @pl.when(q > 0)
+        def _():
+            back_mate(quarter + q - 1)
+
+        return carry
+
+    lax.fori_loop(0, quarter, back_own, 0)
+    back_mate(2 * quarter - 1)
+
+    def back_far(q, carry):
+        @pl.when(q >= ready)
+        def _():
+            far_point(q, carry)
+
+        for k, cols in enumerate(chunks()):
+            grad = d_sc[q, :, cols] - wide(colm_sc, 4) - half_in[q, :, cols].astype(F32) * wide(colm_sc, 5)
+            dm_out[q, :, cols] = (grad * wide(colm_sc, 6)).astype(BF16)
+            if k % 2 == 1:
+                dm_copy(q, k // 2).start()
+        back_view(slot_view(q, c), dm_out.at[q])
+
+        @pl.when(q > 0)
+        def _():
+            back_mate(q - 1)
+
+        return carry
+
+    lax.fori_loop(0, quarter // 2, back_far, 0)
+    gather(spread_refs, 4, wsg_sc)
+    for b in range(4):
+        wsp_sc[b, 0:40, :] = wsg_sc[n_own * b : n_own * b + 40, :].astype(BF16)
+    wsgi_sc[ci] = wsp_sc[ci]
+    wsg_of = lambda other: wsp_sc.at[other]
+    chan_send(6, wsg_of, wsgi_sc)
+    lax.fori_loop(quarter // 2, quarter, back_far, 0)
+    back_mate(quarter - 1)
+
+    scatter(reduce_refs, 6, wg_sc)
+    msg_sc[2] = jnp.zeros_like(msg_sc[2])
+    msg_sc[2, 0:2, :] = cols_to_row(padc_sc, acc_sc[0])
+    msg_sc[2, 2:4, :] = cols_to_row(padc_sc, acc_sc[1]) * rstd_row
+    stat_sc[3, bi] = msg_sc[2]
+    batch_send(3, same(msg_sc.at[2]), stat_sc.at[3])
+
     def spread(q, carry):
         for k, cols in enumerate(chunks()):
             taps = dot(wf_sc[...], actm_sc[q, :, cols])
@@ -1061,116 +1184,7 @@
     lax.fori_loop(0, quarter, spread, 0)
     new_of = lambda other: newo_sc.at[other]
     newi_sc[ci] = newo_sc[ci]
-    reduce_gather(spread_refs, 4)
-    batch_wait(2, same(msg_sc.at[1]), stat_sc.at[2])
-    mid_sums = stat_sc[2, 0]
-    for at in range(1, nb):
-        mid_sums = mid_sums + stat_sc[2, at]
-    row_to_cols(colm_sc.at[4], mid_sums[0:2, :] / pixels)
-    row_to_cols(colm_sc.at[5], mid_sums[2:4, :] / pixels)
-    row_to_cols(colm_sc.at[6], gathered(2) * rstdm_row)
-
-    def dm_copy(i, h):
-        return pltpu.make_async_remote_copy(
-            src_ref=dm_out.at[i, :, half_cols(h)],
-            dst_ref=dm_in.at[i, :, half_cols(h)],
-            send_sem=dm_s.at[i, h],
-            recv_sem=dm_r.at[i, h],
-            device_id=mate,
-            device_id_type=MESH,
-        )
-
-    def store(n):
-        return pltpu.make_async_copy(slope_sc.at[n], dv_hbm.at[n], store_sem.at[n])
-
-    def back_view(n, dm_ref):
-        mean, scale = wide(col_sc, 0), wide(col_sc, 2)
-        first, second = None, None
-        for cols in chunks():
-            grad = dot(wr_sc[...], dm_ref[:, cols]) * slope_sc[n, 0:n_in, cols].astype(F32)
-            slope_sc[n, 0:n_in, cols] = (grad * scale + dp_sc[n, :, cols].astype(F32)).astype(BF16)
-            off = x_sc[n, 0:n_in, cols].astype(F32) - mean
-            one, two = lane_fold(grad), lane_fold(grad * off)
-            first = one if first is None else first + one
-            second = two if second is None else second + two
-        acc_sc[0] += first
-        acc_sc[1] += second
-        wg_sc[:, 0:n_in] += dot_nt(dm_ref[...], act_sc[n])
-
-    def dm_own(q, carry):
-        i = quarter + q
-        for cols in chunks():
-            grad = d_sc[i, :, cols] - wide(colm_sc, 4) - mid_sc[q, :, cols] * wide(colm_sc, 5)
-            dm_out[i, :, cols] = (grad * wide(colm_sc, 6)).astype(BF16)
-        dm_copy(i, 0).start()
-        dm_copy(i, 1).start()
-        return carry
-
-    lax.fori_loop(0, quarter, dm_own, 0)
-
-    def back_mate(i):
-        dm_copy(i, 0).wait_recv()
-        dm_copy(i, 1).wait_recv()
-        back_view(slot_view(i, 1 - c), dm_in.at[i])
-
-    def back_own(q, carry):
-        back_view(slot_view(quarter + q, c), dm_out.at[quarter + q])
-
-        @pl.when(q > 0)
-        def _():
-            back_mate(quarter + q - 1)
-
-        return carry
-
-    lax.fori_loop(0, quarter, back_own, 0)
-    back_mate(2 * quarter - 1)
-
-    def back_far(q, carry):
-        m = quarter // 2 + q // 2
-        rest_copy(quarter + q).wait_recv()
-        unpack_rest(pair_rest[q].astype(F32) + far_rest[quarter + q].astype(F32))
-
-        @pl.when(lax.rem(q, 2) == 0)
-        def _():
-            far_copy(m, 0, 0).wait_recv()
-            far_copy(m, 0, 1).wait_recv()
-
-        @pl.when(lax.rem(q, 2) == 1)
-        def _():
-            unpack_second(m)
-
-        for k, cols in enumerate(chunks()):
-            part = pair_sc[q, :, cols].astype(F32) + far_sc[quarter + q, :, cols].astype(F32)
-            norm, act, slope = mid_point(with_rest(part, k))
-            grad = d_sc[q, :, cols] * slope - wide(colm_sc, 4) - norm * wide(colm_sc, 5)
-            dm_out[q, :, cols] = (grad * wide(colm_sc, 6)).astype(BF16)
-            if k % 2 == 1:
-                dm_copy(q, k // 2).start()
-        back_view(slot_view(q, c), dm_out.at[q])
-
-        @pl.when(q > 0)
-        def _():
-            back_mate(q - 1)
-
-        return carry
-
-    lax.fori_loop(0, quarter // 2, back_far, 0)
-    gather(spread_refs, 4, wsg_sc)
-    for b in range(4):
-        wsp_sc[b, 0:40, :] = wsg_sc[n_own * b : n_own * b + 40, :].astype(BF16)
-    wsgi_sc[ci] = wsp_sc[ci]
-    wsg_of = lambda other: wsp_sc.at[other]
-    chan_send(6, wsg_of, wsgi_sc)
     chan_send(5, new_of, newi_sc)
-    lax.fori_loop(quarter // 2, quarter, back_far, 0)
-    back_mate(quarter - 1)
-
-    scatter(reduce_refs, 6, wg_sc)
-    msg_sc[2] = jnp.zeros_like(msg_sc[2])
-    msg_sc[2, 0:2, :] = cols_to_row(padc_sc, acc_sc[0])
-    msg_sc[2, 2:4, :] = cols_to_row(padc_sc, acc_sc[1]) * rstd_row
-    stat_sc[3, bi] = msg_sc[2]
-    batch_send(3, same(msg_sc.at[2]), stat_sc.at[3])
     reduce_gather(reduce_refs, 6)
     batch_wait(3, same(msg_sc.at[2]), stat_sc.at[3])
     total = stat_sc[3, 0]

time: 102 us -> 102 us (level)
  no operation moved by 1% of the time
where the time goes in v5:
time: 102 us; the launch traced here: 101 us
  Pallas kernels  101 us (99%)
    pallas_call x1, Pallas kernels, layer(): pl.pallas_call(functools.partial(layer_kernel, nb), in_specs=[smem, smem,...  77.6 us
    pallas_call x1, Pallas kernels, crop_views(): pl.pallas_call(crop_kernel, in_specs=[smem, smem, anywhere], out_specs=[a...  12.1 us
    pallas_call x1, Pallas kernels, place_views(): pl.pallas_call(place_kernel, in_specs=[smem, smem, anywhere] + [vmem] * 4...  10.8 us

profile of v5, /device:TPU:0, one launch (start us, length us, event | category | flops | bytes accessed | tf_op | source)
XLA Modules:
  0.0 101.3 jit_solution(3434957454254319718)
XLA Ops:
  0.6 12.1 %crop_views.1 = (bf16[16,160,1024]{2,1,0:T(8,128)(2,1)}, bf16[157,16,1024]{2,1,0:T(8,128)(2,1)}, f32[8,128]{1,0:T(8,128)}) custom-call(s32[2,2,8]{2,1,0:T(2,128)} %bitcast.21, s32[2,8]{1,0:T(2,128)} %bitcast.24, bf16[157,8,2304]{2,1,0:T(8,128)(2,1)} %bitcast.16), custom_call_target="tpu_custom_call" | custom-call | tf_op jit(solution)/shard_map/crop_views/pallas_call | solution.py:200
  12.8 77.6 %layer.1 = (bf16[16,160,1024]{2,1,0:T(8,128)(2,1)}, bf16[16,33,256]{2,1,0:T(8,128)(2,1)}, f32[132,157]{1,0:T(8,128)}, f32[33,432]{1,0:T(8,128)}, f32[8,256]{1,0:T(8,128)}) custom-call(s32[2,2,8]{2,1,0:T(2,128)} %bitcast.22, s32[2,8]{1,0:T(2,128)} %bitcast.25, bf16[16,160,1024]{2,1,0:T(8,128)(2,1)} %get-tuple-element.26.views_hbm, ...), custom_call_target="tpu_custom_call" | custom-call | tf_op jit(solution)/shard_map/layer/pallas_call | solution.py:1269
  90.3 10.8 %place_views.1 = (f32[157,8,2304]{2,1,0:T(8,128)}, bf16[33,16,256]{2,1,0:T(8,128)(2,1)}, f32[132,157]{1,0:T(8,128)}, f32[9,33,33]{2,1,0:T(8,128)}, f32[157]{0:T(...) custom-call(s32[2,2,8]{2,1,0:T(2,128)} %bitcast.23, s32[2,8]{1,0:T(2,128)} %bitcast.26, ...), custom_call_target="tpu_custom_call" | custom-call | tf_op jit(solution)/shard_map/place_views/pallas_call | solution.py:339

commit v6 on v5

--- a/solution.py
+++ b/solution.py
@@ -256,8 +256,8 @@
     lax.fori_loop(0, n_views, build, 0)
 
     def block(b, carry):
+        flat_sc[...] = jnp.zeros_like(flat_sc)
         load(b).wait()
-        flat_sc[...] = jnp.zeros_like(flat_sc)
 
         def place_item(j):
             for v in range(2):

time: 102 us -> 102 us (level)
  no operation moved by 1% of the time
where the time goes in v6:
time: 102 us; the launch traced here: 101 us
  Pallas kernels  100 us (98%)
    pallas_call x1, Pallas kernels, layer(): pl.pallas_call(functools.partial(layer_kernel, nb), in_specs=[smem, smem,...  77.6 us
    pallas_call x1, Pallas kernels, crop_views(): pl.pallas_call(crop_kernel, in_specs=[smem, smem, anywhere], out_specs=[a...  12.1 us
    pallas_call x1, Pallas kernels, place_views(): pl.pallas_call(place_kernel, in_specs=[smem, smem, anywhere] + [vmem] * 4...  10.7 us

profile of v6, /device:TPU:0, one launch (start us, length us, event | category | flops | bytes accessed | tf_op | source)
XLA Modules:
  0.0 101.2 jit_solution(466581440441590522)
XLA Ops:
  0.6 12.1 %crop_views.1 = (bf16[16,160,1024]{2,1,0:T(8,128)(2,1)}, bf16[157,16,1024]{2,1,0:T(8,128)(2,1)}, f32[8,128]{1,0:T(8,128)}) custom-call(s32[2,2,8]{2,1,0:T(2,128)} %bitcast.21, s32[2,8]{1,0:T(2,128)} %bitcast.24, bf16[157,8,2304]{2,1,0:T(8,128)(2,1)} %bitcast.16), custom_call_target="tpu_custom_call" | custom-call | tf_op jit(solution)/shard_map/crop_views/pallas_call | solution.py:200
  12.7 77.6 %layer.1 = (bf16[16,160,1024]{2,1,0:T(8,128)(2,1)}, bf16[16,33,256]{2,1,0:T(8,128)(2,1)}, f32[132,157]{1,0:T(8,128)}, f32[33,432]{1,0:T(8,128)}, f32[8,256]{1,0:T(8,128)}) custom-call(s32[2,2,8]{2,1,0:T(2,128)} %bitcast.22, s32[2,8]{1,0:T(2,128)} %bitcast.25, bf16[16,160,1024]{2,1,0:T(8,128)(2,1)} %get-tuple-element.26.views_hbm, ...), custom_call_target="tpu_custom_call" | custom-call | tf_op jit(solution)/shard_map/layer/pallas_call | solution.py:1269
  90.4 10.7 %place_views.1 = (f32[157,8,2304]{2,1,0:T(8,128)}, bf16[33,16,256]{2,1,0:T(8,128)(2,1)}, f32[132,157]{1,0:T(8,128)}, f32[9,33,33]{2,1,0:T(8,128)}, f32[157]{0:T(...) custom-call(s32[2,2,8]{2,1,0:T(2,128)} %bitcast.23, s32[2,8]{1,0:T(2,128)} %bitcast.26, ...), custom_call_target="tpu_custom_call" | custom-call | tf_op jit(solution)/shard_map/place_views/pallas_call | solution.py:339
